TPU v7x, 32 devices: a whole 2x2x4 slice. The times are simulated.
32 devices in a mesh: seq: 16 (over z, x, core), batch: 2 (over y).
Axes of the slice: x: 2, y: 2, z: 4, core: 2. Of those that a mesh axis runs over, the one named last changes fastest.
Arguments:
- enc_in: bfloat16 [2, 1024, 512], P('batch', 'seq'), may hold values from -6 to 6
- series: bfloat16 [2, 1024, 862], P('batch', 'seq'), may hold values from -6 to 6
- channel_mask: int32 [16, 862], replicated, may hold values 0 or 1
- item_group: int32 [2], P('batch'), may hold values from 0 to 15
- tau_scale: float32 [2], P('batch'), may hold values from 0.6 to 1.8
- delta_shift: bfloat16 [2, 1024], P('batch', 'seq'), may hold values from -16 to 16
- dec_in: bfloat16 [2, 1024, 512], P('batch', 'seq'), may hold values from -6 to 6
- value_embed: bfloat16 [862, 512], replicated, may hold values from -0.21875 to 0.21875
- enc_qkv: bfloat16 [3, 512, 512], replicated, may hold values from -0.25 to 0.25
- enc_out: bfloat16 [512, 512], replicated, may hold values from -6 to 6
- enc_ff_in: bfloat16 [512, 2048], replicated, may hold values from -0.25 to 0.25
- enc_ff_out: bfloat16 [2048, 512], replicated, may hold values from -0.125 to 0.125
- enc_query_bias: float32 [512], replicated, may hold values from -0.6 to 0.6
- enc_bias: float32 [5, 512], replicated, may hold values from -0.3 to 0.3
- enc_gain: float32 [2, 512], replicated, may hold values from 0.5 to 1.5
- dec_qkv: bfloat16 [3, 512, 512], replicated, may hold values from -0.25 to 0.25
- dec_out: bfloat16 [512, 512], replicated, may hold values from -3 to 3
- cross_qkv: bfloat16 [3, 512, 512], replicated, may hold values from -0.25 to 0.25
- cross_out: bfloat16 [512, 512], replicated, may hold values from -6 to 6
- dec_ff_in: bfloat16 [512, 2048], replicated, may hold values from -0.25 to 0.25
- dec_ff_out: bfloat16 [2048, 512], replicated, may hold values from -0.125 to 0.125
- dec_bias: float32 [10, 512], replicated, may hold values from -0.3 to 0.3
- dec_gain: float32 [3, 512], replicated, may hold values from 0.5 to 1.5
- ff_bias: float32 [2, 2048], replicated, may hold values from -1.5 to 1.5
- cotangent: bfloat16 [2, 1024, 512], P('batch', 'seq'), may hold values from -6 to 6
Outputs:
- dec_result: bfloat16 [2, 1024, 512], P('batch', 'seq')
- grad_enc_in: float32 [2, 1024, 512], P('batch', 'seq')
- grad_dec_in: float32 [2, 1024, 512], P('batch', 'seq')
- grad_value_embed: float32 [862, 512], P(None, 'seq')
- grad_enc_qkv: float32 [3, 512, 512], P(None, None, 'seq')
- grad_enc_out: float32 [512, 512], P(None, 'seq')
- grad_enc_ff_in: float32 [512, 2048], P(None, 'seq')
- grad_enc_ff_out: float32 [2048, 512], P(None, 'seq')
- grad_enc_query_bias: float32 [512], P('seq')
- grad_enc_bias: float32 [5, 512], P(None, 'seq')
- grad_enc_gain: float32 [2, 512], P(None, 'seq')
- grad_dec_qkv: float32 [3, 512, 512], P(None, None, 'seq')
- grad_dec_out: float32 [512, 512], P(None, 'seq')
- grad_cross_qkv: float32 [3, 512, 512], P(None, None, 'seq')
- grad_cross_out: float32 [512, 512], P(None, 'seq')
- grad_dec_ff_in: float32 [512, 2048], P(None, 'seq')
- grad_dec_ff_out: float32 [2048, 512], P(None, 'seq')
- grad_dec_bias: float32 [10, 512], P(None, 'seq')
- grad_dec_gain: float32 [3, 512], P(None, 'seq')
- grad_ff_bias: float32 [2, 2048], P(None, 'seq')
All inputs are finite; a program needn't handle non-finite values.
Results may differ from a plain program's by a relative error of at most 0.035.
Values may be sent and summed in bfloat16 or wider, within the bound.
A program may use at most 192 MiB of HBM per device.

v0:
```python
from functools import partial
import math

import jax
import jax.numpy as jnp
from jax import lax
from jax.sharding import PartitionSpec as P

HEADS = 8
GROUPS = 16


epsilon = 1e-05
masked_score = -1e30


def layer_norm(inputs, gain_vector, shift_vector):
    average = jnp.mean(inputs, axis=-1, keepdims=True)
    centred = inputs - average
    variance = jnp.mean(centred * centred, axis=-1, keepdims=True)
    return centred * lax.rsqrt(variance + epsilon) * gain_vector + shift_vector


def norm_backward(inputs, gain_vector, shift_vector, upstream):
    ignored, pullback = jax.vjp(layer_norm, inputs, gain_vector, shift_vector)
    return pullback(upstream)


def project(inputs, weight_matrix):
    return jnp.dot(inputs, weight_matrix, preferred_element_type=jnp.float32)


def project_back(gradient, weight_matrix):
    return jnp.einsum("ilf,kf->ilk", gradient, weight_matrix, preferred_element_type=jnp.float32)


def weight_grad(inputs, gradient):
    return jnp.einsum("ilk,ilf->kf", inputs, gradient, preferred_element_type=jnp.float32)


def row_total(gradient):
    return jnp.sum(gradient.astype(jnp.float32), axis=(0, 1))


def split_heads(values):
    return values.reshape(values.shape[:2] + (HEADS, values.shape[2] // HEADS))


def merge_heads(head_values):
    return jnp.transpose(head_values, (0, 2, 1, 3)).reshape(
        head_values.shape[0], head_values.shape[2], -1
    )


def over_blocks(update, totals, arrays, shard_rows):
    length = arrays[0].shape[1]
    block_rows = shard_rows * math.gcd(length // shard_rows, 8)
    block_count = length // block_rows
    stacked = tuple(
        (
            jnp.moveaxis(
                member.reshape((member.shape[0], block_count, block_rows) + member.shape[2:]), 1, 0
            )
            for member in arrays
        )
    )
    offsets = jnp.arange(block_count, dtype=jnp.int32) * block_rows

    def advance(running, inputs):
        return (update(running, inputs[0], inputs[1]), None)

    totals, ignored = lax.scan(advance, totals, (stacked, offsets))
    return totals


def head_scores(query_heads, key_heads, tau_value, key_shift):
    raw_scores = jnp.einsum(
        "iqhd,ikhd->ihqk", query_heads, key_heads, preferred_element_type=jnp.float32
    )
    return (tau_value[:, None, None, None] * raw_scores + key_shift[:, None, None, :]) * 0.125


def causal_mask(scores, query_pos, key_pos):
    allowed = query_pos[:, None] >= key_pos[None, :]
    return jnp.where(allowed[None, None], scores, masked_score)


def fresh_totals(item_count, row_count, head_size):
    return (
        jnp.full((item_count, HEADS, row_count), masked_score, jnp.float32),
        jnp.zeros((item_count, HEADS, row_count), jnp.float32),
        jnp.zeros((item_count, HEADS, row_count, head_size), jnp.float32),
    )


def finish_forward(totals):
    running_max, running_sum, weighted = totals
    output = merge_heads(weighted / running_sum[..., None])
    log_total = jnp.transpose(running_max + jnp.log(running_sum), (0, 2, 1))
    return (output, log_total)


def row_products(grad_rows, mixed_rows):
    return jnp.sum(split_heads(grad_rows).astype(jnp.float32) * split_heads(mixed_rows), axis=-1)


def scaled_grad(head_totals, tau_value):
    return merge_heads(head_totals * (tau_value * 0.125)[:, None, None, None]).astype(jnp.bfloat16)


def plain_unpack(fetched):
    return (fetched[0], fetched[1], fetched[2].astype(jnp.float32))


def self_unpack(fetched):
    return (fetched[0], fetched[1], jnp.zeros(fetched[0].shape[:2], jnp.float32))


def forward_update(query_heads, tau_value, query_pos, causal, unpack, shard_rows):

    def update(totals, fetched, offset):

        def block_update(running, piece_parts, inner_offset):
            running_max, running_sum, weighted = running
            key_rows, value_rows, key_shift = unpack(piece_parts)
            scores = head_scores(query_heads, split_heads(key_rows), tau_value, key_shift)
            if causal:
                key_pos = inner_offset + jnp.arange(key_rows.shape[1], dtype=jnp.int32)
                scores = causal_mask(scores, query_pos, key_pos)
            new_max = jnp.maximum(running_max, jnp.max(scores, axis=-1))
            factor = jnp.exp(running_max - new_max)
            weights = jnp.exp(scores - new_max[..., None])
            new_sum = running_sum * factor + jnp.sum(weights, axis=-1)
            mixed_values = jnp.einsum(
                "ihqk,ikhd->ihqd",
                weights,
                split_heads(value_rows).astype(jnp.float32),
                preferred_element_type=jnp.float32,
            )
            return (new_max, new_sum, weighted * factor[..., None] + mixed_values)

        return over_blocks(block_update, totals, fetched, shard_rows)

    return update


def query_grad_update(
    query_heads, grad_heads, log_total, row_dot, tau_value, query_pos, causal, unpack, shard_rows
):

    def update(totals, fetched, offset):

        def block_update(running, piece_parts, inner_offset):
            key_rows, value_rows, key_shift = unpack(piece_parts)
            key_heads = split_heads(key_rows)
            scores = head_scores(query_heads, key_heads, tau_value, key_shift)
            if causal:
                key_pos = inner_offset + jnp.arange(key_rows.shape[1], dtype=jnp.int32)
                scores = causal_mask(scores, query_pos, key_pos)
            probabilities = jnp.exp(scores - log_total[..., None])
            prob_grads = jnp.einsum(
                "iqhd,ikhd->ihqk",
                grad_heads,
                split_heads(value_rows),
                preferred_element_type=jnp.float32,
            )
            score_grads = (probabilities * (prob_grads - row_dot[..., None])).astype(jnp.bfloat16)
            return running + jnp.einsum(
                "ihqk,ikhd->ihqd", score_grads, key_heads, preferred_element_type=jnp.float32
            )

        return over_blocks(block_update, totals, fetched, shard_rows)

    return update


def key_grad_update(key_heads, value_heads, key_shift, tau_value, key_pos, causal, shard_rows):

    def update(totals, fetched, offset):

        def block_update(running, piece_parts, inner_offset):
            key_total, value_total = running
            query_heads = split_heads(piece_parts[0].astype(jnp.bfloat16))
            grad_heads = split_heads(piece_parts[1].astype(jnp.bfloat16))
            log_rows = jnp.transpose(piece_parts[2], (0, 2, 1))
            dot_rows = jnp.transpose(piece_parts[3], (0, 2, 1))
            scores = head_scores(query_heads, key_heads, tau_value, key_shift)
            if causal:
                query_pos = inner_offset + jnp.arange(piece_parts[0].shape[1], dtype=jnp.int32)
                scores = causal_mask(scores, query_pos, key_pos)
            probabilities = jnp.exp(scores - log_rows[..., None])
            value_total = value_total + jnp.einsum(
                "ihqk,iqhd->ihkd",
                probabilities,
                grad_heads.astype(jnp.float32),
                preferred_element_type=jnp.float32,
            )
            prob_grads = jnp.einsum(
                "iqhd,ikhd->ihqk", grad_heads, value_heads, preferred_element_type=jnp.float32
            )
            score_grads = (probabilities * (prob_grads - dot_rows[..., None])).astype(jnp.bfloat16)
            key_total = key_total + jnp.einsum(
                "ihqk,iqhd->ihkd", score_grads, query_heads, preferred_element_type=jnp.float32
            )
            return (key_total, value_total)

        return over_blocks(block_update, totals, fetched, shard_rows)

    return update


def feed_forward_back(upstream, hidden, pre_act, activated, weight_in, weight_out):
    out_grad = upstream.astype(jnp.bfloat16)
    out_weight_grad = weight_grad(activated, out_grad)
    out_bias_grad = row_total(out_grad)
    act_grad = project_back(out_grad, weight_out)
    ignored, gelu_back = jax.vjp(partial(jax.nn.gelu, approximate=False), pre_act)
    pre_grad = gelu_back(act_grad)[0].astype(jnp.bfloat16)
    return (
        project_back(pre_grad, weight_in),
        weight_grad(hidden, pre_grad),
        row_total(pre_grad),
        out_weight_grad,
        out_bias_grad,
    )


def local(
    enc_in,
    series,
    channel_mask,
    item_group,
    tau_scale,
    delta_shift,
    dec_in,
    value_embed,
    enc_qkv,
    enc_out,
    enc_ff_in,
    enc_ff_out,
    enc_query_bias,
    enc_bias,
    enc_gain,
    dec_qkv,
    dec_out,
    cross_qkv,
    cross_out,
    dec_ff_in,
    dec_ff_out,
    dec_bias,
    dec_gain,
    ff_bias,
    cotangent,
):
    item_count, enc_rows, width = enc_in.shape
    dec_rows = dec_in.shape[1]
    head_size = width // HEADS
    seq_index = lax.axis_index("seq")
    enc_pos = seq_index * enc_rows + jnp.arange(enc_rows, dtype=jnp.int32)
    dec_pos = seq_index * dec_rows + jnp.arange(dec_rows, dtype=jnp.int32)
    enc_shift = delta_shift.astype(jnp.float32)
    chosen = (item_group[:, None] == jnp.arange(GROUPS, dtype=jnp.int32)[None, :]).astype(
        jnp.float32
    )
    channels = jnp.dot(chosen, channel_mask.astype(jnp.float32), precision=lax.Precision.HIGHEST)
    masked_series = (series.astype(jnp.float32) * channels[:, None, :]).astype(jnp.bfloat16)
    embedded = enc_in.astype(jnp.float32) + project(masked_series, value_embed)
    enc_hidden = embedded.astype(jnp.bfloat16)
    enc_query = (project(enc_hidden, enc_qkv[0]) + enc_query_bias).astype(jnp.bfloat16)
    enc_key = project(enc_hidden, enc_qkv[1]).astype(jnp.bfloat16)
    enc_value = (project(enc_hidden, enc_qkv[2]) + enc_bias[0]).astype(jnp.bfloat16)
    enc_update = forward_update(
        split_heads(enc_query), tau_scale, enc_pos, False, plain_unpack, enc_rows
    )
    enc_mixed, enc_log = finish_forward(
        enc_update(
            fresh_totals(item_count, enc_rows, head_size),
            (
                lax.all_gather(enc_key, "seq", axis=1, tiled=True),
                lax.all_gather(enc_value, "seq", axis=1, tiled=True),
                lax.all_gather(delta_shift, "seq", axis=1, tiled=True),
            ),
            jnp.int32(0),
        )
    )
    enc_attended = enc_mixed.astype(jnp.bfloat16)
    enc_first_in = embedded + project(enc_attended, enc_out) + enc_bias[1]
    enc_first = layer_norm(enc_first_in, enc_gain[0], enc_bias[3])
    enc_ff_hidden = enc_first.astype(jnp.bfloat16)
    enc_ff_pre = project(enc_ff_hidden, enc_ff_in) + ff_bias[0]
    enc_ff_act = jax.nn.gelu(enc_ff_pre, approximate=False).astype(jnp.bfloat16)
    enc_second_in = enc_first + project(enc_ff_act, enc_ff_out) + enc_bias[2]
    encoded = layer_norm(enc_second_in, enc_gain[1], enc_bias[4])
    memory = encoded.astype(jnp.bfloat16)
    self_query = (project(dec_in, dec_qkv[0]) + dec_bias[0]).astype(jnp.bfloat16)
    self_key = project(dec_in, dec_qkv[1]).astype(jnp.bfloat16)
    self_value = (project(dec_in, dec_qkv[2]) + dec_bias[1]).astype(jnp.bfloat16)
    self_update = forward_update(
        split_heads(self_query), tau_scale, dec_pos, True, self_unpack, dec_rows
    )
    self_mixed, self_log = finish_forward(
        self_update(
            fresh_totals(item_count, dec_rows, head_size),
            (
                lax.all_gather(self_key, "seq", axis=1, tiled=True),
                lax.all_gather(self_value, "seq", axis=1, tiled=True),
            ),
            jnp.int32(0),
        )
    )
    self_attended = self_mixed.astype(jnp.bfloat16)
    dec_first_in = dec_in.astype(jnp.float32) + project(self_attended, dec_out) + dec_bias[2]
    dec_first = layer_norm(dec_first_in, dec_gain[0], dec_bias[7])
    cross_hidden = dec_first.astype(jnp.bfloat16)
    cross_query = (project(cross_hidden, cross_qkv[0]) + dec_bias[3]).astype(jnp.bfloat16)
    cross_key = project(memory, cross_qkv[1]).astype(jnp.bfloat16)
    cross_value = (project(memory, cross_qkv[2]) + dec_bias[4]).astype(jnp.bfloat16)
    cross_start = fresh_totals(item_count, dec_rows, head_size)
    cross_update = forward_update(
        split_heads(cross_query), tau_scale, dec_pos, False, plain_unpack, enc_rows
    )
    cross_totals = cross_update(
        cross_start,
        (
            lax.all_gather(cross_key, "seq", axis=1, tiled=True),
            lax.all_gather(cross_value, "seq", axis=1, tiled=True),
            lax.all_gather(delta_shift, "seq", axis=1, tiled=True),
        ),
        jnp.int32(0),
    )
    cross_mixed, cross_log = finish_forward(cross_totals)
    cross_attended = cross_mixed.astype(jnp.bfloat16)
    dec_second_in = dec_first + project(cross_attended, cross_out) + dec_bias[5]
    dec_second = layer_norm(dec_second_in, dec_gain[1], dec_bias[8])
    dec_ff_hidden = dec_second.astype(jnp.bfloat16)
    dec_ff_pre = project(dec_ff_hidden, dec_ff_in) + ff_bias[1]
    dec_ff_act = jax.nn.gelu(dec_ff_pre, approximate=False).astype(jnp.bfloat16)
    dec_third_in = dec_second + project(dec_ff_act, dec_ff_out) + dec_bias[6]
    decoded = layer_norm(dec_third_in, dec_gain[2], dec_bias[9])
    third_grad, dec_gain_three, dec_bias_three = norm_backward(
        dec_third_in, dec_gain[2], dec_bias[9], cotangent.astype(jnp.float32)
    )
    from_dec_ff, dec_ff_in_grad, dec_ff_bias_grad, dec_ff_out_grad, dec_ff_out_bias = (
        feed_forward_back(third_grad, dec_ff_hidden, dec_ff_pre, dec_ff_act, dec_ff_in, dec_ff_out)
    )
    second_grad, dec_gain_two, dec_bias_two = norm_backward(
        dec_second_in, dec_gain[1], dec_bias[8], third_grad + from_dec_ff
    )
    cross_branch_grad = second_grad.astype(jnp.bfloat16)
    cross_out_grad = weight_grad(cross_attended, cross_branch_grad)
    cross_out_bias = row_total(cross_branch_grad)
    cross_mixed_grad = project_back(cross_branch_grad, cross_out).astype(jnp.bfloat16)
    cross_dot = row_products(cross_mixed_grad, cross_mixed)
    cross_query_start = jnp.zeros((item_count, HEADS, dec_rows, head_size), jnp.float32)
    cross_back = query_grad_update(
        split_heads(cross_query),
        split_heads(cross_mixed_grad),
        jnp.transpose(cross_log, (0, 2, 1)),
        jnp.transpose(cross_dot, (0, 2, 1)),
        tau_scale,
        dec_pos,
        False,
        plain_unpack,
        enc_rows,
    )
    cross_query_total = cross_back(
        cross_query_start,
        (
            lax.all_gather(cross_key, "seq", axis=1, tiled=True),
            lax.all_gather(cross_value, "seq", axis=1, tiled=True),
            lax.all_gather(delta_shift, "seq", axis=1, tiled=True),
        ),
        jnp.int32(0),
    )
    cross_query_grad = scaled_grad(cross_query_total, tau_scale)
    cross_key_update = key_grad_update(
        split_heads(cross_key),
        split_heads(cross_value),
        enc_shift,
        tau_scale,
        enc_pos,
        False,
        dec_rows,
    )
    cross_key_start = (
        jnp.zeros((item_count, HEADS, enc_rows, head_size), jnp.float32),
        jnp.zeros((item_count, HEADS, enc_rows, head_size), jnp.float32),
    )
    cross_key_total, cross_value_total = cross_key_update(
        cross_key_start,
        (
            lax.all_gather(cross_query.astype(jnp.float32), "seq", axis=1, tiled=True),
            lax.all_gather(cross_mixed_grad.astype(jnp.float32), "seq", axis=1, tiled=True),
            lax.all_gather(cross_log, "seq", axis=1, tiled=True),
            lax.all_gather(cross_dot, "seq", axis=1, tiled=True),
        ),
        jnp.int32(0),
    )
    cross_key_grad = scaled_grad(cross_key_total, tau_scale)
    cross_value_grad = merge_heads(cross_value_total).astype(jnp.bfloat16)
    cross_qkv_grad = jnp.stack(
        [
            weight_grad(cross_hidden, cross_query_grad),
            weight_grad(memory, cross_key_grad),
            weight_grad(memory, cross_value_grad),
        ]
    )
    memory_grad = project_back(cross_key_grad, cross_qkv[1]) + project_back(
        cross_value_grad, cross_qkv[2]
    )
    first_grad, dec_gain_one, dec_bias_one = norm_backward(
        dec_first_in,
        dec_gain[0],
        dec_bias[7],
        second_grad + project_back(cross_query_grad, cross_qkv[0]),
    )
    self_branch_grad = first_grad.astype(jnp.bfloat16)
    dec_out_grad = weight_grad(self_attended, self_branch_grad)
    self_out_bias = row_total(self_branch_grad)
    self_mixed_grad = project_back(self_branch_grad, dec_out).astype(jnp.bfloat16)
    self_dot = row_products(self_mixed_grad, self_mixed)
    self_back = query_grad_update(
        split_heads(self_query),
        split_heads(self_mixed_grad),
        jnp.transpose(self_log, (0, 2, 1)),
        jnp.transpose(self_dot, (0, 2, 1)),
        tau_scale,
        dec_pos,
        True,
        self_unpack,
        dec_rows,
    )
    self_query_total = self_back(
        jnp.zeros((item_count, HEADS, dec_rows, head_size), jnp.float32),
        (
            lax.all_gather(self_key, "seq", axis=1, tiled=True),
            lax.all_gather(self_value, "seq", axis=1, tiled=True),
        ),
        jnp.int32(0),
    )
    self_query_grad = scaled_grad(self_query_total, tau_scale)
    self_key_update = key_grad_update(
        split_heads(self_key),
        split_heads(self_value),
        jnp.zeros((item_count, dec_rows), jnp.float32),
        tau_scale,
        dec_pos,
        True,
        dec_rows,
    )
    self_key_start = (
        jnp.zeros((item_count, HEADS, dec_rows, head_size), jnp.float32),
        jnp.zeros((item_count, HEADS, dec_rows, head_size), jnp.float32),
    )
    self_key_total, self_value_total = self_key_update(
        self_key_start,
        (
            lax.all_gather(self_query.astype(jnp.float32), "seq", axis=1, tiled=True),
            lax.all_gather(self_mixed_grad.astype(jnp.float32), "seq", axis=1, tiled=True),
            lax.all_gather(self_log, "seq", axis=1, tiled=True),
            lax.all_gather(self_dot, "seq", axis=1, tiled=True),
        ),
        jnp.int32(0),
    )
    self_key_grad = scaled_grad(self_key_total, tau_scale)
    self_value_grad = merge_heads(self_value_total).astype(jnp.bfloat16)
    dec_qkv_grad = jnp.stack(
        [
            weight_grad(dec_in, self_query_grad),
            weight_grad(dec_in, self_key_grad),
            weight_grad(dec_in, self_value_grad),
        ]
    )
    dec_in_grad = (
        first_grad
        + project_back(self_query_grad, dec_qkv[0])
        + project_back(self_key_grad, dec_qkv[1])
        + project_back(self_value_grad, dec_qkv[2])
    )
    enc_second_grad, enc_gain_two, enc_bias_two = norm_backward(
        enc_second_in, enc_gain[1], enc_bias[4], memory_grad
    )
    from_enc_ff, enc_ff_in_grad, enc_ff_bias_grad, enc_ff_out_grad, enc_ff_out_bias = (
        feed_forward_back(
            enc_second_grad, enc_ff_hidden, enc_ff_pre, enc_ff_act, enc_ff_in, enc_ff_out
        )
    )
    enc_first_grad, enc_gain_one, enc_bias_one = norm_backward(
        enc_first_in, enc_gain[0], enc_bias[3], enc_second_grad + from_enc_ff
    )
    enc_branch_grad = enc_first_grad.astype(jnp.bfloat16)
    enc_out_grad = weight_grad(enc_attended, enc_branch_grad)
    enc_out_bias = row_total(enc_branch_grad)
    enc_mixed_grad = project_back(enc_branch_grad, enc_out).astype(jnp.bfloat16)
    enc_dot = row_products(enc_mixed_grad, enc_mixed)
    enc_back = query_grad_update(
        split_heads(enc_query),
        split_heads(enc_mixed_grad),
        jnp.transpose(enc_log, (0, 2, 1)),
        jnp.transpose(enc_dot, (0, 2, 1)),
        tau_scale,
        enc_pos,
        False,
        plain_unpack,
        enc_rows,
    )
    enc_query_total = enc_back(
        jnp.zeros((item_count, HEADS, enc_rows, head_size), jnp.float32),
        (
            lax.all_gather(enc_key, "seq", axis=1, tiled=True),
            lax.all_gather(enc_value, "seq", axis=1, tiled=True),
            lax.all_gather(delta_shift, "seq", axis=1, tiled=True),
        ),
        jnp.int32(0),
    )
    enc_query_grad = scaled_grad(enc_query_total, tau_scale)
    enc_key_update = key_grad_update(
        split_heads(enc_key), split_heads(enc_value), enc_shift, tau_scale, enc_pos, False, enc_rows
    )
    enc_key_start = (
        jnp.zeros((item_count, HEADS, enc_rows, head_size), jnp.float32),
        jnp.zeros((item_count, HEADS, enc_rows, head_size), jnp.float32),
    )
    enc_key_total, enc_value_total = enc_key_update(
        enc_key_start,
        (
            lax.all_gather(enc_query.astype(jnp.float32), "seq", axis=1, tiled=True),
            lax.all_gather(enc_mixed_grad.astype(jnp.float32), "seq", axis=1, tiled=True),
            lax.all_gather(enc_log, "seq", axis=1, tiled=True),
            lax.all_gather(enc_dot, "seq", axis=1, tiled=True),
        ),
        jnp.int32(0),
    )
    enc_key_grad = scaled_grad(enc_key_total, tau_scale)
    enc_value_grad = merge_heads(enc_value_total).astype(jnp.bfloat16)
    enc_qkv_grad = jnp.stack(
        [
            weight_grad(enc_hidden, enc_query_grad),
            weight_grad(enc_hidden, enc_key_grad),
            weight_grad(enc_hidden, enc_value_grad),
        ]
    )
    enc_in_grad = (
        enc_first_grad
        + project_back(enc_query_grad, enc_qkv[0])
        + project_back(enc_key_grad, enc_qkv[1])
        + project_back(enc_value_grad, enc_qkv[2])
    )
    embed_grad = weight_grad(masked_series, enc_in_grad.astype(jnp.bfloat16))
    enc_query_bias_grad = row_total(enc_query_grad)
    enc_bias_grad = jnp.stack(
        [row_total(enc_value_grad), enc_out_bias, enc_ff_out_bias, enc_bias_one, enc_bias_two]
    )
    enc_gain_grad = jnp.stack([enc_gain_one, enc_gain_two])
    dec_bias_grad = jnp.stack(
        [
            row_total(self_query_grad),
            row_total(self_value_grad),
            self_out_bias,
            row_total(cross_query_grad),
            row_total(cross_value_grad),
            cross_out_bias,
            dec_ff_out_bias,
            dec_bias_one,
            dec_bias_two,
            dec_bias_three,
        ]
    )
    dec_gain_grad = jnp.stack([dec_gain_one, dec_gain_two, dec_gain_three])
    ff_bias_grad = jnp.stack([enc_ff_bias_grad, dec_ff_bias_grad])
    shares = (
        lax.psum_scatter(embed_grad, "seq", scatter_dimension=1, tiled=True),
        lax.psum_scatter(enc_qkv_grad, "seq", scatter_dimension=2, tiled=True),
        lax.psum_scatter(enc_out_grad, "seq", scatter_dimension=1, tiled=True),
        lax.psum_scatter(enc_ff_in_grad, "seq", scatter_dimension=1, tiled=True),
        lax.psum_scatter(enc_ff_out_grad, "seq", scatter_dimension=1, tiled=True),
        lax.psum_scatter(enc_query_bias_grad, "seq", scatter_dimension=0, tiled=True),
        lax.psum_scatter(enc_bias_grad, "seq", scatter_dimension=1, tiled=True),
        lax.psum_scatter(enc_gain_grad, "seq", scatter_dimension=1, tiled=True),
        lax.psum_scatter(dec_qkv_grad, "seq", scatter_dimension=2, tiled=True),
        lax.psum_scatter(dec_out_grad, "seq", scatter_dimension=1, tiled=True),
        lax.psum_scatter(cross_qkv_grad, "seq", scatter_dimension=2, tiled=True),
        lax.psum_scatter(cross_out_grad, "seq", scatter_dimension=1, tiled=True),
        lax.psum_scatter(dec_ff_in_grad, "seq", scatter_dimension=1, tiled=True),
        lax.psum_scatter(dec_ff_out_grad, "seq", scatter_dimension=1, tiled=True),
        lax.psum_scatter(dec_bias_grad, "seq", scatter_dimension=1, tiled=True),
        lax.psum_scatter(dec_gain_grad, "seq", scatter_dimension=1, tiled=True),
        lax.psum_scatter(ff_bias_grad, "seq", scatter_dimension=1, tiled=True),
    )
    summed = lax.psum(
        (
            shares[0],
            shares[1],
            shares[2],
            shares[3],
            shares[4],
            shares[5],
            shares[6],
            shares[7],
            shares[8],
            shares[9],
            shares[10],
            shares[11],
            shares[12],
            shares[13],
            shares[14],
            shares[15],
            shares[16],
        ),
        "batch",
    )
    return (
        decoded.astype(jnp.bfloat16),
        enc_in_grad,
        dec_in_grad,
        summed[0],
        summed[1],
        summed[2],
        summed[3],
        summed[4],
        summed[5],
        summed[6],
        summed[7],
        summed[8],
        summed[9],
        summed[10],
        summed[11],
        summed[12],
        summed[13],
        summed[14],
        summed[15],
        summed[16],
    )


def solution(mesh):
    in_specs = (
        P("batch", "seq", None),
        P("batch", "seq", None),
        P(),
        P("batch"),
        P("batch"),
        P("batch", "seq"),
        P("batch", "seq", None),
        P(),
        P(),
        P(),
        P(),
        P(),
        P(),
        P(),
        P(),
        P(),
        P(),
        P(),
        P(),
        P(),
        P(),
        P(),
        P(),
        P(),
        P("batch", "seq", None),
    )
    out_specs = (
        P("batch", "seq", None),
        P("batch", "seq", None),
        P("batch", "seq", None),
        P(None, "seq"),
        P(None, None, "seq"),
        P(None, "seq"),
        P(None, "seq"),
        P(None, "seq"),
        P("seq"),
        P(None, "seq"),
        P(None, "seq"),
        P(None, None, "seq"),
        P(None, "seq"),
        P(None, None, "seq"),
        P(None, "seq"),
        P(None, "seq"),
        P(None, "seq"),
        P(None, "seq"),
        P(None, "seq"),
        P(None, "seq"),
    )
    return jax.shard_map(local, mesh=mesh, in_specs=in_specs, out_specs=out_specs, check_vma=False)
```

profile of v0, /device:TPU:0, one launch (start us, length us, event | category | flops | bytes accessed | tf_op | source)
XLA Modules:
  0.0 1660.2 jit_solution(5009351621007973973)
XLA Ops:
  22.1 34.9 %all-reduce = bf16[1024]{0:T(1024)(128)(2,1)S(1)} all-reduce(bf16[1024]{0:T(1024)(128)(2,1)S(1)} %dynamic-update-slice), channel_id=1, replica_groups=mesh['seq'=16,'batch'=2] {'seq'}, use_global_device_ids=true, to_apply=%add | all-reduce | flops 1024 | bytes 4096
  61.5 33.1 %all-gather.35.cloned.1.call-done = bf16[1024,512]{1,0:T(8,128)(2,1)} async-done(((bf16[64,512]{1,0:T(8,128)(2,1)}), bf16[1024,512]{1,0:T(8,128)(2,1)}) %all-gather.35.cloned.1.call-update) | async-done | bytes 1048592 | tf_op jit(solution)/shard_map/all_gather | solution.py:279
  96.8 6.2 while.118
  115.5 18.1 %all-gather.33.cloned.1.call-done = bf16[1024,512]{1,0:T(8,128)(2,1)} async-done(((bf16[64,512]{1,0:T(8,128)(2,1)}), bf16[1024,512]{1,0:T(8,128)(2,1)}) %all-gather.33.cloned.1.call-update) | async-done | bytes 1048592 | tf_op jit(solution)/shard_map/all_gather | solution.py:306
  135.1 37.4 %all-gather.31.cloned.1.call-done = bf16[1024,512]{1,0:T(8,128)(2,1)} async-done(((bf16[64,512]{1,0:T(8,128)(2,1)}), bf16[1024,512]{1,0:T(8,128)(2,1)}) %all-gather.31.cloned.1.call-update) | async-done | bytes 1048592 | tf_op jit(solution)/shard_map/all_gather | solution.py:305
  176.8 11.1 while.117
  198.6 12.8 all-gather.41.cloned.1.call-done
  213.7 37.2 %all-gather.39.cloned.1.call-done = bf16[1024,512]{1,0:T(8,128)(2,1)} async-done(((bf16[64,512]{1,0:T(8,128)(2,1)}), bf16[1024,512]{1,0:T(8,128)(2,1)}) %all-gather.39.cloned.1.call-update) | async-done | bytes 1048592 | tf_op jit(solution)/shard_map/all_gather | solution.py:325
  253.2 6.9 while.119
  282.8 19.5 %all-gather.15 = f32[16,64,8]{1,2,0:T(8,128)S(1)} all-gather(f32[1,64,8]{1,2,0:T(8,128)S(1)} %copy.228), channel_id=10, replica_groups=mesh['seq'=16,'batch'=2] {'seq'}, dimensions={0}, use_global_device_ids=true | all-gather | bytes 34816 | tf_op jit(solution)/shard_map/all_gather | solution.py:395
  303.1 19.6 %all_gather.74 = f32[1,1024,8]{2,0,1:T(1,128)S(1)} all-gather(f32[1,64,8]{2,0,1:T(1,128)S(1)} %bitcast.996), channel_id=1, replica_groups=mesh['seq'=16,'batch'=2] {'seq'}, dimensions={1}, use_global_device_ids=true | all-gather | bytes 34816 | tf_op jit(solution)/shard_map/all_gather | solution.py:394
  323.4 5.6 all-gather.45.cloned.1.call-done
  329.1 18.2 %while.120 = (s32[]{:T(128)}, f32[1,8,64,64]{3,2,1,0:T(8,128)}, f32[1,8,64,64]{3,2,1,0:T(8,128)}, f32[1]{0:T(128)}, bf16[2,1,512,512]{3,2,0,1:T(8,128)(2,1)}, /*...) while((s32[]{:T(128)}, f32[1,8,64,64]{3,2,1,0:T(8,128)}, ...), condition=%wide.region_28.29_spmd.clone, body=%wide.region_27.28_spmd.clone.sunk | while | flops 136183808 | bytes 10224032 | solution.py:72
  364.4 20.8 %all_gather.78 = f32[1,1024,8]{2,0,1:T(1,128)S(1)} all-gather(f32[1,64,8]{2,0,1:T(1,128)S(1)} %bitcast.997), channel_id=1, replica_groups=mesh['seq'=16,'batch'=2] {'seq'}, dimensions={1}, use_global_device_ids=true | all-gather | bytes 34816 | tf_op jit(solution)/shard_map/all_gather | solution.py:529
  386.7 8.6 while.123
  400.6 7.3 while.121
  409.7 17.7 %all-gather.16 = f32[16,64,8]{1,2,0:T(8,128)S(1)} all-gather(f32[1,64,8]{1,2,0:T(8,128)S(1)} %copy.250), channel_id=13, replica_groups=mesh['seq'=16,'batch'=2] {'seq'}, dimensions={0}, use_global_device_ids=true | all-gather | bytes 34816 | tf_op jit(solution)/shard_map/all_gather | solution.py:530
  433.0 5.2 copy.290
  443.8 16.0 while.122
  464.9 5.1 copy.289
  475.2 3.5 fusion.230
  479.7 2.8 fusion.264
  486.7 3.6 fusion.221
  493.0 23.5 %all_gather.82 = f32[1,1024,8]{2,0,1:T(1,128)S(1)} all-gather(f32[1,64,8]{2,0,1:T(1,128)S(1)} %bitcast.998), channel_id=1, replica_groups=mesh['seq'=16,'batch'=2] {'seq'}, dimensions={1}, use_global_device_ids=true | all-gather | bytes 34816 | tf_op jit(solution)/shard_map/all_gather | solution.py:460
  518.6 18.6 %all-gather.17 = f32[16,64,8]{1,2,0:T(8,128)S(1)} all-gather(f32[1,64,8]{1,2,0:T(8,128)S(1)} %copy.279), channel_id=16, replica_groups=mesh['seq'=16,'batch'=2] {'seq'}, dimensions={0}, use_global_device_ids=true | all-gather | bytes 34816 | tf_op jit(solution)/shard_map/all_gather | solution.py:461
  538.0 2.8 fusion.261
  542.0 11.8 while.124
  545.5 2.4 fusion.494
  551.3 2.5 fusion.494
  557.2 13.7 while.125
  582.4 80.3 %all-reduce.10.cloned.1.call-done = (f32[3,512,512]{1,0,2:T(4,128)}, f32[3,512,512]{1,0,2:T(4,128)}) async-done(((f32[3,512,512]{1,0,2:T(4,128)}, f32[3,512,512]{1,0,2:T(4,128)}), (f32[3,512,512]{1,0,2:T(4,128)}, f32[3,512,512]{1,0,2:T(4,128)})) %all-reduce.10.cloned.1.call-update) | async-done | bytes 6291472
  666.1 57.7 %reduce-scatter.37.cloned.1.call-done = f32[512,32]{0,1:T(8,128)} async-done(((f32[512,512]{0,1:T(8,128)}), f32[512,32]{0,1:T(8,128)}) %reduce-scatter.37.cloned.1.call-update) | async-done | bytes 65552 | tf_op jit(solution)/shard_map/reduce_scatter | solution.py:583
  723.8 59.9 %reduce-scatter.35.cloned.1.call-done = f32[512,32]{0,1:T(8,128)} async-done(((f32[512,512]{0,1:T(8,128)}), f32[512,32]{0,1:T(8,128)}) %reduce-scatter.35.cloned.1.call-update) | async-done | bytes 65552 | tf_op jit(solution)/shard_map/reduce_scatter | solution.py:581
  783.8 60.4 %reduce-scatter.27.cloned.1.call-done = f32[512,32]{0,1:T(8,128)} async-done(((f32[512,512]{0,1:T(8,128)}), f32[512,32]{0,1:T(8,128)}) %reduce-scatter.27.cloned.1.call-update) | async-done | bytes 65552 | tf_op jit(solution)/shard_map/reduce_scatter | solution.py:574
  844.1 75.5 %reduce-scatter.41.cloned.1.call-done = f32[2048,32]{0,1:T(8,128)} async-done(((f32[2048,512]{0,1:T(8,128)}), f32[2048,32]{0,1:T(8,128)}) %reduce-scatter.41.cloned.1.call-update) | async-done | bytes 262160 | tf_op jit(solution)/shard_map/reduce_scatter | solution.py:585
  919.7 75.9 %reduce-scatter.39.cloned.1.call-done = f32[512,128]{1,0:T(8,128)} async-done(((f32[512,2048]{1,0:T(8,128)}), f32[512,128]{1,0:T(8,128)}) %reduce-scatter.39.cloned.1.call-update) | async-done | bytes 262160 | tf_op jit(solution)/shard_map/reduce_scatter | solution.py:584
  995.6 63.4 %reduce-scatter.25.cloned.1.call-done = f32[862,32]{0,1:T(8,128)} async-done(((f32[862,512]{0,1:T(8,128)}), f32[862,32]{0,1:T(8,128)}) %reduce-scatter.25.cloned.1.call-update) | async-done | bytes 110352 | tf_op jit(solution)/shard_map/reduce_scatter | solution.py:572
  1059.0 75.1 %reduce-scatter.31.cloned.1.call-done = f32[2048,32]{0,1:T(8,128)} async-done(((f32[2048,512]{0,1:T(8,128)}), f32[2048,32]{0,1:T(8,128)}) %reduce-scatter.31.cloned.1.call-update) | async-done | bytes 262160 | tf_op jit(solution)/shard_map/reduce_scatter | solution.py:576
  1134.1 76.1 %reduce-scatter.29.cloned.1.call-done = f32[512,128]{1,0:T(8,128)} async-done(((f32[512,2048]{1,0:T(8,128)}), f32[512,128]{1,0:T(8,128)}) %reduce-scatter.29.cloned.1.call-update) | async-done | bytes 262160 | tf_op jit(solution)/shard_map/reduce_scatter | solution.py:575
  1210.2 69.0 %reduce-scatter.33.cloned.1.call-done = f32[3,512,32]{1,2,0:T(8,128)} async-done(((f32[3,512,512]{1,2,0:T(8,128)}), f32[3,512,32]{1,2,0:T(8,128)}) %reduce-scatter.33.cloned.1.call-update) | async-done | bytes 196624 | tf_op jit(solution)/shard_map/reduce_scatter | solution.py:580
  1279.3 29.7 %all-reduce.2 = f32[512]{0:T(512)S(1)} all-reduce(f32[512]{0:T(512)S(1)} %reduce_sum.502), channel_id=22, replica_groups=mesh['seq'=16,'batch'=2] {'seq'}, use_global_device_ids=true, to_apply=%region_58.59.clone | all-reduce | flops 512 | bytes 4096
  1309.1 28.4 %reduce-scatter.45.cloned.1.call-done = f32[32,2]{1,0:T(8,128)} async-done(((f32[512,2]{1,0:T(8,128)}), f32[32,2]{1,0:T(8,128)}) %reduce-scatter.45.cloned.1.call-update) | async-done | bytes 272
  1338.3 56.9 %reduce-scatter.49.cloned.1.call-done = f32[32,3]{1,0:T(8,128)} async-done(((f32[512,3]{1,0:T(8,128)}), f32[32,3]{1,0:T(8,128)}) %reduce-scatter.49.cloned.1.call-update) | async-done | bytes 400
  1396.0 59.3 %reduce-scatter.51.cloned.1.call-done = f32[128,2]{1,0:T(8,128)} async-done(((f32[2048,2]{1,0:T(8,128)}), f32[128,2]{1,0:T(8,128)}) %reduce-scatter.51.cloned.1.call-update) | async-done | bytes 1040
  1459.0 55.0 %reduce-scatter.43.cloned.1.call-done = f32[32,5]{1,0:T(8,128)} async-done(((f32[512,5]{1,0:T(8,128)}), f32[32,5]{1,0:T(8,128)}) %reduce-scatter.43.cloned.1.call-update) | async-done | bytes 656
  1514.8 57.3 %reduce-scatter.47.cloned.1.call-done = f32[32,10]{1,0:T(8,128)} async-done(((f32[512,10]{1,0:T(8,128)}), f32[32,10]{1,0:T(8,128)}) %reduce-scatter.47.cloned.1.call-update) | async-done | bytes 1296
  1572.9 8.9 all-reduce.5
  1581.8 58.2 %all-reduce.12.cloned.1.call-done = (f32[862,32]{0,1:T(8,128)}, f32[3,512,32]{1,0,2:T(4,128)}, f32[512,32]{0,1:T(8,128)}, f32[512,128]{1,0:T(8,128)}, f32[2048,3...) async-done(((f32[862,32]{0,1:T(8,128)}, ...) | async-done | bytes 1945360 | tf_op jit(solution)/shard_map/psum | solution.py:590
  (869 shorter events, 265.3 us)
Async XLA Ops:
  7.2 260.2 %copy-start = (bf16[2048,512]{1,0:T(8,128)(2,1)S(1)}, bf16[2048,512]{1,0:T(8,128)(2,1)}, u32[]{:S(2)}) copy-start(bf16[2048,512]{1,0:T(8,128)(2,1)} %param.63) | copy-start | bytes 6291460
  7.2 51.9 %all-gather.37.cloned.1.call-start = ((), (), s32[]{:S(2)}) async-start(), calls=%async_computation.26 | async-start | bytes 1114112 | tf_op jit(solution)/shard_map/all_gather | solution.py:280
  9.6 97.9 %copy-start.126 = (f32[1,512]{1,0:T(1,128)}, f32[1,512]{1,0:T(1,128)S(1)}, u32[]{:S(2)}) copy-start(f32[1,512]{1,0:T(1,128)S(1)} %get-tuple-element.1592) | copy-start | bytes 6148
  10.6 46.5 %copy-start.172 = (f32[2,512]{1,0:T(2,128)S(1)}, f32[2,512]{1,0:T(2,128)}, u32[]{:S(2)}) copy-start(f32[2,512]{1,0:T(2,128)} %param.57) | copy-start | bytes 12292
  10.6 47.1 %copy-start.192 = (f32[512]{0:T(512)S(1)}, f32[512]{0:T(512)}, u32[]{:S(2)}) copy-start(f32[512]{0:T(512)} %param.55) | copy-start | bytes 6148
  12.1 47.1 %copy-start.39 = (bf16[1,64,512]{2,1,0:T(8,128)(2,1)}, bf16[1,64,512]{2,1,0:T(8,128)(2,1)S(1)}, u32[]{:S(2)}) copy-start(bf16[1,64,512]{2,1,0:T(8,128)(2,1)S(1)} %get-tuple-element.1603) | copy-start | bytes 196612
  14.0 80.5 %all-gather.35.cloned.1.call-start = ((), (), s32[]{:S(2)}) async-start(), calls=%async_computation.25 | async-start | bytes 1114112 | tf_op jit(solution)/shard_map/all_gather | solution.py:279
  16.0 117.6 %all-gather.33.cloned.1.call-start = ((), (), s32[]{:S(2)}) async-start(), calls=%async_computation.24 | async-start | bytes 1114112 | tf_op jit(solution)/shard_map/all_gather | solution.py:306
  18.5 154.0 %all-gather.31.cloned.1.call-start = ((), (), s32[]{:S(2)}) async-start(), calls=%async_computation.23 | async-start | bytes 1114112 | tf_op jit(solution)/shard_map/all_gather | solution.py:305
  20.5 190.9 %all-gather.41.cloned.1.call-start = ((), (), s32[]{:S(2)}) async-start(), calls=%async_computation.28 | async-start | bytes 1114112 | tf_op jit(solution)/shard_map/all_gather | solution.py:326
  57.1 50.4 %copy-start.116 = (f32[1,512]{1,0:T(1,128)}, f32[1,512]{1,0:T(1,128)S(1)}, u32[]{:S(2)}) copy-start(f32[1,512]{1,0:T(1,128)S(1)} %get-tuple-element.1600) | copy-start | bytes 6148
  57.1 53.0 %copy-start.124 = (f32[1,512]{1,0:T(1,128)}, f32[1,512]{1,0:T(1,128)S(1)}, u32[]{:S(2)}) copy-start(f32[1,512]{1,0:T(1,128)S(1)} %get-tuple-element.1599) | copy-start | bytes 6148
  112.1 138.8 %all-gather.39.cloned.1.call-start = ((), (), s32[]{:S(2)}) async-start(), calls=%async_computation.27 | async-start | bytes 1114112 | tf_op jit(solution)/shard_map/all_gather | solution.py:325
  176.7 146.7 %all-gather.43.cloned.1.call-start = ((), (), s32[]{:S(2)}) async-start(), calls=%async_computation.29 | async-start | bytes 1114112 | tf_op jit(solution)/shard_map/all_gather | solution.py:392
  197.4 131.7 %all-gather.45.cloned.1.call-start = ((), (), s32[]{:S(2)}) async-start(), calls=%async_computation.30 | async-start | bytes 1114112 | tf_op jit(solution)/shard_map/all_gather | solution.py:393
  276.0 47.5 %copy-start.188 = (f32[64]{0:T(128)}, f32[64]{0:T(128)S(1)}, u32[]{:S(2)}) copy-start(f32[64]{0:T(128)S(1)} %negate_multiply_fusion.5) | copy-start | bytes 772
  277.3 51.8 %copy-start.60 = (bf16[1,64,512]{2,1,0:T(8,128)(2,1)}, bf16[1,64,512]{2,1,0:T(8,128)(2,1)S(1)}, u32[]{:S(2)}) copy-start(bf16[1,64,512]{2,1,0:T(8,128)(2,1)S(1)} %get-tuple-element.1525) | copy-start | bytes 196612
  278.2 165.5 %all-gather.47.cloned.1.call-start = ((), (), s32[]{:S(2)}) async-start(), calls=%async_computation.31 | async-start | bytes 1114112 | tf_op jit(solution)/shard_map/all_gather | solution.py:527
  279.0 164.8 %all-gather.49.cloned.1.call-start = ((), (), s32[]{:S(2)}) async-start(), calls=%async_computation.32 | async-start | bytes 1114112 | tf_op jit(solution)/shard_map/all_gather | solution.py:528
  361.6 195.6 %all-gather.51.cloned.1.call-start = ((), (), s32[]{:S(2)}) async-start(), calls=%async_computation.33 | async-start | bytes 1114112 | tf_op jit(solution)/shard_map/all_gather | solution.py:458
  362.3 194.9 %all-gather.53.cloned.1.call-start = ((), (), s32[]{:S(2)}) async-start(), calls=%async_computation.34 | async-start | bytes 1114112 | tf_op jit(solution)/shard_map/all_gather | solution.py:459
  443.5 219.2 %all-reduce.10.cloned.1.call-start = ((), (), s32[]{:S(2)}) async-start(), calls=%async_computation.40 | async-start | bytes 16777216
  470.1 253.7 %reduce-scatter.37.cloned.1.call-start = ((), (), s32[]{:S(2)}) async-start(), calls=%async_computation.20 | async-start | bytes 1114112 | tf_op jit(solution)/shard_map/reduce_scatter | solution.py:583
  472.2 311.5 %reduce-scatter.35.cloned.1.call-start = ((), (), s32[]{:S(2)}) async-start(), calls=%async_computation.19 | async-start | bytes 1114112 | tf_op jit(solution)/shard_map/reduce_scatter | solution.py:581
  473.7 370.5 %reduce-scatter.27.cloned.1.call-start = ((), (), s32[]{:S(2)}) async-start(), calls=%async_computation.15 | async-start | bytes 1114112 | tf_op jit(solution)/shard_map/reduce_scatter | solution.py:574
  475.1 444.5 %reduce-scatter.41.cloned.1.call-start = ((), (), s32[]{:S(2)}) async-start(), calls=%async_computation.22 | async-start | bytes 4456448 | tf_op jit(solution)/shard_map/reduce_scatter | solution.py:585
  478.7 516.8 %reduce-scatter.39.cloned.1.call-start = ((), (), s32[]{:S(2)}) async-start(), calls=%async_computation.21 | async-start | bytes 4456448 | tf_op jit(solution)/shard_map/reduce_scatter | solution.py:584
  482.6 576.3 %reduce-scatter.25.cloned.1.call-start = ((), (), s32[]{:S(2)}) async-start(), calls=%async_computation.14 | async-start | bytes 1949696 | tf_op jit(solution)/shard_map/reduce_scatter | solution.py:572
  486.6 647.5 %reduce-scatter.31.cloned.1.call-start = ((), (), s32[]{:S(2)}) async-start(), calls=%async_computation.17 | async-start | bytes 4456448 | tf_op jit(solution)/shard_map/reduce_scatter | solution.py:576
  490.3 47.7 %copy-start.21 = (f32[1,64,512]{2,1,0:T(8,128)S(1)}, f32[1,64,512]{2,1,0:T(8,128)}, u32[]{:S(2)}) copy-start(f32[1,64,512]{2,1,0:T(8,128)} %copy-done.19) | copy-start | bytes 393220
  490.3 47.7 %copy-start.56 = (bf16[64,2048]{1,0:T(8,128)(2,1)S(1)}, bf16[64,2048]{1,0:T(8,128)(2,1)}, u32[]{:S(2)}) copy-start(bf16[64,2048]{1,0:T(8,128)(2,1)} %copy-done.55) | copy-start | bytes 786436
  490.3 47.7 %copy-start.118 = (f32[1,512]{1,0:T(1,128)S(1)}, f32[1,512]{1,0:T(1,128)}, u32[]{:S(2)}) copy-start(f32[1,512]{1,0:T(1,128)} %copy-done.116) | copy-start | bytes 6148
  490.3 47.7 %copy-start.127 = (f32[1,512]{1,0:T(1,128)S(1)}, f32[1,512]{1,0:T(1,128)}, u32[]{:S(2)}) copy-start(f32[1,512]{1,0:T(1,128)} %copy-done.126) | copy-start | bytes 6148
  490.3 47.7 %copy-start.138 = (f32[64]{0:T(128)S(1)}, f32[64]{0:T(128)}, u32[]{:S(2)}) copy-start(f32[64]{0:T(128)} %copy-done.136) | copy-start | bytes 772
  490.4 47.7 %copy-start.163 = (f32[64]{0:T(128)S(1)}, f32[64]{0:T(128)}, u32[]{:S(2)}) copy-start(f32[64]{0:T(128)} %copy-done.161) | copy-start | bytes 772
  490.4 719.8 %reduce-scatter.29.cloned.1.call-start = ((), (), s32[]{:S(2)}) async-start(), calls=%async_computation.16 | async-start | bytes 4456448 | tf_op jit(solution)/shard_map/reduce_scatter | solution.py:575
  540.8 738.4 %reduce-scatter.33.cloned.1.call-start = ((), (), s32[]{:S(2)}) async-start(), calls=%async_computation.18 | async-start | bytes 3342336 | tf_op jit(solution)/shard_map/reduce_scatter | solution.py:580
  575.3 762.2 %reduce-scatter.45.cloned.1.call-start = ((), (), s32[]{:S(2)}) async-start(), calls=%async_computation.36 | async-start | bytes 278528
  576.7 818.5 %reduce-scatter.49.cloned.1.call-start = ((), (), s32[]{:S(2)}) async-start(), calls=%async_computation.38 | async-start | bytes 278528
  577.7 877.7 %reduce-scatter.51.cloned.1.call-start = ((), (), s32[]{:S(2)}) async-start(), calls=%async_computation.39 | async-start | bytes 1114112
  579.2 934.8 %reduce-scatter.43.cloned.1.call-start = ((), (), s32[]{:S(2)}) async-start(), calls=%async_computation.35 | async-start | bytes 278528
  580.2 699.0 %copy-start.132 = (f32[8,64]{1,0:T(8,128)S(1)}, f32[8,64]{1,0:T(8,128)}, u32[]{:S(2)}) copy-start(f32[8,64]{1,0:T(8,128)} %get-tuple-element.1623) | copy-start | bytes 6148
  580.2 876.0 %copy-start.32 = (bf16[3,512,512]{2,1,0:T(8,128)(2,1)S(1)}, bf16[3,512,512]{2,1,0:T(8,128)(2,1)}, u32[]{:S(2)}) copy-start(bf16[3,512,512]{2,1,0:T(8,128)(2,1)} %param.58) | copy-start | bytes 4718596
  580.3 991.9 %reduce-scatter.47.cloned.1.call-start = ((), (), s32[]{:S(2)}) async-start(), calls=%async_computation.37 | async-start | bytes 278528
  582.3 1057.6 %all-reduce.12.cloned.1.call-start = ((), (), s32[]{:S(2)}) async-start(), calls=%async_computation.41 | async-start | bytes 4161536 | tf_op jit(solution)/shard_map/psum | solution.py:590
  664.4 792.5 %copy-start.49 = (f32[1,64,512]{2,1,0:T(8,128)S(1)}, f32[1,64,512]{2,1,0:T(8,128)}, u32[]{:S(2)}) copy-start(f32[1,64,512]{2,1,0:T(8,128)} %copy-done.48) | copy-start | bytes 393220
  664.4 792.5 %copy-start.174 = (f32[64]{0:T(128)S(1)}, f32[64]{0:T(128)}, u32[]{:S(2)}) copy-start(f32[64]{0:T(128)} %copy-done.173) | copy-start | bytes 772
  1456.9 196.3 %copy-start.1 = (bf16[2048,512]{1,0:T(8,128)(2,1)S(1)}, bf16[2048,512]{1,0:T(8,128)(2,1)}, u32[]{:S(2)}) copy-start(bf16[2048,512]{1,0:T(8,128)(2,1)} %param.63) | copy-start | bytes 6291460
  (185 other events, 1229.0 us)
Sparse Core Ops, SparseCore 0:
  14.1 40.6 all-gather.36
  57.6 36.8 all-gather.34
  96.7 36.8 all-gather.32
  135.6 36.8 all-gather.30
  174.5 36.8 all-gather.40
  214.0 36.8 all-gather.38
  253.1 36.8 all-gather.42
  292.2 36.8 all-gather.44
  331.3 37.0 all-gather.46
  370.9 36.8 all-gather.48
  410.0 36.8 all-gather.50
  449.5 36.9 all-gather.52
  490.3 172.3 all-reduce.9
  666.6 57.2 reduce-scatter.36
  727.3 56.4 reduce-scatter.34
  787.7 56.4 reduce-scatter.26
  847.9 71.7 reduce-scatter.40
  923.9 71.6 reduce-scatter.38
  999.3 59.6 reduce-scatter.24
  1062.7 71.3 reduce-scatter.30
  1138.4 71.7 reduce-scatter.28
  1214.0 65.1 reduce-scatter.32
  1283.3 54.1 reduce-scatter.44
  1340.9 54.2 reduce-scatter.48
  1398.9 56.4 reduce-scatter.50
  1459.7 54.2 reduce-scatter.42
  1517.8 54.2 reduce-scatter.46
  1576.5 63.3 all-reduce.11
where the time goes:
time: 1670 us; the launch traced here: 1660 us
  waiting for transfers between devices  1150 us (69%)
  blocking collectives  193 us (12%)
  local copies, waits for them, and re-layouts  130 us (8%)
  matrix products  127 us (8%)
  other arithmetic  32.3 us (2%)
  between operations  20.1 us (1%)
    unnamed x34, waiting for transfers between devices  339 us
    reduce_scatter x1, waiting for transfers between devices, local(): lax.psum_scatter(enc_ff_in_grad, 'seq', scatter_dimension=1, tiled=True)  76.1 us
    reduce_scatter x1, waiting for transfers between devices, local(): lax.psum_scatter(dec_ff_in_grad, 'seq', scatter_dimension=1, tiled=True)  75.9 us
    reduce_scatter x1, waiting for transfers between devices, local(): lax.psum_scatter(dec_ff_out_grad, 'seq', scatter_dimension=1, tiled=True)  75.5 us
    reduce_scatter x1, waiting for transfers between devices, local(): lax.psum_scatter(enc_ff_out_grad, 'seq', scatter_dimension=1, tiled=True)  75.1 us
    reduce_scatter x1, waiting for transfers between devices, local(): lax.psum_scatter(dec_qkv_grad, 'seq', scatter_dimension=2, tiled=True)  69 us
    unnamed x2, blocking collectives  64.6 us
    reduce_scatter x1, waiting for transfers between devices, local(): lax.psum_scatter(embed_grad, 'seq', scatter_dimension=1, tiled=True)  63.4 us
  transfers between devices with their start and end apart: 28, of which 22 were waited for; matrix products, arithmetic and copies ran while one was open for 16% of the time, Pallas kernels for 0%

commit v1 on v0

--- a/solution.py
+++ b/solution.py
@@ -4,10 +4,14 @@
 import jax
 import jax.numpy as jnp
 from jax import lax
+from jax.experimental import pallas as pl
+from jax.experimental.pallas import tpu as pltpu
 from jax.sharding import PartitionSpec as P
 
 HEADS = 8
 GROUPS = 16
+SEQ = "seq"
+BATCH = "batch"
 
 
 epsilon = 1e-05
@@ -255,7 +259,7 @@
     item_count, enc_rows, width = enc_in.shape
     dec_rows = dec_in.shape[1]
     head_size = width // HEADS
-    seq_index = lax.axis_index("seq")
+    seq_index = lax.axis_index(SEQ)
     enc_pos = seq_index * enc_rows + jnp.arange(enc_rows, dtype=jnp.int32)
     dec_pos = seq_index * dec_rows + jnp.arange(dec_rows, dtype=jnp.int32)
     enc_shift = delta_shift.astype(jnp.float32)
@@ -276,9 +280,9 @@
         enc_update(
             fresh_totals(item_count, enc_rows, head_size),
             (
-                lax.all_gather(enc_key, "seq", axis=1, tiled=True),
-                lax.all_gather(enc_value, "seq", axis=1, tiled=True),
-                lax.all_gather(delta_shift, "seq", axis=1, tiled=True),
+                lax.all_gather(enc_key, SEQ, axis=1, tiled=True),
+                lax.all_gather(enc_value, SEQ, axis=1, tiled=True),
+                lax.all_gather(delta_shift, SEQ, axis=1, tiled=True),
             ),
             jnp.int32(0),
         )
@@ -302,8 +306,8 @@
         self_update(
             fresh_totals(item_count, dec_rows, head_size),
             (
-                lax.all_gather(self_key, "seq", axis=1, tiled=True),
-                lax.all_gather(self_value, "seq", axis=1, tiled=True),
+                lax.all_gather(self_key, SEQ, axis=1, tiled=True),
+                lax.all_gather(self_value, SEQ, axis=1, tiled=True),
             ),
             jnp.int32(0),
         )
@@ -322,9 +326,9 @@
     cross_totals = cross_update(
         cross_start,
         (
-            lax.all_gather(cross_key, "seq", axis=1, tiled=True),
-            lax.all_gather(cross_value, "seq", axis=1, tiled=True),
-            lax.all_gather(delta_shift, "seq", axis=1, tiled=True),
+            lax.all_gather(cross_key, SEQ, axis=1, tiled=True),
+            lax.all_gather(cross_value, SEQ, axis=1, tiled=True),
+            lax.all_gather(delta_shift, SEQ, axis=1, tiled=True),
         ),
         jnp.int32(0),
     )
@@ -366,9 +370,9 @@
     cross_query_total = cross_back(
         cross_query_start,
         (
-            lax.all_gather(cross_key, "seq", axis=1, tiled=True),
-            lax.all_gather(cross_value, "seq", axis=1, tiled=True),
-            lax.all_gather(delta_shift, "seq", axis=1, tiled=True),
+            lax.all_gather(cross_key, SEQ, axis=1, tiled=True),
+            lax.all_gather(cross_value, SEQ, axis=1, tiled=True),
+            lax.all_gather(delta_shift, SEQ, axis=1, tiled=True),
         ),
         jnp.int32(0),
     )
@@ -389,10 +393,10 @@
     cross_key_total, cross_value_total = cross_key_update(
         cross_key_start,
         (
-            lax.all_gather(cross_query.astype(jnp.float32), "seq", axis=1, tiled=True),
-            lax.all_gather(cross_mixed_grad.astype(jnp.float32), "seq", axis=1, tiled=True),
-            lax.all_gather(cross_log, "seq", axis=1, tiled=True),
-            lax.all_gather(cross_dot, "seq", axis=1, tiled=True),
+            lax.all_gather(cross_query.astype(jnp.float32), SEQ, axis=1, tiled=True),
+            lax.all_gather(cross_mixed_grad.astype(jnp.float32), SEQ, axis=1, tiled=True),
+            lax.all_gather(cross_log, SEQ, axis=1, tiled=True),
+            lax.all_gather(cross_dot, SEQ, axis=1, tiled=True),
         ),
         jnp.int32(0),
     )
@@ -433,8 +437,8 @@
     self_query_total = self_back(
         jnp.zeros((item_count, HEADS, dec_rows, head_size), jnp.float32),
         (
-            lax.all_gather(self_key, "seq", axis=1, tiled=True),
-            lax.all_gather(self_value, "seq", axis=1, tiled=True),
+            lax.all_gather(self_key, SEQ, axis=1, tiled=True),
+            lax.all_gather(self_value, SEQ, axis=1, tiled=True),
         ),
         jnp.int32(0),
     )
@@ -455,10 +459,10 @@
     self_key_total, self_value_total = self_key_update(
         self_key_start,
         (
-            lax.all_gather(self_query.astype(jnp.float32), "seq", axis=1, tiled=True),
-            lax.all_gather(self_mixed_grad.astype(jnp.float32), "seq", axis=1, tiled=True),
-            lax.all_gather(self_log, "seq", axis=1, tiled=True),
-            lax.all_gather(self_dot, "seq", axis=1, tiled=True),
+            lax.all_gather(self_query.astype(jnp.float32), SEQ, axis=1, tiled=True),
+            lax.all_gather(self_mixed_grad.astype(jnp.float32), SEQ, axis=1, tiled=True),
+            lax.all_gather(self_log, SEQ, axis=1, tiled=True),
+            lax.all_gather(self_dot, SEQ, axis=1, tiled=True),
         ),
         jnp.int32(0),
     )
@@ -507,9 +511,9 @@
     enc_query_total = enc_back(
         jnp.zeros((item_count, HEADS, enc_rows, head_size), jnp.float32),
         (
-            lax.all_gather(enc_key, "seq", axis=1, tiled=True),
-            lax.all_gather(enc_value, "seq", axis=1, tiled=True),
-            lax.all_gather(delta_shift, "seq", axis=1, tiled=True),
+            lax.all_gather(enc_key, SEQ, axis=1, tiled=True),
+            lax.all_gather(enc_value, SEQ, axis=1, tiled=True),
+            lax.all_gather(delta_shift, SEQ, axis=1, tiled=True),
         ),
         jnp.int32(0),
     )
@@ -524,10 +528,10 @@
     enc_key_total, enc_value_total = enc_key_update(
         enc_key_start,
         (
-            lax.all_gather(enc_query.astype(jnp.float32), "seq", axis=1, tiled=True),
-            lax.all_gather(enc_mixed_grad.astype(jnp.float32), "seq", axis=1, tiled=True),
-            lax.all_gather(enc_log, "seq", axis=1, tiled=True),
-            lax.all_gather(enc_dot, "seq", axis=1, tiled=True),
+            lax.all_gather(enc_query.astype(jnp.float32), SEQ, axis=1, tiled=True),
+            lax.all_gather(enc_mixed_grad.astype(jnp.float32), SEQ, axis=1, tiled=True),
+            lax.all_gather(enc_log, SEQ, axis=1, tiled=True),
+            lax.all_gather(enc_dot, SEQ, axis=1, tiled=True),
         ),
         jnp.int32(0),
     )
@@ -569,23 +573,23 @@
     dec_gain_grad = jnp.stack([dec_gain_one, dec_gain_two, dec_gain_three])
     ff_bias_grad = jnp.stack([enc_ff_bias_grad, dec_ff_bias_grad])
     shares = (
-        lax.psum_scatter(embed_grad, "seq", scatter_dimension=1, tiled=True),
-        lax.psum_scatter(enc_qkv_grad, "seq", scatter_dimension=2, tiled=True),
-        lax.psum_scatter(enc_out_grad, "seq", scatter_dimension=1, tiled=True),
-        lax.psum_scatter(enc_ff_in_grad, "seq", scatter_dimension=1, tiled=True),
-        lax.psum_scatter(enc_ff_out_grad, "seq", scatter_dimension=1, tiled=True),
-        lax.psum_scatter(enc_query_bias_grad, "seq", scatter_dimension=0, tiled=True),
-        lax.psum_scatter(enc_bias_grad, "seq", scatter_dimension=1, tiled=True),
-        lax.psum_scatter(enc_gain_grad, "seq", scatter_dimension=1, tiled=True),
-        lax.psum_scatter(dec_qkv_grad, "seq", scatter_dimension=2, tiled=True),
-        lax.psum_scatter(dec_out_grad, "seq", scatter_dimension=1, tiled=True),
-        lax.psum_scatter(cross_qkv_grad, "seq", scatter_dimension=2, tiled=True),
-        lax.psum_scatter(cross_out_grad, "seq", scatter_dimension=1, tiled=True),
-        lax.psum_scatter(dec_ff_in_grad, "seq", scatter_dimension=1, tiled=True),
-        lax.psum_scatter(dec_ff_out_grad, "seq", scatter_dimension=1, tiled=True),
-        lax.psum_scatter(dec_bias_grad, "seq", scatter_dimension=1, tiled=True),
-        lax.psum_scatter(dec_gain_grad, "seq", scatter_dimension=1, tiled=True),
-        lax.psum_scatter(ff_bias_grad, "seq", scatter_dimension=1, tiled=True),
+        lax.psum_scatter(embed_grad, SEQ, scatter_dimension=1, tiled=True),
+        lax.psum_scatter(enc_qkv_grad, SEQ, scatter_dimension=2, tiled=True),
+        lax.psum_scatter(enc_out_grad, SEQ, scatter_dimension=1, tiled=True),
+        lax.psum_scatter(enc_ff_in_grad, SEQ, scatter_dimension=1, tiled=True),
+        lax.psum_scatter(enc_ff_out_grad, SEQ, scatter_dimension=1, tiled=True),
+        lax.psum_scatter(enc_query_bias_grad, SEQ, scatter_dimension=0, tiled=True),
+        lax.psum_scatter(enc_bias_grad, SEQ, scatter_dimension=1, tiled=True),
+        lax.psum_scatter(enc_gain_grad, SEQ, scatter_dimension=1, tiled=True),
+        lax.psum_scatter(dec_qkv_grad, SEQ, scatter_dimension=2, tiled=True),
+        lax.psum_scatter(dec_out_grad, SEQ, scatter_dimension=1, tiled=True),
+        lax.psum_scatter(cross_qkv_grad, SEQ, scatter_dimension=2, tiled=True),
+        lax.psum_scatter(cross_out_grad, SEQ, scatter_dimension=1, tiled=True),
+        lax.psum_scatter(dec_ff_in_grad, SEQ, scatter_dimension=1, tiled=True),
+        lax.psum_scatter(dec_ff_out_grad, SEQ, scatter_dimension=1, tiled=True),
+        lax.psum_scatter(dec_bias_grad, SEQ, scatter_dimension=1, tiled=True),
+        lax.psum_scatter(dec_gain_grad, SEQ, scatter_dimension=1, tiled=True),
+        lax.psum_scatter(ff_bias_grad, SEQ, scatter_dimension=1, tiled=True),
     )
     summed = lax.psum(
         (
@@ -607,7 +611,7 @@
             shares[15],
             shares[16],
         ),
-        "batch",
+        BATCH,
     )
     return (
         decoded.astype(jnp.bfloat16),
@@ -633,15 +637,1178 @@
     )
 
 
+F32 = jnp.float32
+BF16 = jnp.bfloat16
+MESH = pl.DeviceIdType.MESH
+QUAD = 4
+HALVES = 2
+CORES = 2
+LANES = 128
+LINK_COUNT = 320
+VMEM_BYTES = 60 << 20
+LOAD_ORDER = (
+    "value_embed",
+    "enc_qkv",
+    "dec_qkv",
+    "enc_out",
+    "enc_ff_in",
+    "enc_ff_out",
+    "dec_out",
+    "cross_qkv",
+    "cross_out",
+    "dec_ff_in",
+    "dec_ff_out",
+)
+
+
+def mm(left, right):
+    return jnp.dot(left, right, preferred_element_type=F32)
+
+
+def mm_right_t(left, right):
+    return lax.dot_general(left, right, (((1,), (1,)), ((), ())), preferred_element_type=F32)
+
+
+def mm_left_t(left, right):
+    return lax.dot_general(left, right, (((0,), (0,)), ((), ())), preferred_element_type=F32)
+
+
+def lane_index(shape):
+    return lax.broadcasted_iota(jnp.int32, shape, len(shape) - 1)
+
+
+def swap_halves(values):
+    return pltpu.roll(values, LANES // 2, axis=1)
+
+
+def low_lanes(first, second):
+    return jnp.where(lane_index(first.shape) < LANES // 2, first, second)
+
+
+def pack_rows(values):
+    half = values.shape[0] // 2
+    packed = []
+    for pair in range(values.shape[1] // LANES):
+        group = values[:, pair * LANES : (pair + 1) * LANES]
+        top, bottom = group[:half], group[half:]
+        packed.append(low_lanes(top, swap_halves(bottom)))
+        packed.append(low_lanes(swap_halves(top), bottom))
+    return packed
+
+
+def unpack_rows(packed):
+    groups = []
+    for pair in range(len(packed) // 2):
+        first, second = packed[2 * pair], packed[2 * pair + 1]
+        top = low_lanes(first, swap_halves(second))
+        bottom = low_lanes(swap_halves(first), second)
+        groups.append(jnp.concatenate([top, bottom], axis=0))
+    return jnp.concatenate(groups, axis=1)
+
+
+def pack_pairs(keys, values):
+    packed = []
+    for pair in range(keys.shape[1] // LANES):
+        key_group = keys[:, pair * LANES : (pair + 1) * LANES]
+        value_group = values[:, pair * LANES : (pair + 1) * LANES]
+        packed.append(low_lanes(key_group, swap_halves(value_group)))
+        packed.append(low_lanes(swap_halves(key_group), value_group))
+    return packed
+
+
+def unpack_pairs(packed):
+    keys, values = [], []
+    for pair in range(len(packed) // 2):
+        first, second = packed[2 * pair], packed[2 * pair + 1]
+        keys.append(low_lanes(first, swap_halves(second)))
+        values.append(low_lanes(swap_halves(first), second))
+    return jnp.concatenate(keys, axis=1), jnp.concatenate(values, axis=1)
+
+
+def norm_forward(values, gain, shift):
+    centred = values - jnp.mean(values, axis=-1, keepdims=True)
+    scale = lax.rsqrt(jnp.mean(centred * centred, axis=-1, keepdims=True) + epsilon)
+    unit = centred * scale
+    return unit * gain + shift, unit, scale
+
+
+def norm_back(upstream, unit, scale, gain):
+    inner = upstream * gain
+    result = scale * (
+        inner
+        - jnp.mean(inner, axis=-1, keepdims=True)
+        - unit * jnp.mean(inner * unit, axis=-1, keepdims=True)
+    )
+    return (
+        result,
+        jnp.sum(upstream * unit, axis=0, keepdims=True),
+        jnp.sum(upstream, axis=0, keepdims=True),
+    )
+
+
+def rounded(values):
+    return values.astype(BF16).astype(F32)
+
+
+class View:
+    def __init__(self, entries):
+        for name, entry in entries.items():
+            if isinstance(entry, dict):
+                entry = View(entry)
+            elif isinstance(entry, (list, tuple)):
+                entry = [View(part) if isinstance(part, dict) else part for part in entry]
+            setattr(self, name, entry)
+
+
+class Weight:
+    def __init__(self, copy, held):
+        self.copy, self.held, self.here = copy, held, False
+        copy.start()
+
+    def __call__(self):
+        if not self.here:
+            self.copy.wait()
+            self.here = True
+        return self.held
+
+
+def fused_body(structures, *refs):
+    entries = {}
+    for structure in structures:
+        count = structure.num_leaves
+        entries.update(jax.tree.unflatten(structure, refs[:count]))
+        refs = refs[count:]
+    ref = View(entries)
+    rows, width = ref.enc_in.shape
+    hidden, channels, chips = ref.ff_bias.shape[1], ref.series.shape[1], HEADS
+    packed_rows = rows // 2
+    keys_total = chips * CORES * rows
+    block_queries = chips * packed_rows
+    column = width // (chips * CORES)
+    depth = chips * CORES // QUAD
+
+    place = lax.axis_index(SEQ)
+    item = lax.axis_index(BATCH)
+    core = lax.rem(place, 2)
+    chip = place // 2
+    x_place = lax.rem(chip, 2)
+    z_place = chip // 2
+    quad = lax.rem(place, QUAD)
+    core_dev = (chip * 2 + (1 - core), item)
+    x_dev = (z_place * QUAD + (1 - x_place) * 2 + core, item)
+    diagonal_dev = (z_place * QUAD + (1 - x_place) * 2 + (1 - core), item)
+    item_dev = (place, 1 - item)
+    x_quad = (1 - x_place) * 2 + core
+
+    def same_core(step):
+        peer = lax.rem(chip + step, chips)
+        return peer, (peer * 2 + core, item)
+
+    def z_peer(step):
+        peer = lax.rem(z_place + step, depth)
+        return peer, (peer * QUAD + quad, item)
+
+    barrier = pltpu.get_barrier_semaphore()
+    greeted = [core_dev, diagonal_dev, item_dev] + [same_core(step)[1] for step in range(1, chips)]
+    for device in greeted:
+        pl.semaphore_signal(barrier, inc=1, device_id=device, device_id_type=MESH)
+
+    loaded = {}
+    for index, name in enumerate(LOAD_ORDER):
+        source, target = getattr(ref.weight, name), getattr(ref.held, name)
+        copy = pltpu.make_async_copy(source, target, ref.load_sem.at[index])
+        loaded[name] = Weight(copy, target)
+    weight = View(loaded)
+
+    sends = []
+
+    def send(source, target, device):
+        index = len(sends)
+        copy = pltpu.make_async_remote_copy(
+            src_ref=source,
+            dst_ref=target,
+            send_sem=ref.send_sem.at[index],
+            recv_sem=ref.recv_sem.at[index],
+            device_id=device,
+            device_id_type=MESH,
+        )
+        copy.start()
+        sends.append(copy)
+        return copy
+
+    def arrive(copies):
+        for copy in copies:
+            copy.wait_recv()
+
+    def spread(source, target_at):
+        copies = []
+        for step in range(1, chips):
+            peer, device = same_core(step)
+            copies.append(send(source.at[peer], target_at(chip), device))
+        return copies
+
+    def share(block):
+        return [
+            block,
+            send(block.at[quad], block.at[quad], core_dev),
+            send(block.at[quad], block.at[quad], x_dev),
+        ]
+
+    def relay(shared):
+        block = shared[0]
+        shared[2].wait_recv()
+        shared.append(send(block.at[x_quad], block.at[x_quad], core_dev))
+
+    def settle(shared):
+        shared[1].wait_recv()
+        shared[3].wait_recv()
+
+    def gathered(block):
+        value = block[...]
+        return value.reshape(value.shape[0] * value.shape[1], value.shape[2])
+
+    def cut_columns(values, group, start):
+        part = lane_index((rows, LANES)) // column
+        for member in range(QUAD):
+            total = None
+            for level in range(depth):
+                cut = values[:, level * LANES : (level + 1) * LANES]
+                shift = (column * (level - member)) % LANES
+                moved = pltpu.roll(cut, shift, axis=1) if shift else cut
+                total = moved if total is None else jnp.where(part == level, moved, total)
+            group.cut[member, :, start : start + LANES] = total.astype(BF16)
+
+    def share_columns(group, start, stop):
+        source, target = group.cut, group.met
+        target[quad, :, start:stop] = source[quad, :, start:stop]
+        copies = []
+        for device, member in (
+            (core_dev, x_place * 2 + 1 - core),
+            (x_dev, x_quad),
+            (diagonal_dev, (1 - x_place) * 2 + 1 - core),
+        ):
+            copies.append(
+                send(
+                    source.at[member, :, pl.ds(start, stop - start)],
+                    target.at[quad, :, pl.ds(start, stop - start)],
+                    device,
+                )
+            )
+        return copies
+
+    def columns_of(group, start, stop):
+        value = group.met[:, :, start:stop]
+        return value.reshape(QUAD * rows, stop - start)
+
+    def put_rows(target, level, start, values):
+        half = target.shape[2]
+        count = values.shape[0]
+        done = 0
+        while done < count:
+            which, offset = divmod(start + done, half)
+            take = min(count - done, half - offset)
+            target[which, level, offset : offset + take, :] = values[done : done + take, :]
+            done += take
+
+    def put_gradient(target, start, gradient):
+        count = gradient.shape[0] // depth
+        gradient = gradient.astype(BF16)
+        short = -gradient.shape[1] % width
+        pieces = gradient.shape[1] // width
+        for level in range(depth):
+            block = gradient[level * count : (level + 1) * count]
+            for piece in range(pieces):
+                put_rows(
+                    target,
+                    level,
+                    start + piece * count,
+                    block[:, piece * width : (piece + 1) * width],
+                )
+            if short:
+                tail = jnp.concatenate(
+                    [block[:, pieces * width :], jnp.zeros((count, short), BF16)], axis=1
+                )
+                put_rows(target, level, start + pieces * count, tail)
+
+    def reduce_item(group):
+        part, arrived = group.part, group.item
+        return [send(part.at[1 - item], arrived, item_dev)]
+
+    def reduce_depth(group):
+        part, arrived = group.part, group.item
+        total, landing = group.half, group.depth
+        total[...] = (part[item].astype(F32) + arrived[...].astype(F32)).astype(BF16)
+        copies = []
+        for step in range(1, depth):
+            peer, device = z_peer(step)
+            copies.append(send(total.at[peer], landing.at[step - 1], device))
+        return copies
+
+    def reduce_last(group):
+        total, landing = group.half, group.depth
+        result = group.sum
+        value = total[z_place].astype(F32)
+        for step in range(1, depth):
+            value = value + landing[step - 1].astype(F32)
+        result[item] = value.astype(BF16)
+        return [send(result.at[item], result.at[item], item_dev)]
+
+    def set_vector(row, value):
+        ref.vec[row : row + 1, :] = value
+
+    att_enc, att_self, att_cross = ref.attention
+    one, two, three = ref.group
+    for group, result in zip(ref.group, ref.sums):
+        group.sum = result
+    enc_ff = (weight.enc_ff_in, weight.enc_ff_out)
+    dec_ff = (weight.dec_ff_in, weight.dec_ff_out)
+
+    tau = ref.tau_scale[0]
+    group_row = lax.broadcasted_iota(jnp.int32, ref.channel_mask.shape, 0)
+    chosen = jnp.where(
+        group_row == ref.item_group[0], ref.channel_mask[...].astype(F32), 0.0
+    )
+    channel_row = jnp.sum(chosen, axis=0, keepdims=True)
+    masked = (ref.series[...].astype(F32) * channel_row).astype(BF16)
+    ref.x_series[quad] = jnp.zeros(ref.x_series.shape[1:], BF16)
+    ref.x_series[quad, :, 0:channels] = masked
+
+    shift_row = ref.delta_shift[...].astype(F32)
+    ref.t_shift[...] = jnp.broadcast_to(
+        jnp.concatenate([shift_row, shift_row], axis=1), ref.t_shift.shape
+    )
+
+    embedded = ref.enc_in[...].astype(F32) + mm(masked, weight.value_embed()[...])
+    ref.embedded[...] = embedded
+    enc_hidden = embedded.astype(BF16)
+    ref.x_enc_hidden[quad] = enc_hidden
+
+    def send_queries(own, query):
+        for head, packed in enumerate(pack_rows(query)):
+            own.t_query[head] = packed.astype(BF16)
+        own.query[chip] = own.t_query[chip]
+        return spread(own.t_query, lambda at: own.query.at[at])
+
+    def send_pairs(own, keys, values):
+        for head, packed in enumerate(pack_pairs(keys, values)):
+            own.t_pair[head] = packed.astype(BF16)
+        own.pair[chip, core] = own.t_pair[chip]
+        return spread(own.t_pair, lambda at: own.pair.at[at, core])
+
+    def pass_on(own):
+        block = own.pair
+        return [send(block.at[:, core], block.at[:, core], core_dev)]
+
+    qkv = weight.enc_qkv()
+    enc_query = mm(enc_hidden, qkv[0]) + ref.enc_query_bias[...]
+    enc_key = mm(enc_hidden, qkv[1])
+    enc_value = mm(enc_hidden, qkv[2]) + ref.enc_bias[0:1, :]
+    pl.semaphore_wait(barrier, len(greeted))
+    go_enc_pair = send_pairs(att_enc, enc_key, enc_value)
+    go_enc_query = send_queries(att_enc, enc_query)
+    ref.shift[chip, core] = ref.t_shift[...]
+    go_shift = []
+    for step in range(1, chips):
+        go_shift.append(
+            send(ref.t_shift, ref.shift.at[chip, core], same_core(step)[1])
+        )
+
+    dec_hidden = ref.dec_in[...]
+    ref.x_dec_in[quad] = dec_hidden
+    qkv = weight.dec_qkv()
+    self_query = mm(dec_hidden, qkv[0]) + ref.dec_bias[0:1, :]
+    self_key = mm(dec_hidden, qkv[1])
+    self_value = mm(dec_hidden, qkv[2]) + ref.dec_bias[1:2, :]
+    go_self_pair = send_pairs(att_self, self_key, self_value)
+    go_self_query = send_queries(att_self, self_query)
+
+    def attention(own, shifted, causal):
+        pairs = own.pair[...].reshape(keys_total, LANES)
+        pairs_t = pairs.T
+        own.pair_t[...] = pairs_t
+        query_t = own.query[...].reshape(block_queries, LANES).astype(F32).T
+        zeros = jnp.zeros((LANES // 2, block_queries), F32)
+        for half in range(HALVES):
+            part = query_t[half * LANES // 2 : (half + 1) * LANES // 2]
+            side = jnp.concatenate([part, zeros], axis=0).astype(BF16)
+            scores = mm(pairs, side) * (tau * 0.125)
+            if shifted:
+                moved = ref.shift_columns[...]
+                scores = scores + jnp.concatenate([moved] * (block_queries // LANES), axis=1)
+            if causal:
+                key_at = lax.broadcasted_iota(jnp.int32, scores.shape, 0)
+                lane = lane_index(scores.shape)
+                query_at = (
+                    (lane // packed_rows * 2 + core) * rows
+                    + half * packed_rows
+                    + lane % packed_rows
+                )
+                scores = jnp.where(key_at > query_at, masked_score, scores)
+            weights = jnp.exp(scores - jnp.max(scores, axis=0, keepdims=True))
+            inverse = 1.0 / jnp.sum(weights, axis=0, keepdims=True)
+            low_weights = weights.astype(BF16)
+            own.weights[half] = low_weights
+            own.inverse[half] = jnp.broadcast_to(inverse, (8, block_queries))
+            mixed_t = mm(pairs_t, low_weights)[LANES // 2 :] * inverse
+            own.mixed_t[half * LANES // 2 : (half + 1) * LANES // 2, :] = mixed_t
+        mixed = own.mixed_t[...].T.astype(BF16)
+        own.t_mixed[...] = mixed.reshape(chips, packed_rows, LANES)
+        own.mixed[chip] = own.t_mixed[chip]
+        return spread(own.t_mixed, lambda at: own.mixed.at[at])
+
+    def mixed_rows(own):
+        return unpack_rows(
+            [own.mixed[head].astype(F32) for head in range(chips)]
+        ).astype(BF16)
+
+    arrive(go_enc_pair)
+    on_enc = pass_on(att_enc)
+    arrive(go_shift)
+    on_shift = [send(ref.shift.at[:, core], ref.shift.at[:, core], core_dev)]
+    arrive(go_enc_query)
+    arrive(go_self_pair)
+    on_self = pass_on(att_self)
+    arrive(on_shift)
+    for block in range(chips):
+        line = low_lanes(ref.shift[block, 0], ref.shift[block, 1])[0:1, :] * 0.125
+        ref.shift_columns[block * LANES : (block + 1) * LANES, :] = jnp.broadcast_to(
+            line, (LANES, LANES)
+        ).T
+    arrive(on_enc)
+    back_enc = attention(att_enc, True, False)
+    arrive(on_self)
+    arrive(go_self_query)
+    back_self = attention(att_self, False, True)
+    shares = [share(ref.x_series), share(ref.x_enc_hidden), share(ref.x_dec_in)]
+
+    def feed_forward(values, weights, bias_row, out_bias, side):
+        low = values.astype(BF16)
+        side.hidden[quad] = low
+        weight_in, weight_out = weights[0](), weights[1]()
+        total = out_bias
+        for piece in range(hidden // width):
+            cut = slice(piece * width, (piece + 1) * width)
+            pre = mm(low, weight_in[:, cut]) + ref.ff_bias[bias_row : bias_row + 1, cut]
+            normal = 0.5 * (1.0 + lax.erf(pre * 0.7071067811865476))
+            act = (pre * normal).astype(BF16)
+            side.slope[:, cut] = normal + pre * (
+                jnp.exp(pre * pre * -0.5) * 0.3989422804014327
+            )
+            side.act[quad, :, cut] = act
+            total = total + mm(act, weight_out[cut, :])
+        return total
+
+    def feed_forward_back(upstream, weights, side, vector_row, group):
+        low = upstream.astype(BF16)
+        weight_in, weight_out = weights[0](), weights[1]()
+        total = None
+        for piece in range(hidden // width):
+            cut = slice(piece * width, (piece + 1) * width)
+            act_grad = mm_right_t(low, weight_out[cut, :])
+            pre_grad = (act_grad * side.slope[:, cut]).astype(BF16)
+            set_vector(
+                vector_row + piece, jnp.sum(pre_grad.astype(F32), axis=0, keepdims=True)
+            )
+            for member in range(QUAD):
+                at = piece * LANES
+                group.cut[member, :, at : at + LANES] = pre_grad[
+                    :, member * LANES : (member + 1) * LANES
+                ]
+            more = mm_right_t(pre_grad, weight_in[:, cut])
+            total = more if total is None else total + more
+        return total
+
+    def save_norm(index, unit, scale):
+        ref.unit[index] = unit
+        ref.scale[index] = jnp.broadcast_to(scale, (rows, LANES))
+
+    def saved_norm(index):
+        return ref.unit[index], ref.scale[index, :, 0:1]
+
+    arrive(back_enc)
+    attended = mixed_rows(att_enc)
+    ref.x_enc_mixed[quad] = attended
+    first, unit, scale = norm_forward(
+        embedded + mm(attended, weight.enc_out()[...]) + ref.enc_bias[1:2, :],
+        ref.enc_gain[0:1, :],
+        ref.enc_bias[3:4, :],
+    )
+    save_norm(0, unit, scale)
+    second, unit, scale = norm_forward(
+        first + feed_forward(first, enc_ff, 0, ref.enc_bias[2:3, :], ref.enc_ff),
+        ref.enc_gain[1:2, :],
+        ref.enc_bias[4:5, :],
+    )
+    save_norm(1, unit, scale)
+    memory = second.astype(BF16)
+    ref.x_memory[quad] = memory
+    qkv = weight.cross_qkv()
+    cross_key = mm(memory, qkv[1])
+    cross_value = mm(memory, qkv[2]) + ref.dec_bias[4:5, :]
+    go_cross_pair = send_pairs(att_cross, cross_key, cross_value)
+
+    arrive(back_self)
+    attended = mixed_rows(att_self)
+    ref.x_self_mixed[quad] = attended
+    first, unit, scale = norm_forward(
+        ref.dec_in[...].astype(F32)
+        + mm(attended, weight.dec_out()[...])
+        + ref.dec_bias[2:3, :],
+        ref.dec_gain[0:1, :],
+        ref.dec_bias[7:8, :],
+    )
+    save_norm(2, unit, scale)
+    ref.first_dec[...] = first
+    low = first.astype(BF16)
+    ref.x_cross_hidden[quad] = low
+    go_cross_query = send_queries(att_cross, mm(low, qkv[0]) + ref.dec_bias[3:4, :])
+    for shared in shares:
+        relay(shared)
+    shares_two = [
+        share(block)
+        for block in (
+            ref.x_enc_mixed,
+            ref.enc_ff.hidden,
+            ref.x_memory,
+            ref.x_self_mixed,
+            ref.x_cross_hidden,
+        )
+    ]
+
+    arrive(go_cross_pair)
+    on_cross = pass_on(att_cross)
+    arrive(go_cross_query)
+    arrive(on_cross)
+    back_cross = attention(att_cross, True, False)
+    for shared in shares_two:
+        relay(shared)
+    shares_three = [share(ref.enc_ff.act)]
+    arrive(back_cross)
+    attended = mixed_rows(att_cross)
+    ref.x_cross_mixed[quad] = attended
+    second, unit, scale = norm_forward(
+        ref.first_dec[...]
+        + mm(attended, weight.cross_out()[...])
+        + ref.dec_bias[5:6, :],
+        ref.dec_gain[1:2, :],
+        ref.dec_bias[8:9, :],
+    )
+    save_norm(3, unit, scale)
+
+    third, unit, scale = norm_forward(
+        second + feed_forward(second, dec_ff, 1, ref.dec_bias[6:7, :], ref.dec_ff),
+        ref.dec_gain[2:3, :],
+        ref.dec_bias[9:10, :],
+    )
+    ref.dec_result[...] = third.astype(BF16)
+
+    def norm_step(index, upstream, gain, gain_row, gain_vector, shift_vector):
+        unit, scale = saved_norm(index)
+        result, gain_grad, shift_grad = norm_back(
+            upstream, unit, scale, gain[gain_row : gain_row + 1, :]
+        )
+        set_vector(gain_vector, gain_grad)
+        set_vector(shift_vector, shift_grad)
+        return result
+
+    def column_sum(values):
+        return jnp.sum(rounded(values), axis=0, keepdims=True)
+
+    third_grad, gain_grad, shift_grad = norm_back(
+        ref.cotangent[...].astype(F32), unit, scale, ref.dec_gain[2:3, :]
+    )
+    set_vector(20, gain_grad)
+    set_vector(17, shift_grad)
+    from_ff = feed_forward_back(third_grad, dec_ff, ref.dec_ff, 25, one)
+    second_grad = norm_step(3, third_grad + from_ff, ref.dec_gain, 1, 19, 16)
+    ref.second_grad[...] = second_grad
+
+    def send_mixed_grad(own, branch_grad, out_weight):
+        mixed_grad = mm_right_t(branch_grad.astype(BF16), out_weight[...])
+        for head, packed in enumerate(pack_rows(mixed_grad)):
+            own.t_grad[head] = packed.astype(BF16)
+        own.grad[chip] = own.t_grad[chip]
+        return spread(own.t_grad, lambda at: own.grad.at[at])
+
+    go_cross_grad = send_mixed_grad(att_cross, second_grad, weight.cross_out())
+    cut_columns(third_grad, one, hidden // QUAD)
+    cut_columns(second_grad, one, hidden // QUAD + LANES)
+    set_vector(14, column_sum(third_grad))
+    set_vector(13, column_sum(second_grad))
+    columns_one = share_columns(one, 0, hidden // QUAD + 2 * LANES)
+    for shared in shares_three:
+        relay(shared)
+    shares_four = [share(block) for block in (ref.x_cross_mixed, ref.dec_ff.hidden, ref.dec_ff.act)]
+
+    def attention_back(own):
+        pairs = own.pair[...].reshape(keys_total, LANES)
+        pairs_t = own.pair_t[...]
+        queries = own.query[...].reshape(block_queries, LANES).astype(F32)
+        grads = own.grad[...].reshape(block_queries, LANES).astype(F32)
+        grads_t = grads.T
+        zeros = jnp.zeros((LANES // 2, block_queries), F32)
+        blank = jnp.zeros_like(queries)
+        query_grads = []
+        key_total = value_total = None
+        for half in range(HALVES):
+            cut = slice(half * LANES // 2, (half + 1) * LANES // 2)
+            grad_t = grads_t[cut]
+            row_dot = jnp.sum(grad_t * own.mixed_t[cut, :], axis=0, keepdims=True)
+            side = jnp.concatenate([zeros, grad_t], axis=0).astype(BF16)
+            prob_grads = mm(pairs, side)
+            probabilities = own.weights[half].astype(F32) * own.inverse[half, 0:1, :]
+            score_grads = (probabilities * (prob_grads - row_dot)).astype(BF16)
+            query_grads.append(mm(pairs_t, score_grads)[: LANES // 2])
+            if half == 0:
+                query_side = low_lanes(queries, blank)
+                grad_side = low_lanes(blank, swap_halves(grads))
+            else:
+                query_side = low_lanes(swap_halves(queries), blank)
+                grad_side = low_lanes(blank, grads)
+            key_part = mm(score_grads, query_side.astype(BF16))
+            value_part = mm(probabilities.astype(BF16), grad_side.astype(BF16))
+            key_total = key_part if key_total is None else key_total + key_part
+            value_total = value_part if value_total is None else value_total + value_part
+        factor = tau * 0.125
+        query_grad = (jnp.concatenate(query_grads, axis=0) * factor).T.astype(BF16)
+        own.t_query_grad[...] = query_grad.reshape(chips, packed_rows, LANES)
+        own.query_grad[chip] = own.t_query_grad[chip]
+        go_query = spread(
+            own.t_query_grad, lambda at: own.query_grad.at[at]
+        )
+        pair_grad = (key_total * factor + value_total).reshape(chips, CORES, rows, LANES)
+        for which in range(CORES):
+            ref.pair_sum[which] = pair_grad[:, which]
+            own.t_part[which] = pair_grad[:, which].astype(BF16)
+        exchange = send(own.t_part.at[1 - core], own.part, core_dev)
+        return go_query, exchange
+
+    def attention_back_pairs(own, exchange):
+        exchange.wait_recv()
+        total = ref.pair_sum[core] + own.part[...].astype(F32)
+        own.t_pair_grad[...] = total.astype(BF16)
+        own.pair_grad[chip] = own.t_pair_grad[chip]
+        return spread(own.t_pair_grad, lambda at: own.pair_grad.at[at])
+
+    def query_grad_rows(own):
+        return unpack_rows(
+            [own.query_grad[head].astype(F32) for head in range(chips)]
+        )
+
+    def pair_grad_rows(own):
+        return unpack_pairs([own.pair_grad[head].astype(F32) for head in range(chips)])
+
+    arrive(go_cross_grad)
+    go_query, exchange = attention_back(att_cross)
+    for shared in shares_four:
+        relay(shared)
+    go_pair = attention_back_pairs(att_cross, exchange)
+
+    ff_width = hidden // QUAD
+    for shared in shares_four:
+        settle(shared)
+    arrive(columns_one)
+    put_gradient(
+        one.part, 0, mm_left_t(columns_of(one, 0, ff_width), gathered(ref.dec_ff.hidden))
+    )
+    put_gradient(
+        one.part,
+        LANES,
+        mm_left_t(columns_of(one, ff_width, ff_width + LANES), gathered(ref.dec_ff.act)),
+    )
+    put_gradient(
+        one.part,
+        2 * LANES,
+        mm_left_t(
+            columns_of(one, ff_width + LANES, ff_width + 2 * LANES), gathered(ref.x_cross_mixed)
+        ),
+    )
+    item_one = reduce_item(one)
+
+    qkv = weight.cross_qkv()
+    arrive(go_query)
+    cross_query_grad = query_grad_rows(att_cross)
+    first_grad = norm_step(
+        2,
+        ref.second_grad[...] + mm_right_t(cross_query_grad.astype(BF16), qkv[0]),
+        ref.dec_gain,
+        0,
+        18,
+        15,
+    )
+    ref.first_grad[...] = first_grad
+    go_self_grad = send_mixed_grad(att_self, first_grad, weight.dec_out())
+    set_vector(10, column_sum(first_grad))
+
+    arrive(go_pair)
+    cross_key_grad, cross_value_grad = pair_grad_rows(att_cross)
+    memory_grad = mm_right_t(cross_key_grad.astype(BF16), qkv[1]) + mm_right_t(
+        cross_value_grad.astype(BF16), qkv[2]
+    )
+    enc_second_grad = norm_step(1, memory_grad, ref.enc_gain, 1, 7, 5)
+    from_ff = feed_forward_back(enc_second_grad, enc_ff, ref.enc_ff, 21, two)
+    enc_first_grad = norm_step(0, enc_second_grad + from_ff, ref.enc_gain, 0, 6, 4)
+    ref.enc_first_grad[...] = enc_first_grad
+    go_enc_grad = send_mixed_grad(att_enc, enc_first_grad, weight.enc_out())
+    set_vector(3, column_sum(enc_second_grad))
+    set_vector(2, column_sum(enc_first_grad))
+    set_vector(11, column_sum(cross_query_grad))
+    set_vector(12, column_sum(cross_value_grad))
+    for row in (0, 1, 8, 9, 29, 30, 31):
+        set_vector(row, jnp.zeros((1, width), F32))
+    vec_item = send(ref.vec, ref.vec_item, item_dev)
+    for index, values in enumerate(
+        (enc_second_grad, enc_first_grad, first_grad)
+        + (cross_query_grad, cross_key_grad, cross_value_grad)
+    ):
+        cut_columns(values, two, ff_width + index * LANES)
+    columns_two = share_columns(two, 0, ff_width + 6 * LANES)
+
+    arrive(go_self_grad)
+    go_self_query_grad, exchange = attention_back(att_self)
+    arrive(item_one)
+    depth_one = reduce_depth(one)
+    go_self_pair_grad = attention_back_pairs(att_self, exchange)
+    vec_item.wait_recv()
+    ref.vec_a[...] = ref.vec[...] + ref.vec_item[...]
+    vec_core = send(ref.vec_a, ref.vec_core, core_dev)
+    arrive(go_enc_grad)
+    go_enc_query_grad, exchange = attention_back(att_enc)
+    vec_core.wait_recv()
+    ref.vec_b[...] = ref.vec_a[...] + ref.vec_core[...]
+    vec_x = send(ref.vec_b, ref.vec_x, x_dev)
+    go_enc_pair_grad = attention_back_pairs(att_enc, exchange)
+
+    for shared in shares + shares_two + shares_three:
+        settle(shared)
+    arrive(columns_two)
+    put_gradient(
+        two.part, 0, mm_left_t(columns_of(two, 0, ff_width), gathered(ref.enc_ff.hidden))
+    )
+    put_gradient(
+        two.part,
+        LANES,
+        mm_left_t(columns_of(two, ff_width, ff_width + LANES), gathered(ref.enc_ff.act)),
+    )
+    for index, (block, count) in enumerate(
+        ((ref.x_enc_mixed, 1), (ref.x_self_mixed, 1), (ref.x_cross_hidden, 1), (ref.x_memory, 2))
+    ):
+        start = ff_width + (index + 1) * LANES
+        gradient = mm_left_t(columns_of(two, start, start + count * LANES), gathered(block))
+        for which in range(count):
+            put_gradient(
+                two.part,
+                2 * LANES + (index + which) * column,
+                gradient[which * LANES : (which + 1) * LANES],
+            )
+    item_two = reduce_item(two)
+    vec_x.wait_recv()
+    ref.vec_c[...] = ref.vec_b[...] + ref.vec_x[...]
+    vec_depth = [
+        send(ref.vec_c, ref.vec_depth.at[step - 1], z_peer(step)[1])
+        for step in range(1, depth)
+    ]
+    arrive(depth_one)
+    last_one = reduce_last(one)
+
+    def input_grad(own, weights, first):
+        query_grad = query_grad_rows(own)
+        key_grad, value_grad = pair_grad_rows(own)
+        total = (
+            first[...]
+            + mm_right_t(query_grad.astype(BF16), weights[0])
+            + mm_right_t(key_grad.astype(BF16), weights[1])
+            + mm_right_t(value_grad.astype(BF16), weights[2])
+        )
+        return total, query_grad, key_grad, value_grad
+
+    arrive(go_self_query_grad)
+    arrive(go_self_pair_grad)
+    total, query_grad, key_grad, value_grad = input_grad(att_self, weight.dec_qkv(), ref.first_grad)
+    ref.dec_grad[...] = total
+    for index, values in enumerate((query_grad, key_grad, value_grad)):
+        cut_columns(values, three, index * LANES)
+    columns_self = share_columns(three, 0, 3 * LANES)
+    arrive(item_two)
+    depth_two = reduce_depth(two)
+    arrive(go_enc_query_grad)
+    arrive(go_enc_pair_grad)
+    total, query_grad, key_grad, value_grad = input_grad(att_enc, weight.enc_qkv(), ref.enc_first_grad)
+    ref.enc_grad[...] = total
+    for index, values in enumerate((query_grad, key_grad, value_grad, total)):
+        cut_columns(values, three, (3 + index) * LANES)
+    columns_enc = share_columns(three, 3 * LANES, 7 * LANES)
+    arrive(columns_self)
+
+    def gradient_three(start, count, block, row):
+        gradient = mm_left_t(
+            columns_of(three, start * LANES, (start + count) * LANES), gathered(block)
+        )
+        for which in range(count):
+            put_gradient(
+                three.part, row + which * column, gradient[which * LANES : (which + 1) * LANES]
+            )
+
+    gradient_three(0, 3, ref.x_dec_in, 0)
+    arrive(columns_enc)
+    gradient_three(3, 3, ref.x_enc_hidden, 3 * column)
+    gradient_three(6, 1, ref.x_series, 6 * column)
+    totals = [
+        jnp.sum(
+            columns_of(three, index * LANES, (index + 1) * LANES).astype(F32),
+            axis=0,
+            keepdims=True,
+        )
+        for index in (0, 2, 3, 5)
+    ]
+    totals = jnp.concatenate(totals + [jnp.zeros((column - 4, LANES), F32)], axis=0)
+    totals = jnp.concatenate([totals, jnp.zeros((column, width - LANES), F32)], axis=1)
+    for level in range(depth):
+        put_rows(three.part, level, 8 * column, totals.astype(BF16))
+    item_three = reduce_item(three)
+    arrive(vec_depth)
+    total = ref.vec_c[...]
+    for step in range(1, depth):
+        total = total + ref.vec_depth[step - 1]
+    ref.vectors[...] = total
+    arrive(depth_two)
+    last_two = reduce_last(two)
+    arrive(item_three)
+    depth_three = reduce_depth(three)
+    arrive(last_one)
+    arrive(last_two)
+    arrive(depth_three)
+    last_three = reduce_last(three)
+    arrive(last_three)
+    for copy in sends:
+        copy.wait_send()
+
+
+def finish_body(*refs):
+    (
+        dec_in,
+        enc_grad_in,
+        dec_grad_in,
+        one,
+        two,
+        three,
+        vectors,
+        dec_out,
+        enc_grad,
+        dec_grad,
+        g_embed,
+        g_enc_qkv,
+        g_enc_out,
+        g_enc_ff_in,
+        g_enc_ff_out,
+        g_enc_query_bias,
+        g_enc_bias,
+        g_enc_gain,
+        g_dec_qkv,
+        g_dec_out,
+        g_cross_qkv,
+        g_cross_out,
+        g_dec_ff_in,
+        g_dec_ff_out,
+        g_dec_bias,
+        g_dec_gain,
+        g_ff_bias,
+    ) = refs
+    place = lax.axis_index(SEQ)
+    column, width = g_enc_out.shape
+    channels = g_embed.shape[1]
+    level, member = place // QUAD, lax.rem(place, QUAD)
+    dec_out[...] = dec_in[...]
+    enc_grad[...] = enc_grad_in[...]
+    dec_grad[...] = dec_grad_in[...]
+
+    def whole(block):
+        value = block[...]
+        return value.reshape(value.shape[0] * value.shape[1], value.shape[2]).astype(F32)
+
+    def narrow(target, block, start):
+        for piece in range(target.shape[1] // width):
+            target[:, piece * width : (piece + 1) * width] = block[
+                start + piece * column : start + (piece + 1) * column
+            ]
+
+    first = whole(one)
+    g_dec_ff_in[...] = first[0:LANES].T
+    narrow(g_dec_ff_out, first, LANES)
+    narrow(g_cross_out, first, 2 * LANES)
+    second = whole(two)
+    g_enc_ff_in[...] = second[0:LANES].T
+    narrow(g_enc_ff_out, second, LANES)
+    narrow(g_enc_out, second, 2 * LANES)
+    narrow(g_dec_out, second, 2 * LANES + column)
+    for index in range(3):
+        start = 2 * LANES + (2 + index) * column
+        g_cross_qkv[index] = second[start : start + column]
+    third = whole(three)
+    for index in range(3):
+        g_dec_qkv[index] = third[index * column : (index + 1) * column]
+        g_enc_qkv[index] = third[(3 + index) * column : (4 + index) * column]
+    g_embed[:, 0:width] = third[6 * column : 7 * column]
+    g_embed[:, width:channels] = third[7 * column : 8 * column, 0 : channels - width]
+
+    group = vectors[:, pl.ds(pl.multiple_of(level * LANES, LANES), LANES)]
+    moved = pltpu.roll(group, lax.rem(LANES - member * column, LANES), axis=1)
+    rows = moved[:, 0:column]
+    late = third[2 * LANES : 2 * LANES + 8, 0:LANES]
+    late = pltpu.roll(late, lax.rem(LANES - level * column, LANES), axis=1)[:, 0:column]
+    g_enc_query_bias[...] = late[2:3]
+    g_enc_bias[...] = jnp.concatenate([late[3:4], rows[2:6]], axis=0)
+    g_enc_gain[...] = rows[6:8]
+    g_dec_bias[...] = jnp.concatenate([late[0:2], rows[10:18]], axis=0)
+    g_dec_gain[...] = rows[18:21]
+    lanes = pl.ds(pl.multiple_of(member * LANES, LANES), LANES)
+    hidden_rows = vectors[:, lanes]
+    row_index = lax.broadcasted_iota(jnp.int32, hidden_rows.shape, 0)
+    for index in range(2):
+        chosen = jnp.where(row_index == 21 + 4 * index + level, hidden_rows, 0.0)
+        g_ff_bias[index : index + 1, :] = jnp.sum(chosen, axis=0, keepdims=True)
+
+
+def fused_local(
+    enc_in,
+    series,
+    channel_mask,
+    item_group,
+    tau_scale,
+    delta_shift,
+    dec_in,
+    value_embed,
+    enc_qkv,
+    enc_out,
+    enc_ff_in,
+    enc_ff_out,
+    enc_query_bias,
+    enc_bias,
+    enc_gain,
+    dec_qkv,
+    dec_out,
+    cross_qkv,
+    cross_out,
+    dec_ff_in,
+    dec_ff_out,
+    dec_bias,
+    dec_gain,
+    ff_bias,
+    cotangent,
+):
+    rows, width = enc_in.shape[1:]
+    hidden = enc_ff_in.shape[1]
+    channels = value_embed.shape[0]
+    chips = HEADS
+    column = width // (chips * CORES)
+    depth = chips * CORES // QUAD
+    padded = -(-channels // LANES) * LANES
+    keys_total = chips * CORES * rows
+    queries = chips * rows // 2
+    in_smem = pl.BlockSpec(memory_space=pltpu.SMEM)
+    in_vmem = pl.BlockSpec(memory_space=pltpu.VMEM)
+    anywhere = pl.BlockSpec(memory_space=pl.ANY)
+
+    weights = dict(
+        value_embed=value_embed,
+        enc_qkv=enc_qkv,
+        enc_out=enc_out,
+        enc_ff_in=enc_ff_in,
+        enc_ff_out=enc_ff_out,
+        dec_qkv=dec_qkv,
+        dec_out=dec_out,
+        cross_qkv=cross_qkv,
+        cross_out=cross_out,
+        dec_ff_in=dec_ff_in,
+        dec_ff_out=dec_ff_out,
+    )
+    scalars = dict(item_group=item_group, tau_scale=tau_scale)
+    blocks = dict(
+        enc_in=enc_in[0],
+        series=series[0],
+        channel_mask=channel_mask,
+        delta_shift=delta_shift,
+        dec_in=dec_in[0],
+        cotangent=cotangent[0],
+        enc_query_bias=enc_query_bias[None],
+        enc_bias=enc_bias,
+        enc_gain=enc_gain,
+        dec_bias=dec_bias,
+        dec_gain=dec_gain,
+        ff_bias=ff_bias,
+    )
+    inputs = (scalars, blocks, dict(weight=weights))
+    in_specs = (
+        [in_smem] * len(scalars) + [in_vmem] * len(blocks) + [anywhere] * len(weights)
+    )
+
+    def low(*shape):
+        return pltpu.VMEM(shape, BF16)
+
+    def full(*shape):
+        return pltpu.VMEM(shape, F32)
+
+    def exchanged(features):
+        return low(QUAD, rows, features)
+
+    def attention_space():
+        packed = low(chips, rows // 2, LANES)
+        paired = low(chips, rows, LANES)
+        both = low(chips, CORES, rows, LANES)
+        return dict(
+            query=packed,
+            t_query=packed,
+            mixed=packed,
+            t_mixed=packed,
+            grad=packed,
+            t_grad=packed,
+            query_grad=packed,
+            t_query_grad=packed,
+            t_pair=paired,
+            pair=both,
+            t_pair_grad=paired,
+            pair_grad=paired,
+            t_part=low(CORES, chips, rows, LANES),
+            part=paired,
+            pair_t=low(LANES, keys_total),
+            weights=low(HALVES, keys_total, queries),
+            inverse=full(HALVES, 8, queries),
+            mixed_t=full(LANES, queries),
+        )
+
+    def feed_forward_space():
+        return dict(
+            hidden=exchanged(width), act=exchanged(hidden), slope=full(rows, hidden)
+        )
+
+    def group_space(count, features):
+        half = count // 2
+        return dict(
+            cut=exchanged(features),
+            met=exchanged(features),
+            part=low(2, depth, half, width),
+            item=low(depth, half, width),
+            half=low(depth, half, width),
+            depth=low(depth - 1, half, width),
+        )
+
+    group_rows = (2 * LANES + column, 3 * LANES + column, 2 * LANES + column)
+    group_features = (hidden // QUAD + 2 * LANES, hidden // QUAD + 6 * LANES, 7 * LANES)
+    scratch = dict(
+        held={name: low(*value.shape) for name, value in weights.items()},
+        x_series=exchanged(padded),
+        x_enc_hidden=exchanged(width),
+        x_dec_in=exchanged(width),
+        x_enc_mixed=exchanged(width),
+        x_memory=exchanged(width),
+        x_self_mixed=exchanged(width),
+        x_cross_hidden=exchanged(width),
+        x_cross_mixed=exchanged(width),
+        enc_ff=feed_forward_space(),
+        dec_ff=feed_forward_space(),
+        attention=[attention_space() for index in range(3)],
+        group=[group_space(*sizes) for sizes in zip(group_rows, group_features)],
+        pair_sum=full(CORES, chips, rows, LANES),
+        t_shift=full(8, LANES),
+        shift=full(chips, CORES, 8, LANES),
+        shift_columns=full(keys_total, LANES),
+        embedded=full(rows, width),
+        first_dec=full(rows, width),
+        second_grad=full(rows, width),
+        first_grad=full(rows, width),
+        enc_first_grad=full(rows, width),
+        unit=full(4, rows, width),
+        scale=full(4, rows, LANES),
+        vec=full(32, width),
+        vec_item=full(32, width),
+        vec_a=full(32, width),
+        vec_core=full(32, width),
+        vec_b=full(32, width),
+        vec_x=full(32, width),
+        vec_c=full(32, width),
+        vec_depth=full(depth - 1, 32, width),
+        load_sem=pltpu.SemaphoreType.DMA((len(weights),)),
+        send_sem=pltpu.SemaphoreType.DMA((LINK_COUNT,)),
+        recv_sem=pltpu.SemaphoreType.DMA((LINK_COUNT,)),
+    )
+    outputs = dict(
+        dec_result=jax.ShapeDtypeStruct((rows, width), BF16),
+        enc_grad=jax.ShapeDtypeStruct((rows, width), F32),
+        dec_grad=jax.ShapeDtypeStruct((rows, width), F32),
+        sums=[jax.ShapeDtypeStruct((2, count // 2, width), BF16) for count in group_rows],
+        vectors=jax.ShapeDtypeStruct((32, width), F32),
+    )
+    out_shapes, out_structure = jax.tree.flatten(outputs)
+    scratch_shapes, scratch_structure = jax.tree.flatten(scratch)
+    operands = jax.tree.leaves(inputs)
+    structures = [jax.tree.structure(part) for part in inputs]
+    results = pl.pallas_call(
+        partial(fused_body, structures + [out_structure, scratch_structure]),
+        out_shape=out_shapes,
+        in_specs=in_specs,
+        out_specs=[in_vmem] * len(out_shapes),
+        scratch_shapes=scratch_shapes,
+        compiler_params=pltpu.CompilerParams(
+            collective_id=1, has_side_effects=True, vmem_limit_bytes=VMEM_BYTES
+        ),
+        name="layers",
+    )(*operands)
+    results = jax.tree.unflatten(out_structure, results)
+    results = [
+        results[key] for key in ("dec_result", "enc_grad", "dec_grad")
+    ] + results["sums"] + [results["vectors"]]
+
+    final = [
+        (rows, width),
+        (rows, width),
+        (rows, width),
+        (column, channels),
+        (3, column, width),
+        (column, width),
+        (width, hidden // (chips * CORES)),
+        (column, hidden),
+        (1, column),
+        (5, column),
+        (2, column),
+        (3, column, width),
+        (column, width),
+        (3, column, width),
+        (column, width),
+        (width, hidden // (chips * CORES)),
+        (column, hidden),
+        (10, column),
+        (3, column),
+        (2, hidden // (chips * CORES)),
+    ]
+    outputs = pl.pallas_call(
+        finish_body,
+        out_shape=[
+            jax.ShapeDtypeStruct(shape, BF16 if index == 0 else F32)
+            for index, shape in enumerate(final)
+        ],
+        in_specs=[in_vmem] * len(results),
+        out_specs=[in_vmem] * len(final),
+        compiler_params=pltpu.CompilerParams(vmem_limit_bytes=VMEM_BYTES),
+        name="columns",
+    )(*results)
+    outputs = list(outputs)
+    for index in range(3):
+        outputs[index] = outputs[index][None]
+    outputs[8] = outputs[8][0]
+    for index in (3, 4, 5, 7, 11, 12, 13, 14, 16):
+        outputs[index] = jnp.swapaxes(outputs[index], -1, -2)
+    return tuple(outputs)
+
+
 def solution(mesh):
     in_specs = (
-        P("batch", "seq", None),
-        P("batch", "seq", None),
+        P(BATCH, SEQ, None),
+        P(BATCH, SEQ, None),
         P(),
-        P("batch"),
-        P("batch"),
-        P("batch", "seq"),
-        P("batch", "seq", None),
+        P(BATCH),
+        P(BATCH),
+        P(BATCH, SEQ),
+        P(BATCH, SEQ, None),
         P(),
         P(),
         P(),
@@ -659,28 +1826,30 @@
         P(),
         P(),
         P(),
-        P("batch", "seq", None),
+        P(BATCH, SEQ, None),
     )
     out_specs = (
-        P("batch", "seq", None),
-        P("batch", "seq", None),
-        P("batch", "seq", None),
-        P(None, "seq"),
-        P(None, None, "seq"),
-        P(None, "seq"),
-        P(None, "seq"),
-        P(None, "seq"),
-        P("seq"),
-        P(None, "seq"),
-        P(None, "seq"),
-        P(None, None, "seq"),
-        P(None, "seq"),
-        P(None, None, "seq"),
-        P(None, "seq"),
-        P(None, "seq"),
-        P(None, "seq"),
-        P(None, "seq"),
-        P(None, "seq"),
-        P(None, "seq"),
-    )
-    return jax.shard_map(local, mesh=mesh, in_specs=in_specs, out_specs=out_specs, check_vma=False)
+        P(BATCH, SEQ, None),
+        P(BATCH, SEQ, None),
+        P(BATCH, SEQ, None),
+        P(None, SEQ),
+        P(None, None, SEQ),
+        P(None, SEQ),
+        P(None, SEQ),
+        P(None, SEQ),
+        P(SEQ),
+        P(None, SEQ),
+        P(None, SEQ),
+        P(None, None, SEQ),
+        P(None, SEQ),
+        P(None, None, SEQ),
+        P(None, SEQ),
+        P(None, SEQ),
+        P(None, SEQ),
+        P(None, SEQ),
+        P(None, SEQ),
+        P(None, SEQ),
+    )
+    fits = mesh.shape[SEQ] == HEADS * CORES and mesh.shape[BATCH] == 2
+    return jax.shard_map(
+        fused_local if fits else local, mesh=mesh, in_specs=in_specs, out_specs=out_specs, check_vma=False)

time: 1670 us -> 152 us (0.09)
  waiting for transfers between devices: 1150 us -> 0 us
  blocking collectives: 193 us -> 0 us
  Pallas kernels: 0 us -> 149 us
  local copies, waits for them, and re-layouts: 130 us -> 0 us
  matrix products: 127 us -> 0 us
  other arithmetic: 32.3 us -> 0 us
  between operations: 20.1 us -> 2.12 us
    reduce_scatter x9 -> x0, waiting for transfers between devices: 613 us -> none  [the longest x1 76.1 us: local(): lax.psum_scatter(enc_ff_in_grad, 'seq', scatter_dimension=1, tiled=True)]
    unnamed x34 -> x0, waiting for transfers between devices: 339 us -> none
    pallas_call x0 -> x2, Pallas kernels: none -> 149 us  [the longest x1 146 us: fused_local(): pl.pallas_call(partial(fused_body, structures + [out_structure, scratch_s...]
    all_gather x12 -> x0, waiting for transfers between devices: 144 us -> none  [the longest x1 37.4 us: local(): lax.all_gather(self_key, 'seq', axis=1, tiled=True)]
    dot_general x93 -> x0, matrix products: 127 us -> none  [the longest x17 29.8 us: project(): return jnp.dot(inputs, weight_matrix, preferred_element_type=jnp.float32)]
    all_gather x6 -> x0, blocking collectives: 120 us -> none  [the longest x1 23.5 us: local(): lax.all_gather(self_log, 'seq', axis=1, tiled=True)]
    unnamed x2 -> x0, blocking collectives: 64.6 us -> none
    unnamed x431 -> x0, local copies, waits for them, and re-layouts: 58.4 us -> none
  transfers between devices with their start and end apart: 28 -> 0, of which waited for: 22 -> 0; matrix products, arithmetic and copies ran while one was open for 16% -> 0% of each run, Pallas kernels for 0% -> 0%
where the time goes in v1:
time: 152 us; the launch traced here: 151 us
  Pallas kernels  149 us (98%)
  between operations  2.12 us (1%)
    pallas_call x1, Pallas kernels, fused_local(): pl.pallas_call(partial(fused_body, structures + [out_structure, scratch_s...  146 us

profile of v1, /device:TPU:0, one launch (start us, length us, event | category | flops | bytes accessed | tf_op | source)
XLA Modules:
  0.0 151.3 jit_solution(9800706870780994255)
XLA Ops:
  2.0 146.4 %layers.1 = (f32[64,512]{1,0:T(8,128)}, bf16[64,512]{1,0:T(8,128)(2,1)}, f32[64,512]{1,0:T(8,128)}, bf16[2,144,512]{2,1,0:T(8,128)(2,1)}, bf16[2,208,512]{2,1,0:...) custom-call(s32[1]{0:T(128)S(6)} %copy.45.refs_0_, f32[1]{0:T(128)S(6)} %copy.46.refs_1_, ...), custom_call_target="tpu_custom_call" | custom-call | tf_op jit(solution)/shard_map/layers/pallas_call | solution.py:1745
  148.3 2.8 %columns.1 = (bf16[64,512]{1,0:T(8,128)(2,1)}, f32[64,512]{1,0:T(8,128)}, f32[64,512]{1,0:T(8,128)}, f32[32,862]{1,0:T(8,128)}, f32[3,32,512]{2,1,0:T(8,128)}, /...) custom-call(bf16[64,512]{1,0:T(8,128)(2,1)} %get-tuple-element.47.re, ...), custom_call_target="tpu_custom_call" | custom-call | tf_op jit(solution)/shard_map/columns/pallas_call | solution.py:1783

commit v2 on v1

--- a/solution.py
+++ b/solution.py
@@ -646,6 +646,7 @@
 LANES = 128
 LINK_COUNT = 320
 VMEM_BYTES = 60 << 20
+LOAD_FIRST = 3
 LOAD_ORDER = (
     "value_embed",
     "enc_qkv",
@@ -763,7 +764,9 @@
 class Weight:
     def __init__(self, copy, held):
         self.copy, self.held, self.here = copy, held, False
-        copy.start()
+
+    def start(self):
+        self.copy.start()
 
     def __call__(self):
         if not self.here:
@@ -779,6 +782,7 @@
         entries.update(jax.tree.unflatten(structure, refs[:count]))
         refs = refs[count:]
     ref = View(entries)
+    small = View(entries["held_blocks"])
     rows, width = ref.enc_in.shape
     hidden, channels, chips = ref.ff_bias.shape[1], ref.series.shape[1], HEADS
     packed_rows = rows // 2
@@ -813,12 +817,27 @@
     for device in greeted:
         pl.semaphore_signal(barrier, inc=1, device_id=device, device_id_type=MESH)
 
+    blocks = []
+    for index, (name, target) in enumerate(entries["held_blocks"].items()):
+        blocks.append(pltpu.make_async_copy(entries[name], target, ref.block_sem.at[index]))
+        blocks[-1].start()
     loaded = {}
     for index, name in enumerate(LOAD_ORDER):
         source, target = getattr(ref.weight, name), getattr(ref.held, name)
         copy = pltpu.make_async_copy(source, target, ref.load_sem.at[index])
         loaded[name] = Weight(copy, target)
     weight = View(loaded)
+    for name in LOAD_ORDER[:LOAD_FIRST]:
+        loaded[name].start()
+    for copy in blocks:
+        copy.wait()
+
+    stores = []
+
+    def store(source, target):
+        index = len(stores)
+        stores.append(pltpu.make_async_copy(source, target, ref.store_sem.at[index]))
+        stores[-1].start()
 
     sends = []
 
@@ -953,35 +972,53 @@
         result[item] = value.astype(BF16)
         return [send(result.at[item], result.at[item], item_dev)]
 
+    def finish(group, index, copies):
+        arrive(copies)
+        store(group.sum, ref.sums[index])
+
     def set_vector(row, value):
         ref.vec[row : row + 1, :] = value
 
     att_enc, att_self, att_cross = ref.attention
-    one, two, three = ref.group
-    for group, result in zip(ref.group, ref.sums):
-        group.sum = result
+    dec_in_part, dec_out_part, cross_part, enc_in_part, enc_out_part, self_part, last_part = (
+        ref.group
+    )
     enc_ff = (weight.enc_ff_in, weight.enc_ff_out)
     dec_ff = (weight.dec_ff_in, weight.dec_ff_out)
 
+    def build(group, row, start, features, block, wide=False):
+        gradient = mm_left_t(columns_of(group, start, start + features), gathered(block))
+        if wide:
+            put_gradient(group.part, row, gradient)
+            return
+        for which in range(features // LANES):
+            put_gradient(
+                group.part,
+                row + which * column,
+                gradient[which * LANES : (which + 1) * LANES],
+            )
+
     tau = ref.tau_scale[0]
-    group_row = lax.broadcasted_iota(jnp.int32, ref.channel_mask.shape, 0)
+    group_row = lax.broadcasted_iota(jnp.int32, small.channel_mask.shape, 0)
     chosen = jnp.where(
-        group_row == ref.item_group[0], ref.channel_mask[...].astype(F32), 0.0
+        group_row == ref.item_group[0], small.channel_mask[...].astype(F32), 0.0
     )
     channel_row = jnp.sum(chosen, axis=0, keepdims=True)
-    masked = (ref.series[...].astype(F32) * channel_row).astype(BF16)
+    masked = (small.series[...].astype(F32) * channel_row).astype(BF16)
     ref.x_series[quad] = jnp.zeros(ref.x_series.shape[1:], BF16)
     ref.x_series[quad, :, 0:channels] = masked
 
-    shift_row = ref.delta_shift[...].astype(F32)
+    shift_row = small.delta_shift[...].astype(F32)
     ref.t_shift[...] = jnp.broadcast_to(
         jnp.concatenate([shift_row, shift_row], axis=1), ref.t_shift.shape
     )
 
-    embedded = ref.enc_in[...].astype(F32) + mm(masked, weight.value_embed()[...])
+    embedded = small.enc_in[...].astype(F32) + mm(masked, weight.value_embed()[...])
     ref.embedded[...] = embedded
     enc_hidden = embedded.astype(BF16)
     ref.x_enc_hidden[quad] = enc_hidden
+    for name in LOAD_ORDER[LOAD_FIRST:]:
+        loaded[name].start()
 
     def send_queries(own, query):
         for head, packed in enumerate(pack_rows(query)):
@@ -1000,9 +1037,9 @@
         return [send(block.at[:, core], block.at[:, core], core_dev)]
 
     qkv = weight.enc_qkv()
-    enc_query = mm(enc_hidden, qkv[0]) + ref.enc_query_bias[...]
+    enc_query = mm(enc_hidden, qkv[0]) + small.enc_query_bias[...]
     enc_key = mm(enc_hidden, qkv[1])
-    enc_value = mm(enc_hidden, qkv[2]) + ref.enc_bias[0:1, :]
+    enc_value = mm(enc_hidden, qkv[2]) + small.enc_bias[0:1, :]
     pl.semaphore_wait(barrier, len(greeted))
     go_enc_pair = send_pairs(att_enc, enc_key, enc_value)
     go_enc_query = send_queries(att_enc, enc_query)
@@ -1013,12 +1050,12 @@
             send(ref.t_shift, ref.shift.at[chip, core], same_core(step)[1])
         )
 
-    dec_hidden = ref.dec_in[...]
+    dec_hidden = small.dec_in[...]
     ref.x_dec_in[quad] = dec_hidden
     qkv = weight.dec_qkv()
-    self_query = mm(dec_hidden, qkv[0]) + ref.dec_bias[0:1, :]
+    self_query = mm(dec_hidden, qkv[0]) + small.dec_bias[0:1, :]
     self_key = mm(dec_hidden, qkv[1])
-    self_value = mm(dec_hidden, qkv[2]) + ref.dec_bias[1:2, :]
+    self_value = mm(dec_hidden, qkv[2]) + small.dec_bias[1:2, :]
     go_self_pair = send_pairs(att_self, self_key, self_value)
     go_self_query = send_queries(att_self, self_query)
 
@@ -1088,7 +1125,7 @@
         total = out_bias
         for piece in range(hidden // width):
             cut = slice(piece * width, (piece + 1) * width)
-            pre = mm(low, weight_in[:, cut]) + ref.ff_bias[bias_row : bias_row + 1, cut]
+            pre = mm(low, weight_in[:, cut]) + small.ff_bias[bias_row : bias_row + 1, cut]
             normal = 0.5 * (1.0 + lax.erf(pre * 0.7071067811865476))
             act = (pre * normal).astype(BF16)
             side.slope[:, cut] = normal + pre * (
@@ -1129,39 +1166,39 @@
     attended = mixed_rows(att_enc)
     ref.x_enc_mixed[quad] = attended
     first, unit, scale = norm_forward(
-        embedded + mm(attended, weight.enc_out()[...]) + ref.enc_bias[1:2, :],
-        ref.enc_gain[0:1, :],
-        ref.enc_bias[3:4, :],
+        embedded + mm(attended, weight.enc_out()[...]) + small.enc_bias[1:2, :],
+        small.enc_gain[0:1, :],
+        small.enc_bias[3:4, :],
     )
     save_norm(0, unit, scale)
     second, unit, scale = norm_forward(
-        first + feed_forward(first, enc_ff, 0, ref.enc_bias[2:3, :], ref.enc_ff),
-        ref.enc_gain[1:2, :],
-        ref.enc_bias[4:5, :],
+        first + feed_forward(first, enc_ff, 0, small.enc_bias[2:3, :], ref.enc_ff),
+        small.enc_gain[1:2, :],
+        small.enc_bias[4:5, :],
     )
     save_norm(1, unit, scale)
     memory = second.astype(BF16)
     ref.x_memory[quad] = memory
     qkv = weight.cross_qkv()
     cross_key = mm(memory, qkv[1])
-    cross_value = mm(memory, qkv[2]) + ref.dec_bias[4:5, :]
+    cross_value = mm(memory, qkv[2]) + small.dec_bias[4:5, :]
     go_cross_pair = send_pairs(att_cross, cross_key, cross_value)
 
     arrive(back_self)
     attended = mixed_rows(att_self)
     ref.x_self_mixed[quad] = attended
     first, unit, scale = norm_forward(
-        ref.dec_in[...].astype(F32)
+        small.dec_in[...].astype(F32)
         + mm(attended, weight.dec_out()[...])
-        + ref.dec_bias[2:3, :],
-        ref.dec_gain[0:1, :],
-        ref.dec_bias[7:8, :],
+        + small.dec_bias[2:3, :],
+        small.dec_gain[0:1, :],
+        small.dec_bias[7:8, :],
     )
     save_norm(2, unit, scale)
     ref.first_dec[...] = first
     low = first.astype(BF16)
     ref.x_cross_hidden[quad] = low
-    go_cross_query = send_queries(att_cross, mm(low, qkv[0]) + ref.dec_bias[3:4, :])
+    go_cross_query = send_queries(att_cross, mm(low, qkv[0]) + small.dec_bias[3:4, :])
     for shared in shares:
         relay(shared)
     shares_two = [
@@ -1189,18 +1226,22 @@
     second, unit, scale = norm_forward(
         ref.first_dec[...]
         + mm(attended, weight.cross_out()[...])
-        + ref.dec_bias[5:6, :],
-        ref.dec_gain[1:2, :],
-        ref.dec_bias[8:9, :],
+        + small.dec_bias[5:6, :],
+        small.dec_gain[1:2, :],
+        small.dec_bias[8:9, :],
     )
     save_norm(3, unit, scale)
-
+    shares_four = [share(ref.x_cross_mixed)]
+
+    forward = feed_forward(second, dec_ff, 1, small.dec_bias[6:7, :], ref.dec_ff)
+    shares_four += [share(ref.dec_ff.hidden), share(ref.dec_ff.act)]
     third, unit, scale = norm_forward(
-        second + feed_forward(second, dec_ff, 1, ref.dec_bias[6:7, :], ref.dec_ff),
-        ref.dec_gain[2:3, :],
-        ref.dec_bias[9:10, :],
-    )
-    ref.dec_result[...] = third.astype(BF16)
+        second + forward,
+        small.dec_gain[2:3, :],
+        small.dec_bias[9:10, :],
+    )
+    ref.o_dec_result[...] = third.astype(BF16)
+    store(ref.o_dec_result, ref.dec_result)
 
     def norm_step(index, upstream, gain, gain_row, gain_vector, shift_vector):
         unit, scale = saved_norm(index)
@@ -1215,12 +1256,12 @@
         return jnp.sum(rounded(values), axis=0, keepdims=True)
 
     third_grad, gain_grad, shift_grad = norm_back(
-        ref.cotangent[...].astype(F32), unit, scale, ref.dec_gain[2:3, :]
+        small.cotangent[...].astype(F32), unit, scale, small.dec_gain[2:3, :]
     )
     set_vector(20, gain_grad)
     set_vector(17, shift_grad)
-    from_ff = feed_forward_back(third_grad, dec_ff, ref.dec_ff, 25, one)
-    second_grad = norm_step(3, third_grad + from_ff, ref.dec_gain, 1, 19, 16)
+    from_ff = feed_forward_back(third_grad, dec_ff, ref.dec_ff, 25, dec_in_part)
+    second_grad = norm_step(3, third_grad + from_ff, small.dec_gain, 1, 19, 16)
     ref.second_grad[...] = second_grad
 
     def send_mixed_grad(own, branch_grad, out_weight):
@@ -1231,14 +1272,15 @@
         return spread(own.t_grad, lambda at: own.grad.at[at])
 
     go_cross_grad = send_mixed_grad(att_cross, second_grad, weight.cross_out())
-    cut_columns(third_grad, one, hidden // QUAD)
-    cut_columns(second_grad, one, hidden // QUAD + LANES)
+    ff_width = hidden // QUAD
+    columns_dec_in = share_columns(dec_in_part, 0, ff_width)
+    cut_columns(third_grad, dec_out_part, 0)
+    cut_columns(second_grad, dec_out_part, LANES)
+    columns_dec_out = share_columns(dec_out_part, 0, 2 * LANES)
     set_vector(14, column_sum(third_grad))
     set_vector(13, column_sum(second_grad))
-    columns_one = share_columns(one, 0, hidden // QUAD + 2 * LANES)
-    for shared in shares_three:
+    for shared in shares_three + shares_four:
         relay(shared)
-    shares_four = [share(block) for block in (ref.x_cross_mixed, ref.dec_ff.hidden, ref.dec_ff.act)]
 
     def attention_back(own):
         pairs = own.pair[...].reshape(keys_total, LANES)
@@ -1300,30 +1342,17 @@
 
     arrive(go_cross_grad)
     go_query, exchange = attention_back(att_cross)
-    for shared in shares_four:
-        relay(shared)
     go_pair = attention_back_pairs(att_cross, exchange)
 
-    ff_width = hidden // QUAD
     for shared in shares_four:
         settle(shared)
-    arrive(columns_one)
-    put_gradient(
-        one.part, 0, mm_left_t(columns_of(one, 0, ff_width), gathered(ref.dec_ff.hidden))
-    )
-    put_gradient(
-        one.part,
-        LANES,
-        mm_left_t(columns_of(one, ff_width, ff_width + LANES), gathered(ref.dec_ff.act)),
-    )
-    put_gradient(
-        one.part,
-        2 * LANES,
-        mm_left_t(
-            columns_of(one, ff_width + LANES, ff_width + 2 * LANES), gathered(ref.x_cross_mixed)
-        ),
-    )
-    item_one = reduce_item(one)
+    arrive(columns_dec_in)
+    build(dec_in_part, 0, 0, ff_width, ref.dec_ff.hidden, wide=True)
+    item_dec_in = reduce_item(dec_in_part)
+    arrive(columns_dec_out)
+    build(dec_out_part, 0, 0, LANES, ref.dec_ff.act)
+    build(dec_out_part, LANES, LANES, LANES, ref.x_cross_mixed)
+    item_dec_out = reduce_item(dec_out_part)
 
     qkv = weight.cross_qkv()
     arrive(go_query)
@@ -1331,7 +1360,7 @@
     first_grad = norm_step(
         2,
         ref.second_grad[...] + mm_right_t(cross_query_grad.astype(BF16), qkv[0]),
-        ref.dec_gain,
+        small.dec_gain,
         0,
         18,
         15,
@@ -1345,9 +1374,9 @@
     memory_grad = mm_right_t(cross_key_grad.astype(BF16), qkv[1]) + mm_right_t(
         cross_value_grad.astype(BF16), qkv[2]
     )
-    enc_second_grad = norm_step(1, memory_grad, ref.enc_gain, 1, 7, 5)
-    from_ff = feed_forward_back(enc_second_grad, enc_ff, ref.enc_ff, 21, two)
-    enc_first_grad = norm_step(0, enc_second_grad + from_ff, ref.enc_gain, 0, 6, 4)
+    enc_second_grad = norm_step(1, memory_grad, small.enc_gain, 1, 7, 5)
+    from_ff = feed_forward_back(enc_second_grad, enc_ff, ref.enc_ff, 21, enc_in_part)
+    enc_first_grad = norm_step(0, enc_second_grad + from_ff, small.enc_gain, 0, 6, 4)
     ref.enc_first_grad[...] = enc_first_grad
     go_enc_grad = send_mixed_grad(att_enc, enc_first_grad, weight.enc_out())
     set_vector(3, column_sum(enc_second_grad))
@@ -1358,58 +1387,52 @@
         set_vector(row, jnp.zeros((1, width), F32))
     vec_item = send(ref.vec, ref.vec_item, item_dev)
     for index, values in enumerate(
-        (enc_second_grad, enc_first_grad, first_grad)
-        + (cross_query_grad, cross_key_grad, cross_value_grad)
+        (cross_query_grad, cross_key_grad, cross_value_grad, first_grad)
     ):
-        cut_columns(values, two, ff_width + index * LANES)
-    columns_two = share_columns(two, 0, ff_width + 6 * LANES)
+        cut_columns(values, cross_part, index * LANES)
+    columns_cross = share_columns(cross_part, 0, 4 * LANES)
+    columns_enc_in = share_columns(enc_in_part, 0, ff_width)
+    cut_columns(enc_second_grad, enc_out_part, 0)
+    cut_columns(enc_first_grad, enc_out_part, LANES)
+    columns_enc_out = share_columns(enc_out_part, 0, 2 * LANES)
 
     arrive(go_self_grad)
     go_self_query_grad, exchange = attention_back(att_self)
-    arrive(item_one)
-    depth_one = reduce_depth(one)
+    arrive(item_dec_in)
+    depth_dec_in = reduce_depth(dec_in_part)
     go_self_pair_grad = attention_back_pairs(att_self, exchange)
+    for shared in shares + shares_two + shares_three:
+        settle(shared)
+    arrive(columns_cross)
+    build(cross_part, 0, 0, LANES, ref.x_cross_hidden)
+    build(cross_part, column, LANES, 2 * LANES, ref.x_memory)
+    build(cross_part, 3 * column, 3 * LANES, LANES, ref.x_self_mixed)
+    item_cross = reduce_item(cross_part)
     vec_item.wait_recv()
     ref.vec_a[...] = ref.vec[...] + ref.vec_item[...]
     vec_core = send(ref.vec_a, ref.vec_core, core_dev)
     arrive(go_enc_grad)
     go_enc_query_grad, exchange = attention_back(att_enc)
+    go_enc_pair_grad = attention_back_pairs(att_enc, exchange)
     vec_core.wait_recv()
     ref.vec_b[...] = ref.vec_a[...] + ref.vec_core[...]
     vec_x = send(ref.vec_b, ref.vec_x, x_dev)
-    go_enc_pair_grad = attention_back_pairs(att_enc, exchange)
-
-    for shared in shares + shares_two + shares_three:
-        settle(shared)
-    arrive(columns_two)
-    put_gradient(
-        two.part, 0, mm_left_t(columns_of(two, 0, ff_width), gathered(ref.enc_ff.hidden))
-    )
-    put_gradient(
-        two.part,
-        LANES,
-        mm_left_t(columns_of(two, ff_width, ff_width + LANES), gathered(ref.enc_ff.act)),
-    )
-    for index, (block, count) in enumerate(
-        ((ref.x_enc_mixed, 1), (ref.x_self_mixed, 1), (ref.x_cross_hidden, 1), (ref.x_memory, 2))
-    ):
-        start = ff_width + (index + 1) * LANES
-        gradient = mm_left_t(columns_of(two, start, start + count * LANES), gathered(block))
-        for which in range(count):
-            put_gradient(
-                two.part,
-                2 * LANES + (index + which) * column,
-                gradient[which * LANES : (which + 1) * LANES],
-            )
-    item_two = reduce_item(two)
+    arrive(item_dec_out)
+    depth_dec_out = reduce_depth(dec_out_part)
+
+    arrive(columns_enc_in)
+    build(enc_in_part, 0, 0, ff_width, ref.enc_ff.hidden, wide=True)
+    item_enc_in = reduce_item(enc_in_part)
+    arrive(columns_enc_out)
+    build(enc_out_part, 0, 0, LANES, ref.enc_ff.act)
+    build(enc_out_part, LANES, LANES, LANES, ref.x_enc_mixed)
+    item_enc_out = reduce_item(enc_out_part)
     vec_x.wait_recv()
     ref.vec_c[...] = ref.vec_b[...] + ref.vec_x[...]
     vec_depth = [
         send(ref.vec_c, ref.vec_depth.at[step - 1], z_peer(step)[1])
         for step in range(1, depth)
     ]
-    arrive(depth_one)
-    last_one = reduce_last(one)
 
     def input_grad(own, weights, first):
         query_grad = query_grad_rows(own)
@@ -1425,61 +1448,77 @@
     arrive(go_self_query_grad)
     arrive(go_self_pair_grad)
     total, query_grad, key_grad, value_grad = input_grad(att_self, weight.dec_qkv(), ref.first_grad)
-    ref.dec_grad[...] = total
+    ref.o_dec_grad[...] = total
+    store(ref.o_dec_grad, ref.dec_grad)
     for index, values in enumerate((query_grad, key_grad, value_grad)):
-        cut_columns(values, three, index * LANES)
-    columns_self = share_columns(three, 0, 3 * LANES)
-    arrive(item_two)
-    depth_two = reduce_depth(two)
+        cut_columns(values, self_part, index * LANES)
+    columns_self = share_columns(self_part, 0, 3 * LANES)
+    arrive(depth_dec_in)
+    last_dec_in = reduce_last(dec_in_part)
+    arrive(item_cross)
+    depth_cross = reduce_depth(cross_part)
     arrive(go_enc_query_grad)
     arrive(go_enc_pair_grad)
     total, query_grad, key_grad, value_grad = input_grad(att_enc, weight.enc_qkv(), ref.enc_first_grad)
-    ref.enc_grad[...] = total
+    ref.o_enc_grad[...] = total
+    store(ref.o_enc_grad, ref.enc_grad)
     for index, values in enumerate((query_grad, key_grad, value_grad, total)):
-        cut_columns(values, three, (3 + index) * LANES)
-    columns_enc = share_columns(three, 3 * LANES, 7 * LANES)
+        cut_columns(values, last_part, index * LANES)
+    columns_enc = share_columns(last_part, 0, 4 * LANES)
     arrive(columns_self)
-
-    def gradient_three(start, count, block, row):
-        gradient = mm_left_t(
-            columns_of(three, start * LANES, (start + count) * LANES), gathered(block)
-        )
-        for which in range(count):
-            put_gradient(
-                three.part, row + which * column, gradient[which * LANES : (which + 1) * LANES]
-            )
-
-    gradient_three(0, 3, ref.x_dec_in, 0)
+    build(self_part, 0, 0, 3 * LANES, ref.x_dec_in)
+    item_self = reduce_item(self_part)
+    arrive(depth_dec_out)
+    last_dec_out = reduce_last(dec_out_part)
+    arrive(item_enc_in)
+    depth_enc_in = reduce_depth(enc_in_part)
     arrive(columns_enc)
-    gradient_three(3, 3, ref.x_enc_hidden, 3 * column)
-    gradient_three(6, 1, ref.x_series, 6 * column)
+    build(last_part, 0, 0, 3 * LANES, ref.x_enc_hidden)
+    build(last_part, 3 * column, 3 * LANES, LANES, ref.x_series)
     totals = [
         jnp.sum(
-            columns_of(three, index * LANES, (index + 1) * LANES).astype(F32),
+            columns_of(group, index * LANES, (index + 1) * LANES).astype(F32),
             axis=0,
             keepdims=True,
         )
-        for index in (0, 2, 3, 5)
+        for group, index in ((self_part, 0), (self_part, 2), (last_part, 0), (last_part, 2))
     ]
     totals = jnp.concatenate(totals + [jnp.zeros((column - 4, LANES), F32)], axis=0)
     totals = jnp.concatenate([totals, jnp.zeros((column, width - LANES), F32)], axis=1)
     for level in range(depth):
-        put_rows(three.part, level, 8 * column, totals.astype(BF16))
-    item_three = reduce_item(three)
+        put_rows(last_part.part, level, 5 * column, totals.astype(BF16))
+    item_last = reduce_item(last_part)
     arrive(vec_depth)
     total = ref.vec_c[...]
     for step in range(1, depth):
         total = total + ref.vec_depth[step - 1]
-    ref.vectors[...] = total
-    arrive(depth_two)
-    last_two = reduce_last(two)
-    arrive(item_three)
-    depth_three = reduce_depth(three)
-    arrive(last_one)
-    arrive(last_two)
-    arrive(depth_three)
-    last_three = reduce_last(three)
-    arrive(last_three)
+    ref.o_vectors[...] = total
+    store(ref.o_vectors, ref.vectors)
+    arrive(item_enc_out)
+    depth_enc_out = reduce_depth(enc_out_part)
+    arrive(depth_cross)
+    last_cross = reduce_last(cross_part)
+    arrive(item_self)
+    depth_self = reduce_depth(self_part)
+    arrive(depth_enc_in)
+    last_enc_in = reduce_last(enc_in_part)
+    arrive(item_last)
+    depth_last = reduce_depth(last_part)
+    arrive(depth_enc_out)
+    last_enc_out = reduce_last(enc_out_part)
+    finish(dec_in_part, 0, last_dec_in)
+    finish(dec_out_part, 1, last_dec_out)
+    finish(cross_part, 2, last_cross)
+    arrive(depth_self)
+    last_self = reduce_last(self_part)
+    arrive(depth_last)
+    last_last = reduce_last(last_part)
+    finish(enc_in_part, 3, last_enc_in)
+    finish(enc_out_part, 4, last_enc_out)
+    finish(self_part, 5, last_self)
+    finish(last_part, 6, last_last)
+    for copy in stores:
+        copy.wait()
     for copy in sends:
         copy.wait_send()
 
@@ -1489,9 +1528,13 @@
         dec_in,
         enc_grad_in,
         dec_grad_in,
-        one,
-        two,
-        three,
+        ff_in_two,
+        ff_out_two,
+        cross,
+        ff_in_one,
+        ff_out_one,
+        self_part,
+        last,
         vectors,
         dec_out,
         enc_grad,
@@ -1532,29 +1575,31 @@
                 start + piece * column : start + (piece + 1) * column
             ]
 
-    first = whole(one)
-    g_dec_ff_in[...] = first[0:LANES].T
-    narrow(g_dec_ff_out, first, LANES)
-    narrow(g_cross_out, first, 2 * LANES)
-    second = whole(two)
-    g_enc_ff_in[...] = second[0:LANES].T
-    narrow(g_enc_ff_out, second, LANES)
-    narrow(g_enc_out, second, 2 * LANES)
-    narrow(g_dec_out, second, 2 * LANES + column)
+    g_dec_ff_in[...] = whole(ff_in_two).T
+    block = whole(ff_out_two)
+    narrow(g_dec_ff_out, block, 0)
+    narrow(g_cross_out, block, LANES)
+    block = whole(cross)
     for index in range(3):
-        start = 2 * LANES + (2 + index) * column
-        g_cross_qkv[index] = second[start : start + column]
-    third = whole(three)
+        g_cross_qkv[index] = block[index * column : (index + 1) * column]
+    narrow(g_dec_out, block, 3 * column)
+    g_enc_ff_in[...] = whole(ff_in_one).T
+    block = whole(ff_out_one)
+    narrow(g_enc_ff_out, block, 0)
+    narrow(g_enc_out, block, LANES)
+    block = whole(self_part)
     for index in range(3):
-        g_dec_qkv[index] = third[index * column : (index + 1) * column]
-        g_enc_qkv[index] = third[(3 + index) * column : (4 + index) * column]
-    g_embed[:, 0:width] = third[6 * column : 7 * column]
-    g_embed[:, width:channels] = third[7 * column : 8 * column, 0 : channels - width]
+        g_dec_qkv[index] = block[index * column : (index + 1) * column]
+    block = whole(last)
+    for index in range(3):
+        g_enc_qkv[index] = block[index * column : (index + 1) * column]
+    g_embed[:, 0:width] = block[3 * column : 4 * column]
+    g_embed[:, width:channels] = block[4 * column : 5 * column, 0 : channels - width]
 
     group = vectors[:, pl.ds(pl.multiple_of(level * LANES, LANES), LANES)]
     moved = pltpu.roll(group, lax.rem(LANES - member * column, LANES), axis=1)
     rows = moved[:, 0:column]
-    late = third[2 * LANES : 2 * LANES + 8, 0:LANES]
+    late = block[5 * column : 5 * column + 8, 0:LANES]
     late = pltpu.roll(late, lax.rem(LANES - level * column, LANES), axis=1)[:, 0:column]
     g_enc_query_bias[...] = late[2:3]
     g_enc_bias[...] = jnp.concatenate([late[3:4], rows[2:6]], axis=0)
@@ -1638,9 +1683,7 @@
         ff_bias=ff_bias,
     )
     inputs = (scalars, blocks, dict(weight=weights))
-    in_specs = (
-        [in_smem] * len(scalars) + [in_vmem] * len(blocks) + [anywhere] * len(weights)
-    )
+    in_specs = [in_smem] * len(scalars) + [anywhere] * (len(blocks) + len(weights))
 
     def low(*shape):
         return pltpu.VMEM(shape, BF16)
@@ -1690,12 +1733,39 @@
             item=low(depth, half, width),
             half=low(depth, half, width),
             depth=low(depth - 1, half, width),
+            sum=low(2, half, width),
         )
 
-    group_rows = (2 * LANES + column, 3 * LANES + column, 2 * LANES + column)
-    group_features = (hidden // QUAD + 2 * LANES, hidden // QUAD + 6 * LANES, 7 * LANES)
+    ff_width = hidden // QUAD
+    group_rows = (
+        LANES,
+        LANES + column,
+        4 * column,
+        LANES,
+        LANES + column,
+        3 * column,
+        6 * column,
+    )
+    group_features = (
+        ff_width,
+        2 * LANES,
+        4 * LANES,
+        ff_width,
+        2 * LANES,
+        3 * LANES,
+        4 * LANES,
+    )
     scratch = dict(
         held={name: low(*value.shape) for name, value in weights.items()},
+        held_blocks={
+            name: pltpu.VMEM(value.shape, value.dtype) for name, value in blocks.items()
+        },
+        block_sem=pltpu.SemaphoreType.DMA((len(blocks),)),
+        store_sem=pltpu.SemaphoreType.DMA((4 + len(group_rows),)),
+        o_dec_result=low(rows, width),
+        o_enc_grad=full(rows, width),
+        o_dec_grad=full(rows, width),
+        o_vectors=full(32, width),
         x_series=exchanged(padded),
         x_enc_hidden=exchanged(width),
         x_dec_in=exchanged(width),
@@ -1746,7 +1816,7 @@
         partial(fused_body, structures + [out_structure, scratch_structure]),
         out_shape=out_shapes,
         in_specs=in_specs,
-        out_specs=[in_vmem] * len(out_shapes),
+        out_specs=[anywhere] * len(out_shapes),
         scratch_shapes=scratch_shapes,
         compiler_params=pltpu.CompilerParams(
             collective_id=1, has_side_effects=True, vmem_limit_bytes=VMEM_BYTES

time: 152 us -> 142 us (0.934)
  Pallas kernels: 149 us -> 140 us
    pallas_call x1, Pallas kernels: 146 us -> 137 us  [fused_local(): pl.pallas_call(partial(fused_body, structures + [out_structure, scratch_s...]
where the time goes in v2:
time: 142 us
  Pallas kernels  140 us (99%)
  between operations  2.12 us (1%)
    pallas_call x1, Pallas kernels, fused_local(): pl.pallas_call(partial(fused_body, structures + [out_structure, scratch_s...  137 us
    pallas_call x1, Pallas kernels, fused_local(): pl.pallas_call(finish_body, out_shape=[jax.ShapeDtypeStruct(shape, BF16 i...  2.9 us

profile of v2, /device:TPU:0, one launch (start us, length us, event | category | flops | bytes accessed | tf_op | source)
XLA Modules:
  0.0 142.0 jit_solution(6167050646180613117)
XLA Ops:
  2.0 136.9 %layers.1 = (f32[64,512]{1,0:T(8,128)}, bf16[64,512]{1,0:T(8,128)(2,1)}, f32[64,512]{1,0:T(8,128)}, bf16[2,64,512]{2,1,0:T(8,128)(2,1)}, bf16[2,80,512]{2,1,0:T(...) custom-call(s32[1]{0:T(128)S(6)} %copy.45.refs_0_, ...), custom_call_target="tpu_custom_call" | custom-call | tf_op jit(solution)/shard_map/layers/pallas_call | solution.py:1815
  138.9 2.9 %columns.1 = (bf16[64,512]{1,0:T(8,128)(2,1)}, f32[64,512]{1,0:T(8,128)}, f32[64,512]{1,0:T(8,128)}, f32[32,862]{1,0:T(8,128)}, f32[3,32,512]{2,1,0:T(8,128)}, /...) custom-call(bf16[64,512]{1,0:T(8,128)(2,1)} %get-tuple-element.51.re, ...), custom_call_target="tpu_custom_call" | custom-call | tf_op jit(solution)/shard_map/columns/pallas_call | solution.py:1853

commit v3 on v2

--- a/solution.py
+++ b/solution.py
@@ -644,7 +644,8 @@
 HALVES = 2
 CORES = 2
 LANES = 128
-LINK_COUNT = 320
+LINK_COUNT = 81
+ITEM_FIRST = (True, False, True, True, False, True, True)
 VMEM_BYTES = 60 << 20
 LOAD_FIRST = 3
 LOAD_ORDER = (
@@ -802,6 +803,9 @@
     x_dev = (z_place * QUAD + (1 - x_place) * 2 + core, item)
     diagonal_dev = (z_place * QUAD + (1 - x_place) * 2 + (1 - core), item)
     item_dev = (place, 1 - item)
+    z_high, z_odd = z_place // 2, lax.rem(z_place, 2)
+    near_dev = ((z_high * 2 + 1 - z_odd) * QUAD + quad, item)
+    far_dev = (((1 - z_high) * 2 + z_odd) * QUAD + quad, item)
     x_quad = (1 - x_place) * 2 + core
 
     def same_core(step):
@@ -839,32 +843,49 @@
         stores.append(pltpu.make_async_copy(source, target, ref.store_sem.at[index]))
         stores[-1].start()
 
-    sends = []
+    batches = []
+
+    def ship(copies, meter=None):
+        index = len(batches)
+        made = []
+        for source, target, device in copies:
+            made.append(
+                pltpu.make_async_remote_copy(
+                    src_ref=source,
+                    dst_ref=target,
+                    send_sem=ref.send_sem.at[index],
+                    recv_sem=ref.recv_sem.at[index],
+                    device_id=device,
+                    device_id_type=MESH,
+                )
+            )
+            made[-1].start()
+        batches.append((index, made, meter))
+        return batches[-1]
 
     def send(source, target, device):
-        index = len(sends)
-        copy = pltpu.make_async_remote_copy(
-            src_ref=source,
-            dst_ref=target,
-            send_sem=ref.send_sem.at[index],
-            recv_sem=ref.recv_sem.at[index],
-            device_id=device,
-            device_id_type=MESH,
-        )
-        copy.start()
-        sends.append(copy)
-        return copy
-
-    def arrive(copies):
-        for copy in copies:
-            copy.wait_recv()
+        return ship([(source, target, device)])
+
+    def arrive(batch):
+        index, made, meter = batch
+        if meter is None:
+            made[0].wait_recv()
+        else:
+            pltpu.make_async_copy(meter, meter, ref.recv_sem.at[index]).wait()
+
+    def depart(batch):
+        index, made, meter = batch
+        if meter is None:
+            made[0].wait_send()
+        else:
+            pltpu.make_async_copy(meter, meter, ref.send_sem.at[index]).wait()
 
     def spread(source, target_at):
         copies = []
         for step in range(1, chips):
             peer, device = same_core(step)
-            copies.append(send(source.at[peer], target_at(chip), device))
-        return copies
+            copies.append((source.at[peer], target_at(chip), device))
+        return ship(copies, source.at[pl.ds(0, chips - 1)])
 
     def share(block):
         return [
@@ -875,15 +896,15 @@
 
     def relay(shared):
         block = shared[0]
-        shared[2].wait_recv()
+        arrive(shared[2])
         shared.append(send(block.at[x_quad], block.at[x_quad], core_dev))
 
     def settle(shared):
-        shared[1].wait_recv()
-        shared[3].wait_recv()
-
-    def gathered(block):
-        value = block[...]
+        arrive(shared[1])
+        arrive(shared[3])
+
+    def gathered(block, start, features):
+        value = block[:, :, start : start + features]
         return value.reshape(value.shape[0] * value.shape[1], value.shape[2])
 
     def cut_columns(values, group, start):
@@ -907,26 +928,28 @@
             (diagonal_dev, (1 - x_place) * 2 + 1 - core),
         ):
             copies.append(
-                send(
+                (
                     source.at[member, :, pl.ds(start, stop - start)],
                     target.at[quad, :, pl.ds(start, stop - start)],
                     device,
                 )
             )
-        return copies
+        return ship(copies, target.at[pl.ds(0, QUAD - 1), :, pl.ds(start, stop - start)])
 
     def columns_of(group, start, stop):
         value = group.met[:, :, start:stop]
         return value.reshape(QUAD * rows, stop - start)
 
     def put_rows(target, level, start, values):
-        half = target.shape[2]
+        half = target.shape[3]
         count = values.shape[0]
         done = 0
         while done < count:
             which, offset = divmod(start + done, half)
             take = min(count - done, half - offset)
-            target[which, level, offset : offset + take, :] = values[done : done + take, :]
+            target[which, level // 2, level % 2, offset : offset + take, :] = values[
+                done : done + take, :
+            ]
             done += take
 
     def put_gradient(target, start, gradient):
@@ -949,45 +972,69 @@
                 )
                 put_rows(target, level, start + pieces * count, tail)
 
-    def reduce_item(group):
-        part, arrived = group.part, group.item
-        return [send(part.at[1 - item], arrived, item_dev)]
-
-    def reduce_depth(group):
-        part, arrived = group.part, group.item
-        total, landing = group.half, group.depth
-        total[...] = (part[item].astype(F32) + arrived[...].astype(F32)).astype(BF16)
-        copies = []
-        for step in range(1, depth):
-            peer, device = z_peer(step)
-            copies.append(send(total.at[peer], landing.at[step - 1], device))
-        return copies
-
-    def reduce_last(group):
-        total, landing = group.half, group.depth
-        result = group.sum
-        value = total[z_place].astype(F32)
-        for step in range(1, depth):
-            value = value + landing[step - 1].astype(F32)
-        result[item] = value.astype(BF16)
-        return [send(result.at[item], result.at[item], item_dev)]
-
-    def finish(group, index, copies):
-        arrive(copies)
-        store(group.sum, ref.sums[index])
+    def both_sums(left, right):
+        return (left.astype(F32) + right.astype(F32)).astype(BF16)
+
+    def item_first(group):
+        def near():
+            group.half[...] = both_sums(group.part[item], group.item[...])
+            return send(group.half.at[:, 1 - z_odd], group.near, near_dev)
+
+        def far():
+            group.pair[...] = both_sums(group.half[:, z_odd], group.near[...])
+            return send(group.pair.at[1 - z_high], group.far, far_dev)
+
+        def last():
+            group.sum[item] = both_sums(group.pair[z_high], group.far[...])
+            return send(group.sum.at[item], group.sum.at[item], item_dev)
+
+        return [lambda: send(group.part.at[1 - item], group.item, item_dev), near, far, last]
+
+    def depth_first(group):
+        def far():
+            group.pair[...] = both_sums(group.part[0, :, z_odd], group.near[...])
+            return send(group.pair.at[1 - z_high], group.far, far_dev)
+
+        def items():
+            group.half[...] = both_sums(group.pair[z_high], group.far[...])
+            return send(group.half, group.item, item_dev)
+
+        def last():
+            group.sum[0] = both_sums(group.half[...], group.item[...])
+            return None
+
+        return [
+            lambda: send(group.part.at[0, :, 1 - z_odd], group.near, near_dev),
+            far,
+            items,
+            last,
+        ]
+
+    def advance(group):
+        if group.batch is not None:
+            arrive(group.batch)
+        group.batch = group.steps.pop(0)()
+
+    def finish(group):
+        if group.batch is not None:
+            arrive(group.batch)
+        store(group.sum, group.result)
 
     def set_vector(row, value):
         ref.vec[row : row + 1, :] = value
 
     att_enc, att_self, att_cross = ref.attention
+    for group, result, by_item in zip(ref.group, ref.sums, ITEM_FIRST):
+        group.result, group.batch = result, None
+        group.steps = item_first(group) if by_item else depth_first(group)
     dec_in_part, dec_out_part, cross_part, enc_in_part, enc_out_part, self_part, last_part = (
         ref.group
     )
     enc_ff = (weight.enc_ff_in, weight.enc_ff_out)
     dec_ff = (weight.dec_ff_in, weight.dec_ff_out)
 
-    def build(group, row, start, features, block, wide=False):
-        gradient = mm_left_t(columns_of(group, start, start + features), gathered(block))
+    def build(group, row, start, features, tokens, wide=False):
+        gradient = mm_left_t(columns_of(group, start, start + features), tokens)
         if wide:
             put_gradient(group.part, row, gradient)
             return
@@ -1005,8 +1052,12 @@
     )
     channel_row = jnp.sum(chosen, axis=0, keepdims=True)
     masked = (small.series[...].astype(F32) * channel_row).astype(BF16)
-    ref.x_series[quad] = jnp.zeros(ref.x_series.shape[1:], BF16)
-    ref.x_series[quad, :, 0:channels] = masked
+    dec_hidden = small.dec_in[...]
+    ref.x_first[quad, :, 0:width] = dec_hidden
+    ref.x_first[quad, :, width:] = jnp.zeros((rows, ref.x_first.shape[2] - width), BF16)
+    ref.x_first[quad, :, width : width + channels] = masked
+    pl.semaphore_wait(barrier, len(greeted))
+    share_first = share(ref.x_first)
 
     shift_row = small.delta_shift[...].astype(F32)
     ref.t_shift[...] = jnp.broadcast_to(
@@ -1034,30 +1085,30 @@
 
     def pass_on(own):
         block = own.pair
-        return [send(block.at[:, core], block.at[:, core], core_dev)]
+        return send(block.at[:, core], block.at[:, core], core_dev)
 
     qkv = weight.enc_qkv()
     enc_query = mm(enc_hidden, qkv[0]) + small.enc_query_bias[...]
     enc_key = mm(enc_hidden, qkv[1])
     enc_value = mm(enc_hidden, qkv[2]) + small.enc_bias[0:1, :]
-    pl.semaphore_wait(barrier, len(greeted))
     go_enc_pair = send_pairs(att_enc, enc_key, enc_value)
     go_enc_query = send_queries(att_enc, enc_query)
     ref.shift[chip, core] = ref.t_shift[...]
-    go_shift = []
-    for step in range(1, chips):
-        go_shift.append(
-            send(ref.t_shift, ref.shift.at[chip, core], same_core(step)[1])
-        )
-
-    dec_hidden = small.dec_in[...]
-    ref.x_dec_in[quad] = dec_hidden
+    go_shift = ship(
+        [
+            (ref.t_shift, ref.shift.at[chip, core], same_core(step)[1])
+            for step in range(1, chips)
+        ],
+        ref.shift.at[pl.ds(0, chips - 1), 0],
+    )
+
     qkv = weight.dec_qkv()
     self_query = mm(dec_hidden, qkv[0]) + small.dec_bias[0:1, :]
     self_key = mm(dec_hidden, qkv[1])
     self_value = mm(dec_hidden, qkv[2]) + small.dec_bias[1:2, :]
     go_self_pair = send_pairs(att_self, self_key, self_value)
     go_self_query = send_queries(att_self, self_query)
+    share_enc_hidden = share(ref.x_enc_hidden)
 
     def attention(own, shifted, causal):
         pairs = own.pair[...].reshape(keys_total, LANES)
@@ -1101,7 +1152,7 @@
     arrive(go_enc_pair)
     on_enc = pass_on(att_enc)
     arrive(go_shift)
-    on_shift = [send(ref.shift.at[:, core], ref.shift.at[:, core], core_dev)]
+    on_shift = send(ref.shift.at[:, core], ref.shift.at[:, core], core_dev)
     arrive(go_enc_query)
     arrive(go_self_pair)
     on_self = pass_on(att_self)
@@ -1116,11 +1167,11 @@
     arrive(on_self)
     arrive(go_self_query)
     back_self = attention(att_self, False, True)
-    shares = [share(ref.x_series), share(ref.x_enc_hidden), share(ref.x_dec_in)]
-
-    def feed_forward(values, weights, bias_row, out_bias, side):
+    relay(share_first)
+
+    def feed_forward(values, weights, bias_row, out_bias, low_at, act_at, slope):
         low = values.astype(BF16)
-        side.hidden[quad] = low
+        low_at[0][quad, :, low_at[1] : low_at[1] + width] = low
         weight_in, weight_out = weights[0](), weights[1]()
         total = out_bias
         for piece in range(hidden // width):
@@ -1128,26 +1179,28 @@
             pre = mm(low, weight_in[:, cut]) + small.ff_bias[bias_row : bias_row + 1, cut]
             normal = 0.5 * (1.0 + lax.erf(pre * 0.7071067811865476))
             act = (pre * normal).astype(BF16)
-            side.slope[:, cut] = normal + pre * (
+            slope[:, cut] = normal + pre * (
                 jnp.exp(pre * pre * -0.5) * 0.3989422804014327
             )
-            side.act[quad, :, cut] = act
+            at = act_at[1] + piece * width
+            act_at[0][quad, :, at : at + width] = act
             total = total + mm(act, weight_out[cut, :])
         return total
 
-    def feed_forward_back(upstream, weights, side, vector_row, group):
+    def feed_forward_back(upstream, weights, slope, vector_row, group):
         low = upstream.astype(BF16)
         weight_in, weight_out = weights[0](), weights[1]()
         total = None
         for piece in range(hidden // width):
             cut = slice(piece * width, (piece + 1) * width)
             act_grad = mm_right_t(low, weight_out[cut, :])
-            pre_grad = (act_grad * side.slope[:, cut]).astype(BF16)
-            set_vector(
-                vector_row + piece, jnp.sum(pre_grad.astype(F32), axis=0, keepdims=True)
-            )
+            pre_grad = (act_grad * slope[:, cut]).astype(BF16)
+            sums = jnp.sum(pre_grad.astype(F32), axis=0, keepdims=True)
             for member in range(QUAD):
                 at = piece * LANES
+                ref.vec[vector_row + member : vector_row + member + 1, at : at + LANES] = sums[
+                    :, member * LANES : (member + 1) * LANES
+                ]
                 group.cut[member, :, at : at + LANES] = pre_grad[
                     :, member * LANES : (member + 1) * LANES
                 ]
@@ -1164,7 +1217,7 @@
 
     arrive(back_enc)
     attended = mixed_rows(att_enc)
-    ref.x_enc_mixed[quad] = attended
+    ref.x_early[quad, :, 0:width] = attended
     first, unit, scale = norm_forward(
         embedded + mm(attended, weight.enc_out()[...]) + small.enc_bias[1:2, :],
         small.enc_gain[0:1, :],
@@ -1172,13 +1225,21 @@
     )
     save_norm(0, unit, scale)
     second, unit, scale = norm_forward(
-        first + feed_forward(first, enc_ff, 0, small.enc_bias[2:3, :], ref.enc_ff),
+        first + feed_forward(
+            first,
+            enc_ff,
+            0,
+            small.enc_bias[2:3, :],
+            (ref.x_early, width),
+            (ref.x_act, 0),
+            ref.enc_slope,
+        ),
         small.enc_gain[1:2, :],
         small.enc_bias[4:5, :],
     )
     save_norm(1, unit, scale)
     memory = second.astype(BF16)
-    ref.x_memory[quad] = memory
+    ref.x_early[quad, :, 2 * width : 3 * width] = memory
     qkv = weight.cross_qkv()
     cross_key = mm(memory, qkv[1])
     cross_value = mm(memory, qkv[2]) + small.dec_bias[4:5, :]
@@ -1186,7 +1247,7 @@
 
     arrive(back_self)
     attended = mixed_rows(att_self)
-    ref.x_self_mixed[quad] = attended
+    ref.x_early[quad, :, 3 * width : 4 * width] = attended
     first, unit, scale = norm_forward(
         small.dec_in[...].astype(F32)
         + mm(attended, weight.dec_out()[...])
@@ -1197,32 +1258,20 @@
     save_norm(2, unit, scale)
     ref.first_dec[...] = first
     low = first.astype(BF16)
-    ref.x_cross_hidden[quad] = low
+    ref.x_early[quad, :, 4 * width : 5 * width] = low
     go_cross_query = send_queries(att_cross, mm(low, qkv[0]) + small.dec_bias[3:4, :])
-    for shared in shares:
-        relay(shared)
-    shares_two = [
-        share(block)
-        for block in (
-            ref.x_enc_mixed,
-            ref.enc_ff.hidden,
-            ref.x_memory,
-            ref.x_self_mixed,
-            ref.x_cross_hidden,
-        )
-    ]
+    share_early = share(ref.x_early)
 
     arrive(go_cross_pair)
     on_cross = pass_on(att_cross)
     arrive(go_cross_query)
     arrive(on_cross)
     back_cross = attention(att_cross, True, False)
-    for shared in shares_two:
-        relay(shared)
-    shares_three = [share(ref.enc_ff.act)]
+    share_act = share(ref.x_act)
+    relay(share_enc_hidden)
     arrive(back_cross)
     attended = mixed_rows(att_cross)
-    ref.x_cross_mixed[quad] = attended
+    ref.x_late[quad, :, 0:width] = attended
     second, unit, scale = norm_forward(
         ref.first_dec[...]
         + mm(attended, weight.cross_out()[...])
@@ -1231,10 +1280,16 @@
         small.dec_bias[8:9, :],
     )
     save_norm(3, unit, scale)
-    shares_four = [share(ref.x_cross_mixed)]
-
-    forward = feed_forward(second, dec_ff, 1, small.dec_bias[6:7, :], ref.dec_ff)
-    shares_four += [share(ref.dec_ff.hidden), share(ref.dec_ff.act)]
+
+    forward = feed_forward(
+        second,
+        dec_ff,
+        1,
+        small.dec_bias[6:7, :],
+        (ref.x_late, width),
+        (ref.x_late_act, 0),
+        ref.dec_slope,
+    )
     third, unit, scale = norm_forward(
         second + forward,
         small.dec_gain[2:3, :],
@@ -1260,7 +1315,7 @@
     )
     set_vector(20, gain_grad)
     set_vector(17, shift_grad)
-    from_ff = feed_forward_back(third_grad, dec_ff, ref.dec_ff, 25, dec_in_part)
+    from_ff = feed_forward_back(third_grad, dec_ff, ref.dec_slope, 25, dec_in_part)
     second_grad = norm_step(3, third_grad + from_ff, small.dec_gain, 1, 19, 16)
     ref.second_grad[...] = second_grad
 
@@ -1272,15 +1327,13 @@
         return spread(own.t_grad, lambda at: own.grad.at[at])
 
     go_cross_grad = send_mixed_grad(att_cross, second_grad, weight.cross_out())
+    share_late_act = share(ref.x_late_act)
     ff_width = hidden // QUAD
-    columns_dec_in = share_columns(dec_in_part, 0, ff_width)
     cut_columns(third_grad, dec_out_part, 0)
     cut_columns(second_grad, dec_out_part, LANES)
-    columns_dec_out = share_columns(dec_out_part, 0, 2 * LANES)
     set_vector(14, column_sum(third_grad))
     set_vector(13, column_sum(second_grad))
-    for shared in shares_three + shares_four:
-        relay(shared)
+    relay(share_early)
 
     def attention_back(own):
         pairs = own.pair[...].reshape(keys_total, LANES)
@@ -1320,14 +1373,14 @@
         )
         pair_grad = (key_total * factor + value_total).reshape(chips, CORES, rows, LANES)
         for which in range(CORES):
-            ref.pair_sum[which] = pair_grad[:, which]
+            own.pair_sum[which] = pair_grad[:, which]
             own.t_part[which] = pair_grad[:, which].astype(BF16)
         exchange = send(own.t_part.at[1 - core], own.part, core_dev)
         return go_query, exchange
 
     def attention_back_pairs(own, exchange):
-        exchange.wait_recv()
-        total = ref.pair_sum[core] + own.part[...].astype(F32)
+        arrive(exchange)
+        total = own.pair_sum[core] + own.part[...].astype(F32)
         own.t_pair_grad[...] = total.astype(BF16)
         own.pair_grad[chip] = own.t_pair_grad[chip]
         return spread(own.t_pair_grad, lambda at: own.pair_grad.at[at])
@@ -1343,16 +1396,10 @@
     arrive(go_cross_grad)
     go_query, exchange = attention_back(att_cross)
     go_pair = attention_back_pairs(att_cross, exchange)
-
-    for shared in shares_four:
-        settle(shared)
-    arrive(columns_dec_in)
-    build(dec_in_part, 0, 0, ff_width, ref.dec_ff.hidden, wide=True)
-    item_dec_in = reduce_item(dec_in_part)
-    arrive(columns_dec_out)
-    build(dec_out_part, 0, 0, LANES, ref.dec_ff.act)
-    build(dec_out_part, LANES, LANES, LANES, ref.x_cross_mixed)
-    item_dec_out = reduce_item(dec_out_part)
+    share_late = share(ref.x_late)
+    columns_dec_in = share_columns(dec_in_part, 0, ff_width)
+    columns_dec_out = share_columns(dec_out_part, 0, 2 * LANES)
+    relay(share_act)
 
     qkv = weight.cross_qkv()
     arrive(go_query)
@@ -1375,7 +1422,7 @@
         cross_value_grad.astype(BF16), qkv[2]
     )
     enc_second_grad = norm_step(1, memory_grad, small.enc_gain, 1, 7, 5)
-    from_ff = feed_forward_back(enc_second_grad, enc_ff, ref.enc_ff, 21, enc_in_part)
+    from_ff = feed_forward_back(enc_second_grad, enc_ff, ref.enc_slope, 21, enc_in_part)
     enc_first_grad = norm_step(0, enc_second_grad + from_ff, small.enc_gain, 0, 6, 4)
     ref.enc_first_grad[...] = enc_first_grad
     go_enc_grad = send_mixed_grad(att_enc, enc_first_grad, weight.enc_out())
@@ -1386,53 +1433,54 @@
     for row in (0, 1, 8, 9, 29, 30, 31):
         set_vector(row, jnp.zeros((1, width), F32))
     vec_item = send(ref.vec, ref.vec_item, item_dev)
+    columns_enc_in = share_columns(enc_in_part, 0, ff_width)
+    cut_columns(enc_second_grad, enc_out_part, 0)
+    cut_columns(enc_first_grad, enc_out_part, LANES)
+    columns_enc_out = share_columns(enc_out_part, 0, 2 * LANES)
     for index, values in enumerate(
         (cross_query_grad, cross_key_grad, cross_value_grad, first_grad)
     ):
         cut_columns(values, cross_part, index * LANES)
     columns_cross = share_columns(cross_part, 0, 4 * LANES)
-    columns_enc_in = share_columns(enc_in_part, 0, ff_width)
-    cut_columns(enc_second_grad, enc_out_part, 0)
-    cut_columns(enc_first_grad, enc_out_part, LANES)
-    columns_enc_out = share_columns(enc_out_part, 0, 2 * LANES)
+    relay(share_late_act)
+    relay(share_late)
+
+    settle(share_late)
+    arrive(columns_dec_in)
+    build(dec_in_part, 0, 0, ff_width, gathered(ref.x_late, width, width), wide=True)
+    advance(dec_in_part)
+    settle(share_late_act)
+    arrive(columns_dec_out)
+    build(dec_out_part, 0, 0, LANES, gathered(ref.x_late_act, 0, hidden))
+    build(dec_out_part, LANES, LANES, LANES, gathered(ref.x_late, 0, width))
+    advance(dec_out_part)
 
     arrive(go_self_grad)
-    go_self_query_grad, exchange = attention_back(att_self)
-    arrive(item_dec_in)
-    depth_dec_in = reduce_depth(dec_in_part)
-    go_self_pair_grad = attention_back_pairs(att_self, exchange)
-    for shared in shares + shares_two + shares_three:
-        settle(shared)
+    go_self_query_grad, exchange_self = attention_back(att_self)
+    arrive(go_enc_grad)
+    go_enc_query_grad, exchange_enc = attention_back(att_enc)
+    go_enc_pair_grad = attention_back_pairs(att_enc, exchange_enc)
+    go_self_pair_grad = attention_back_pairs(att_self, exchange_self)
+    advance(dec_in_part)
+
+    settle(share_early)
+    settle(share_act)
+    arrive(columns_enc_in)
+    build(enc_in_part, 0, 0, ff_width, gathered(ref.x_early, width, width), wide=True)
+    advance(enc_in_part)
+    advance(dec_out_part)
+    arrive(columns_enc_out)
+    build(enc_out_part, 0, 0, LANES, gathered(ref.x_act, 0, hidden))
+    build(enc_out_part, LANES, LANES, LANES, gathered(ref.x_early, 0, width))
+    advance(enc_out_part)
     arrive(columns_cross)
-    build(cross_part, 0, 0, LANES, ref.x_cross_hidden)
-    build(cross_part, column, LANES, 2 * LANES, ref.x_memory)
-    build(cross_part, 3 * column, 3 * LANES, LANES, ref.x_self_mixed)
-    item_cross = reduce_item(cross_part)
-    vec_item.wait_recv()
+    build(cross_part, 0, 0, LANES, gathered(ref.x_early, 4 * width, width))
+    build(cross_part, column, LANES, 2 * LANES, gathered(ref.x_early, 2 * width, width))
+    build(cross_part, 3 * column, 3 * LANES, LANES, gathered(ref.x_early, 3 * width, width))
+    advance(cross_part)
+    arrive(vec_item)
     ref.vec_a[...] = ref.vec[...] + ref.vec_item[...]
     vec_core = send(ref.vec_a, ref.vec_core, core_dev)
-    arrive(go_enc_grad)
-    go_enc_query_grad, exchange = attention_back(att_enc)
-    go_enc_pair_grad = attention_back_pairs(att_enc, exchange)
-    vec_core.wait_recv()
-    ref.vec_b[...] = ref.vec_a[...] + ref.vec_core[...]
-    vec_x = send(ref.vec_b, ref.vec_x, x_dev)
-    arrive(item_dec_out)
-    depth_dec_out = reduce_depth(dec_out_part)
-
-    arrive(columns_enc_in)
-    build(enc_in_part, 0, 0, ff_width, ref.enc_ff.hidden, wide=True)
-    item_enc_in = reduce_item(enc_in_part)
-    arrive(columns_enc_out)
-    build(enc_out_part, 0, 0, LANES, ref.enc_ff.act)
-    build(enc_out_part, LANES, LANES, LANES, ref.x_enc_mixed)
-    item_enc_out = reduce_item(enc_out_part)
-    vec_x.wait_recv()
-    ref.vec_c[...] = ref.vec_b[...] + ref.vec_x[...]
-    vec_depth = [
-        send(ref.vec_c, ref.vec_depth.at[step - 1], z_peer(step)[1])
-        for step in range(1, depth)
-    ]
 
     def input_grad(own, weights, first):
         query_grad = query_grad_rows(own)
@@ -1445,36 +1493,43 @@
         )
         return total, query_grad, key_grad, value_grad
 
+    arrive(go_enc_query_grad)
+    arrive(go_enc_pair_grad)
+    total, query_grad, key_grad, value_grad = input_grad(
+        att_enc, weight.enc_qkv(), ref.enc_first_grad
+    )
+    ref.o_enc_grad[...] = total
+    store(ref.o_enc_grad, ref.enc_grad)
+    for index, values in enumerate((query_grad, key_grad, value_grad, total)):
+        cut_columns(values, last_part, index * LANES)
+    columns_last = share_columns(last_part, 0, 4 * LANES)
+    arrive(vec_core)
+    ref.vec_b[...] = ref.vec_a[...] + ref.vec_core[...]
+    vec_x = send(ref.vec_b, ref.vec_x, x_dev)
     arrive(go_self_query_grad)
     arrive(go_self_pair_grad)
-    total, query_grad, key_grad, value_grad = input_grad(att_self, weight.dec_qkv(), ref.first_grad)
+    total, query_grad, key_grad, value_grad = input_grad(
+        att_self, weight.dec_qkv(), ref.first_grad
+    )
     ref.o_dec_grad[...] = total
     store(ref.o_dec_grad, ref.dec_grad)
     for index, values in enumerate((query_grad, key_grad, value_grad)):
         cut_columns(values, self_part, index * LANES)
     columns_self = share_columns(self_part, 0, 3 * LANES)
-    arrive(depth_dec_in)
-    last_dec_in = reduce_last(dec_in_part)
-    arrive(item_cross)
-    depth_cross = reduce_depth(cross_part)
-    arrive(go_enc_query_grad)
-    arrive(go_enc_pair_grad)
-    total, query_grad, key_grad, value_grad = input_grad(att_enc, weight.enc_qkv(), ref.enc_first_grad)
-    ref.o_enc_grad[...] = total
-    store(ref.o_enc_grad, ref.enc_grad)
-    for index, values in enumerate((query_grad, key_grad, value_grad, total)):
-        cut_columns(values, last_part, index * LANES)
-    columns_enc = share_columns(last_part, 0, 4 * LANES)
+    advance(dec_in_part)
+    settle(share_first)
+    settle(share_enc_hidden)
+    arrive(columns_last)
+    build(last_part, 0, 0, 3 * LANES, gathered(ref.x_enc_hidden, 0, width))
+    build(
+        last_part,
+        3 * column,
+        3 * LANES,
+        LANES,
+        gathered(ref.x_first, width, ref.x_first.shape[2] - width),
+    )
     arrive(columns_self)
-    build(self_part, 0, 0, 3 * LANES, ref.x_dec_in)
-    item_self = reduce_item(self_part)
-    arrive(depth_dec_out)
-    last_dec_out = reduce_last(dec_out_part)
-    arrive(item_enc_in)
-    depth_enc_in = reduce_depth(enc_in_part)
-    arrive(columns_enc)
-    build(last_part, 0, 0, 3 * LANES, ref.x_enc_hidden)
-    build(last_part, 3 * column, 3 * LANES, LANES, ref.x_series)
+    build(self_part, 0, 0, 3 * LANES, gathered(ref.x_first, 0, width))
     totals = [
         jnp.sum(
             columns_of(group, index * LANES, (index + 1) * LANES).astype(F32),
@@ -1487,40 +1542,54 @@
     totals = jnp.concatenate([totals, jnp.zeros((column, width - LANES), F32)], axis=1)
     for level in range(depth):
         put_rows(last_part.part, level, 5 * column, totals.astype(BF16))
-    item_last = reduce_item(last_part)
+    advance(last_part)
+    advance(enc_in_part)
+    advance(self_part)
+    advance(dec_out_part)
+    arrive(vec_x)
+    ref.vec_c[...] = ref.vec_b[...] + ref.vec_x[...]
+    copies = []
+    for step in range(1, depth):
+        peer, device = z_peer(step)
+        lanes = pl.ds(pl.multiple_of(peer * LANES, LANES), LANES)
+        copies.append((ref.vec_c.at[:, lanes], ref.vec_depth.at[step - 1], device))
+    vec_depth = ship(copies, ref.vec_depth)
+    advance(enc_out_part)
+    advance(cross_part)
+    advance(dec_in_part)
+    advance(enc_in_part)
+    advance(last_part)
+    advance(cross_part)
+    advance(enc_out_part)
+    advance(self_part)
+    advance(enc_in_part)
     arrive(vec_depth)
-    total = ref.vec_c[...]
+    lanes = pl.ds(pl.multiple_of(z_place * LANES, LANES), LANES)
+    total = ref.vec_c[:, lanes]
     for step in range(1, depth):
         total = total + ref.vec_depth[step - 1]
     ref.o_vectors[...] = total
     store(ref.o_vectors, ref.vectors)
-    arrive(item_enc_out)
-    depth_enc_out = reduce_depth(enc_out_part)
-    arrive(depth_cross)
-    last_cross = reduce_last(cross_part)
-    arrive(item_self)
-    depth_self = reduce_depth(self_part)
-    arrive(depth_enc_in)
-    last_enc_in = reduce_last(enc_in_part)
-    arrive(item_last)
-    depth_last = reduce_depth(last_part)
-    arrive(depth_enc_out)
-    last_enc_out = reduce_last(enc_out_part)
-    finish(dec_in_part, 0, last_dec_in)
-    finish(dec_out_part, 1, last_dec_out)
-    finish(cross_part, 2, last_cross)
-    arrive(depth_self)
-    last_self = reduce_last(self_part)
-    arrive(depth_last)
-    last_last = reduce_last(last_part)
-    finish(enc_in_part, 3, last_enc_in)
-    finish(enc_out_part, 4, last_enc_out)
-    finish(self_part, 5, last_self)
-    finish(last_part, 6, last_last)
+    advance(dec_out_part)
+    finish(dec_out_part)
+    advance(last_part)
+    finish(dec_in_part)
+    advance(cross_part)
+    advance(self_part)
+    advance(enc_out_part)
+    finish(enc_out_part)
+    finish(enc_in_part)
+    advance(last_part)
+    finish(cross_part)
+    advance(self_part)
+    finish(last_part)
+    finish(self_part)
     for copy in stores:
         copy.wait()
-    for copy in sends:
-        copy.wait_send()
+    for batch in batches:
+        depart(batch)
+    if len(batches) != LINK_COUNT:
+        raise ValueError(len(batches))
 
 
 def finish_body(*refs):
@@ -1560,7 +1629,7 @@
     place = lax.axis_index(SEQ)
     column, width = g_enc_out.shape
     channels = g_embed.shape[1]
-    level, member = place // QUAD, lax.rem(place, QUAD)
+    member = lax.rem(place, QUAD)
     dec_out[...] = dec_in[...]
     enc_grad[...] = enc_grad_in[...]
     dec_grad[...] = dec_grad_in[...]
@@ -1595,22 +1664,23 @@
         g_enc_qkv[index] = block[index * column : (index + 1) * column]
     g_embed[:, 0:width] = block[3 * column : 4 * column]
     g_embed[:, width:channels] = block[4 * column : 5 * column, 0 : channels - width]
-
-    group = vectors[:, pl.ds(pl.multiple_of(level * LANES, LANES), LANES)]
-    moved = pltpu.roll(group, lax.rem(LANES - member * column, LANES), axis=1)
+    late = block[5 * column : 5 * column + 8, 0:LANES]
+    level = place // QUAD
+    late = pltpu.roll(late, lax.rem(LANES - level * column, LANES), axis=1)[:, 0:column]
+
+    values = vectors[...]
+    moved = pltpu.roll(values, lax.rem(LANES - member * column, LANES), axis=1)
     rows = moved[:, 0:column]
-    late = block[5 * column : 5 * column + 8, 0:LANES]
-    late = pltpu.roll(late, lax.rem(LANES - level * column, LANES), axis=1)[:, 0:column]
     g_enc_query_bias[...] = late[2:3]
     g_enc_bias[...] = jnp.concatenate([late[3:4], rows[2:6]], axis=0)
     g_enc_gain[...] = rows[6:8]
-    g_dec_bias[...] = jnp.concatenate([late[0:2], rows[10:18]], axis=0)
+    g_dec_bias[...] = jnp.concatenate(
+        [late[0:2], rows[10:18]], axis=0
+    )
     g_dec_gain[...] = rows[18:21]
-    lanes = pl.ds(pl.multiple_of(member * LANES, LANES), LANES)
-    hidden_rows = vectors[:, lanes]
-    row_index = lax.broadcasted_iota(jnp.int32, hidden_rows.shape, 0)
+    row_index = lax.broadcasted_iota(jnp.int32, values.shape, 0)
     for index in range(2):
-        chosen = jnp.where(row_index == 21 + 4 * index + level, hidden_rows, 0.0)
+        chosen = jnp.where(row_index == 21 + QUAD * index + member, values, 0.0)
         g_ff_bias[index : index + 1, :] = jnp.sum(chosen, axis=0, keepdims=True)
 
 
@@ -1713,27 +1783,26 @@
             pair_grad=paired,
             t_part=low(CORES, chips, rows, LANES),
             part=paired,
+            pair_sum=full(CORES, chips, rows, LANES),
             pair_t=low(LANES, keys_total),
             weights=low(HALVES, keys_total, queries),
             inverse=full(HALVES, 8, queries),
             mixed_t=full(LANES, queries),
         )
 
-    def feed_forward_space():
-        return dict(
-            hidden=exchanged(width), act=exchanged(hidden), slope=full(rows, hidden)
-        )
-
-    def group_space(count, features):
-        half = count // 2
+    def group_space(count, features, by_item):
+        halves = 2 if by_item else 1
+        half = count // halves
         return dict(
             cut=exchanged(features),
             met=exchanged(features),
-            part=low(2, depth, half, width),
-            item=low(depth, half, width),
-            half=low(depth, half, width),
-            depth=low(depth - 1, half, width),
-            sum=low(2, half, width),
+            part=low(halves, 2, 2, half, width),
+            item=low(2, 2, half, width) if by_item else low(half, width),
+            half=low(2, 2, half, width) if by_item else low(half, width),
+            near=low(2, half, width),
+            pair=low(2, half, width),
+            far=low(half, width),
+            sum=low(halves, half, width),
         )
 
     ff_width = hidden // QUAD
@@ -1765,20 +1834,17 @@
         o_dec_result=low(rows, width),
         o_enc_grad=full(rows, width),
         o_dec_grad=full(rows, width),
-        o_vectors=full(32, width),
-        x_series=exchanged(padded),
+        o_vectors=full(32, LANES),
+        x_first=exchanged(width + padded),
         x_enc_hidden=exchanged(width),
-        x_dec_in=exchanged(width),
-        x_enc_mixed=exchanged(width),
-        x_memory=exchanged(width),
-        x_self_mixed=exchanged(width),
-        x_cross_hidden=exchanged(width),
-        x_cross_mixed=exchanged(width),
-        enc_ff=feed_forward_space(),
-        dec_ff=feed_forward_space(),
+        x_early=exchanged(5 * width),
+        x_act=exchanged(hidden),
+        x_late=exchanged(2 * width),
+        x_late_act=exchanged(hidden),
+        enc_slope=full(rows, hidden),
+        dec_slope=full(rows, hidden),
         attention=[attention_space() for index in range(3)],
-        group=[group_space(*sizes) for sizes in zip(group_rows, group_features)],
-        pair_sum=full(CORES, chips, rows, LANES),
+        group=[group_space(*sizes) for sizes in zip(group_rows, group_features, ITEM_FIRST)],
         t_shift=full(8, LANES),
         shift=full(chips, CORES, 8, LANES),
         shift_columns=full(keys_total, LANES),
@@ -1796,7 +1862,7 @@
         vec_b=full(32, width),
         vec_x=full(32, width),
         vec_c=full(32, width),
-        vec_depth=full(depth - 1, 32, width),
+        vec_depth=full(depth - 1, 32, LANES),
         load_sem=pltpu.SemaphoreType.DMA((len(weights),)),
         send_sem=pltpu.SemaphoreType.DMA((LINK_COUNT,)),
         recv_sem=pltpu.SemaphoreType.DMA((LINK_COUNT,)),
@@ -1805,8 +1871,11 @@
         dec_result=jax.ShapeDtypeStruct((rows, width), BF16),
         enc_grad=jax.ShapeDtypeStruct((rows, width), F32),
         dec_grad=jax.ShapeDtypeStruct((rows, width), F32),
-        sums=[jax.ShapeDtypeStruct((2, count // 2, width), BF16) for count in group_rows],
-        vectors=jax.ShapeDtypeStruct((32, width), F32),
+        sums=[
+            jax.ShapeDtypeStruct((2, count // 2, width) if by_item else (1, count, width), BF16)
+            for count, by_item in zip(group_rows, ITEM_FIRST)
+        ],
+        vectors=jax.ShapeDtypeStruct((32, LANES), F32),
     )
     out_shapes, out_structure = jax.tree.flatten(outputs)
     scratch_shapes, scratch_structure = jax.tree.flatten(scratch)

time: 142 us -> 127 us (0.89)
  Pallas kernels: 140 us -> 125 us
    pallas_call x1, Pallas kernels: 137 us -> 122 us  [fused_local(): pl.pallas_call(partial(fused_body, structures + [out_structure, scratch_s...]
where the time goes in v3:
time: 127 us
  Pallas kernels  125 us (98%)
  between operations  2.12 us (2%)
    pallas_call x1, Pallas kernels, fused_local(): pl.pallas_call(partial(fused_body, structures + [out_structure, scratch_s...  122 us
    pallas_call x1, Pallas kernels, fused_local(): pl.pallas_call(finish_body, out_shape=[jax.ShapeDtypeStruct(shape, BF16 i...  2.9 us

profile of v3, /device:TPU:0, one launch (start us, length us, event | category | flops | bytes accessed | tf_op | source)
XLA Modules:
  0.0 126.8 jit_solution(10162763360983109581)
XLA Ops:
  2.0 121.8 %layers.1 = (f32[64,512]{1,0:T(8,128)}, bf16[64,512]{1,0:T(8,128)(2,1)}, f32[64,512]{1,0:T(8,128)}, bf16[2,64,512]{2,1,0:T(8,128)(2,1)}, bf16[1,160,512]{2,1,0:T...) custom-call(s32[1]{0:T(128)S(6)} %copy.45.refs_0_, ...), custom_call_target="tpu_custom_call" | custom-call | tf_op jit(solution)/shard_map/layers/pallas_call | solution.py:1884
  123.7 2.9 %columns.1 = (bf16[64,512]{1,0:T(8,128)(2,1)}, f32[64,512]{1,0:T(8,128)}, f32[64,512]{1,0:T(8,128)}, f32[32,862]{1,0:T(8,128)}, f32[3,32,512]{2,1,0:T(8,128)}, /...) custom-call(bf16[64,512]{1,0:T(8,128)(2,1)} %get-tuple-element.51.re, ...), custom_call_target="tpu_custom_call" | custom-call | tf_op jit(solution)/shard_map/columns/pallas_call | solution.py:1922

commit v4 on v3

--- a/solution.py
+++ b/solution.py
@@ -644,8 +644,7 @@
 HALVES = 2
 CORES = 2
 LANES = 128
-LINK_COUNT = 81
-ITEM_FIRST = (True, False, True, True, False, True, True)
+LINK_COUNT = 83
 VMEM_BYTES = 60 << 20
 LOAD_FIRST = 3
 LOAD_ORDER = (
@@ -807,6 +806,9 @@
     near_dev = ((z_high * 2 + 1 - z_odd) * QUAD + quad, item)
     far_dev = (((1 - z_high) * 2 + z_odd) * QUAD + quad, item)
     x_quad = (1 - x_place) * 2 + core
+    other_dev = (chip * 2 + (1 - core), 1 - item)
+    item_quad = item * 2 + core
+    next_quad = (1 - item) * 2 + core
 
     def same_core(step):
         peer = lax.rem(chip + step, chips)
@@ -817,7 +819,7 @@
         return peer, (peer * QUAD + quad, item)
 
     barrier = pltpu.get_barrier_semaphore()
-    greeted = [core_dev, diagonal_dev, item_dev] + [same_core(step)[1] for step in range(1, chips)]
+    greeted = [core_dev, diagonal_dev, item_dev, other_dev] + [same_core(step)[1] for step in range(1, chips)]
     for device in greeted:
         pl.semaphore_signal(barrier, inc=1, device_id=device, device_id_type=MESH)
 
@@ -935,6 +937,58 @@
                 )
             )
         return ship(copies, target.at[pl.ds(0, QUAD - 1), :, pl.ds(start, stop - start)])
+
+    def share_item(group):
+        group.tokens[item_quad] = group.own[item]
+        return [
+            group.tokens,
+            send(group.own.at[item], group.tokens.at[item_quad], core_dev),
+            send(group.own.at[1 - item], group.tokens.at[item_quad], item_dev),
+        ]
+
+    def relay_item(shared):
+        arrive(shared[2])
+        block = shared[0]
+        shared.append(send(block.at[next_quad], block.at[next_quad], core_dev))
+
+    def cut_cores(values, group, start):
+        part = lane_index((rows, LANES)) // column
+        for member in range(CORES):
+            for pair in range(depth // 2):
+                total = None
+                for piece in range(QUAD):
+                    level = pair * 2 + piece // 2
+                    cut = values[:, level * LANES : (level + 1) * LANES]
+                    place_in = 2 * (piece % 2) + member
+                    shift = (column * (piece - place_in)) % LANES
+                    moved = pltpu.roll(cut, shift, axis=1) if shift else cut
+                    total = moved if total is None else jnp.where(part == piece, moved, total)
+                at = start + pair * LANES
+                group.cut[member, :, at : at + LANES] = total.astype(BF16)
+
+    def share_cores(group):
+        group.met[item_quad] = group.cut[core]
+        return ship(
+            [
+                (group.cut.at[1 - core], group.met.at[item_quad], core_dev),
+                (group.cut.at[core], group.met.at[item_quad], item_dev),
+                (group.cut.at[1 - core], group.met.at[item_quad], other_dev),
+            ],
+            group.met.at[pl.ds(0, QUAD - 1)],
+        )
+
+    def build_cores(group):
+        lanes = width // 2
+        met = group.met[...].reshape(QUAD * rows, 2 * lanes)
+        tokens = group.tokens[...]
+        tokens = tokens.reshape(QUAD * rows, tokens.shape[2])
+        for index, (start, stop) in enumerate(((0, hidden // 2), (hidden // 2, tokens.shape[1]))):
+            gradient = mm_left_t(met[:, index * lanes : (index + 1) * lanes], tokens[:, start:stop])
+            gradient = gradient.astype(BF16)
+            for at in range(chips):
+                group.part[at % 2, at // 4, at // 2 % 2, :, start:stop] = gradient[
+                    at * column : (at + 1) * column
+                ]
 
     def columns_of(group, start, stop):
         value = group.met[:, :, start:stop]
@@ -975,9 +1029,9 @@
     def both_sums(left, right):
         return (left.astype(F32) + right.astype(F32)).astype(BF16)
 
-    def item_first(group):
+    def steps_of(group, which, device):
         def near():
-            group.half[...] = both_sums(group.part[item], group.item[...])
+            group.half[...] = both_sums(group.part[which], group.item[...])
             return send(group.half.at[:, 1 - z_odd], group.near, near_dev)
 
         def far():
@@ -988,27 +1042,7 @@
             group.sum[item] = both_sums(group.pair[z_high], group.far[...])
             return send(group.sum.at[item], group.sum.at[item], item_dev)
 
-        return [lambda: send(group.part.at[1 - item], group.item, item_dev), near, far, last]
-
-    def depth_first(group):
-        def far():
-            group.pair[...] = both_sums(group.part[0, :, z_odd], group.near[...])
-            return send(group.pair.at[1 - z_high], group.far, far_dev)
-
-        def items():
-            group.half[...] = both_sums(group.pair[z_high], group.far[...])
-            return send(group.half, group.item, item_dev)
-
-        def last():
-            group.sum[0] = both_sums(group.half[...], group.item[...])
-            return None
-
-        return [
-            lambda: send(group.part.at[0, :, 1 - z_odd], group.near, near_dev),
-            far,
-            items,
-            last,
-        ]
+        return [lambda: send(group.part.at[1 - which], group.item, device), near, far, last]
 
     def advance(group):
         if group.batch is not None:
@@ -1020,16 +1054,60 @@
             arrive(group.batch)
         store(group.sum, group.result)
 
+    def gather_depth(block):
+        copies = []
+        for step in range(1, depth):
+            device = z_peer(step)[1]
+            copies.append((block.at[z_place, x_place], block.at[z_place, x_place], device))
+        return ship(copies, block.at[pl.ds(0, depth - 1), 0])
+
+    def gather_x(block, batch):
+        arrive(batch)
+        return send(block.at[:, x_place], block.at[:, x_place], x_dev)
+
+    def head_gradients(own, space, block):
+        value = block[...]
+        tokens = value.reshape((chips,) + value.shape[2:])
+        tokens = jnp.concatenate([tokens, jnp.ones((chips, rows, LANES), BF16)], axis=2)
+        features = tokens.shape[2]
+        queries = own.t_query_grad[...].reshape(block_queries, LANES)
+        total = None
+        for half in range(HALVES):
+            part = tokens[:, half * packed_rows : (half + 1) * packed_rows]
+            part = mm_left_t(queries, part.reshape(block_queries, features))
+            part = part[half * LANES // 2 : (half + 1) * LANES // 2]
+            total = part if total is None else total + part
+        pairs = own.t_pair_grad[...].reshape(chips * rows, LANES)
+        both = mm_left_t(pairs, tokens.reshape(chips * rows, features))
+        for index, gradient in enumerate((total, both[: LANES // 2], both[LANES // 2 :])):
+            for which in range(CORES):
+                space.mine[which, index * column : (index + 1) * column, :] = gradient[
+                    which * column : (which + 1) * column
+                ].astype(BF16)
+        return send(space.mine.at[1 - core], space.core, core_dev)
+
+    def heads_item(space, batch):
+        arrive(batch)
+        space.both[...] = both_sums(space.mine[core], space.core[...])
+        return send(space.both, space.item, item_dev)
+
+    def heads_done(space, batch, target):
+        arrive(batch)
+        space.sum[...] = space.both[...].astype(F32) + space.item[...].astype(F32)
+        store(space.sum, target)
+
     def set_vector(row, value):
         ref.vec[row : row + 1, :] = value
 
     att_enc, att_self, att_cross = ref.attention
-    for group, result, by_item in zip(ref.group, ref.sums, ITEM_FIRST):
+    dec_in_part, cross_part, enc_in_part, embed_part = ref.group
+    dec_out_part, enc_out_part = ref.core_group
+    for group in ref.group:
+        group.steps = steps_of(group, item, item_dev)
+    for group in ref.core_group:
+        group.steps = steps_of(group, x_place, x_dev)
+    for group, result in zip(ref.group + ref.core_group, ref.sums):
         group.result, group.batch = result, None
-        group.steps = item_first(group) if by_item else depth_first(group)
-    dec_in_part, dec_out_part, cross_part, enc_in_part, enc_out_part, self_part, last_part = (
-        ref.group
-    )
     enc_ff = (weight.enc_ff_in, weight.enc_ff_out)
     dec_ff = (weight.dec_ff_in, weight.dec_ff_out)
 
@@ -1053,21 +1131,28 @@
     channel_row = jnp.sum(chosen, axis=0, keepdims=True)
     masked = (small.series[...].astype(F32) * channel_row).astype(BF16)
     dec_hidden = small.dec_in[...]
-    ref.x_first[quad, :, 0:width] = dec_hidden
-    ref.x_first[quad, :, width:] = jnp.zeros((rows, ref.x_first.shape[2] - width), BF16)
-    ref.x_first[quad, :, width : width + channels] = masked
-    pl.semaphore_wait(barrier, len(greeted))
-    share_first = share(ref.x_first)
+    ref.g_dec_in[z_place, x_place] = dec_hidden
+    ref.x_series[quad] = jnp.zeros(ref.x_series.shape[1:], BF16)
+    ref.x_series[quad, :, 0:channels] = masked
 
     shift_row = small.delta_shift[...].astype(F32)
     ref.t_shift[...] = jnp.broadcast_to(
         jnp.concatenate([shift_row, shift_row], axis=1), ref.t_shift.shape
     )
+    ref.shift[chip, core] = ref.t_shift[...]
+    pl.semaphore_wait(barrier, len(greeted))
+    go_shift = ship(
+        [
+            (ref.t_shift, ref.shift.at[chip, core], same_core(step)[1])
+            for step in range(1, chips)
+        ],
+        ref.shift.at[pl.ds(0, chips - 1), 0],
+    )
 
     embedded = small.enc_in[...].astype(F32) + mm(masked, weight.value_embed()[...])
     ref.embedded[...] = embedded
     enc_hidden = embedded.astype(BF16)
-    ref.x_enc_hidden[quad] = enc_hidden
+    ref.g_enc_hidden[z_place, x_place] = enc_hidden
     for name in LOAD_ORDER[LOAD_FIRST:]:
         loaded[name].start()
 
@@ -1093,22 +1178,12 @@
     enc_value = mm(enc_hidden, qkv[2]) + small.enc_bias[0:1, :]
     go_enc_pair = send_pairs(att_enc, enc_key, enc_value)
     go_enc_query = send_queries(att_enc, enc_query)
-    ref.shift[chip, core] = ref.t_shift[...]
-    go_shift = ship(
-        [
-            (ref.t_shift, ref.shift.at[chip, core], same_core(step)[1])
-            for step in range(1, chips)
-        ],
-        ref.shift.at[pl.ds(0, chips - 1), 0],
-    )
-
     qkv = weight.dec_qkv()
     self_query = mm(dec_hidden, qkv[0]) + small.dec_bias[0:1, :]
     self_key = mm(dec_hidden, qkv[1])
     self_value = mm(dec_hidden, qkv[2]) + small.dec_bias[1:2, :]
     go_self_pair = send_pairs(att_self, self_key, self_value)
     go_self_query = send_queries(att_self, self_query)
-    share_enc_hidden = share(ref.x_enc_hidden)
 
     def attention(own, shifted, causal):
         pairs = own.pair[...].reshape(keys_total, LANES)
@@ -1149,29 +1224,30 @@
             [own.mixed[head].astype(F32) for head in range(chips)]
         ).astype(BF16)
 
-    arrive(go_enc_pair)
-    on_enc = pass_on(att_enc)
     arrive(go_shift)
     on_shift = send(ref.shift.at[:, core], ref.shift.at[:, core], core_dev)
-    arrive(go_enc_query)
-    arrive(go_self_pair)
-    on_self = pass_on(att_self)
     arrive(on_shift)
     for block in range(chips):
         line = low_lanes(ref.shift[block, 0], ref.shift[block, 1])[0:1, :] * 0.125
         ref.shift_columns[block * LANES : (block + 1) * LANES, :] = jnp.broadcast_to(
             line, (LANES, LANES)
         ).T
+    arrive(go_enc_pair)
+    on_enc = pass_on(att_enc)
+    arrive(go_enc_query)
     arrive(on_enc)
     back_enc = attention(att_enc, True, False)
+    go_dec_in = gather_depth(ref.g_dec_in)
+    share_series = share(ref.x_series)
+    arrive(go_self_pair)
+    on_self = pass_on(att_self)
+    arrive(go_self_query)
     arrive(on_self)
-    arrive(go_self_query)
     back_self = attention(att_self, False, True)
-    relay(share_first)
-
-    def feed_forward(values, weights, bias_row, out_bias, low_at, act_at, slope):
+
+    def feed_forward(values, weights, bias_row, out_bias, low_at, group, slope):
         low = values.astype(BF16)
-        low_at[0][quad, :, low_at[1] : low_at[1] + width] = low
+        low_at[quad, :, 0:width] = low
         weight_in, weight_out = weights[0](), weights[1]()
         total = out_bias
         for piece in range(hidden // width):
@@ -1182,8 +1258,8 @@
             slope[:, cut] = normal + pre * (
                 jnp.exp(pre * pre * -0.5) * 0.3989422804014327
             )
-            at = act_at[1] + piece * width
-            act_at[0][quad, :, at : at + width] = act
+            half, at = divmod(piece * width, hidden // 2)
+            group.own[half, :, at : at + width] = act
             total = total + mm(act, weight_out[cut, :])
         return total
 
@@ -1215,9 +1291,15 @@
     def saved_norm(index):
         return ref.unit[index], ref.scale[index, :, 0:1]
 
+    def keep_mixed(group, values):
+        for half in range(HALVES):
+            group.own[half, :, hidden // 2 :] = values[
+                :, half * width // 2 : (half + 1) * width // 2
+            ]
+
     arrive(back_enc)
     attended = mixed_rows(att_enc)
-    ref.x_early[quad, :, 0:width] = attended
+    keep_mixed(enc_out_part, attended)
     first, unit, scale = norm_forward(
         embedded + mm(attended, weight.enc_out()[...]) + small.enc_bias[1:2, :],
         small.enc_gain[0:1, :],
@@ -1230,8 +1312,8 @@
             enc_ff,
             0,
             small.enc_bias[2:3, :],
-            (ref.x_early, width),
-            (ref.x_act, 0),
+            ref.x_early,
+            enc_out_part,
             ref.enc_slope,
         ),
         small.enc_gain[1:2, :],
@@ -1239,7 +1321,8 @@
     )
     save_norm(1, unit, scale)
     memory = second.astype(BF16)
-    ref.x_early[quad, :, 2 * width : 3 * width] = memory
+    ref.x_early[quad, :, width : 2 * width] = memory
+    share_enc_out = share_item(enc_out_part)
     qkv = weight.cross_qkv()
     cross_key = mm(memory, qkv[1])
     cross_value = mm(memory, qkv[2]) + small.dec_bias[4:5, :]
@@ -1247,7 +1330,7 @@
 
     arrive(back_self)
     attended = mixed_rows(att_self)
-    ref.x_early[quad, :, 3 * width : 4 * width] = attended
+    ref.x_early[quad, :, 2 * width : 3 * width] = attended
     first, unit, scale = norm_forward(
         small.dec_in[...].astype(F32)
         + mm(attended, weight.dec_out()[...])
@@ -1258,7 +1341,7 @@
     save_norm(2, unit, scale)
     ref.first_dec[...] = first
     low = first.astype(BF16)
-    ref.x_early[quad, :, 4 * width : 5 * width] = low
+    ref.x_early[quad, :, 3 * width : 4 * width] = low
     go_cross_query = send_queries(att_cross, mm(low, qkv[0]) + small.dec_bias[3:4, :])
     share_early = share(ref.x_early)
 
@@ -1267,11 +1350,13 @@
     arrive(go_cross_query)
     arrive(on_cross)
     back_cross = attention(att_cross, True, False)
-    share_act = share(ref.x_act)
-    relay(share_enc_hidden)
+    go_enc_hidden = gather_depth(ref.g_enc_hidden)
+    on_dec_in = gather_x(ref.g_dec_in, go_dec_in)
+    relay_item(share_enc_out)
+    relay(share_series)
     arrive(back_cross)
     attended = mixed_rows(att_cross)
-    ref.x_late[quad, :, 0:width] = attended
+    keep_mixed(dec_out_part, attended)
     second, unit, scale = norm_forward(
         ref.first_dec[...]
         + mm(attended, weight.cross_out()[...])
@@ -1286,10 +1371,11 @@
         dec_ff,
         1,
         small.dec_bias[6:7, :],
-        (ref.x_late, width),
-        (ref.x_late_act, 0),
+        ref.x_late,
+        dec_out_part,
         ref.dec_slope,
     )
+    share_dec_out = share_item(dec_out_part)
     third, unit, scale = norm_forward(
         second + forward,
         small.dec_gain[2:3, :],
@@ -1327,12 +1413,14 @@
         return spread(own.t_grad, lambda at: own.grad.at[at])
 
     go_cross_grad = send_mixed_grad(att_cross, second_grad, weight.cross_out())
-    share_late_act = share(ref.x_late_act)
     ff_width = hidden // QUAD
-    cut_columns(third_grad, dec_out_part, 0)
-    cut_columns(second_grad, dec_out_part, LANES)
+    cut_cores(third_grad, dec_out_part, 0)
+    cut_cores(second_grad, dec_out_part, width // 2)
+    columns_dec_out = share_cores(dec_out_part)
     set_vector(14, column_sum(third_grad))
     set_vector(13, column_sum(second_grad))
+    share_late = share(ref.x_late)
+    columns_dec_in = share_columns(dec_in_part, 0, ff_width)
     relay(share_early)
 
     def attention_back(own):
@@ -1395,11 +1483,17 @@
 
     arrive(go_cross_grad)
     go_query, exchange = attention_back(att_cross)
+    relay(share_late)
+    relay_item(share_dec_out)
     go_pair = attention_back_pairs(att_cross, exchange)
-    share_late = share(ref.x_late)
-    columns_dec_in = share_columns(dec_in_part, 0, ff_width)
-    columns_dec_out = share_columns(dec_out_part, 0, 2 * LANES)
-    relay(share_act)
+    settle(share_late)
+    arrive(columns_dec_in)
+    build(dec_in_part, 0, 0, ff_width, gathered(ref.x_late, 0, width), wide=True)
+    advance(dec_in_part)
+    settle(share_dec_out)
+    arrive(columns_dec_out)
+    build_cores(dec_out_part)
+    advance(dec_out_part)
 
     qkv = weight.cross_qkv()
     arrive(go_query)
@@ -1434,27 +1528,16 @@
         set_vector(row, jnp.zeros((1, width), F32))
     vec_item = send(ref.vec, ref.vec_item, item_dev)
     columns_enc_in = share_columns(enc_in_part, 0, ff_width)
-    cut_columns(enc_second_grad, enc_out_part, 0)
-    cut_columns(enc_first_grad, enc_out_part, LANES)
-    columns_enc_out = share_columns(enc_out_part, 0, 2 * LANES)
     for index, values in enumerate(
         (cross_query_grad, cross_key_grad, cross_value_grad, first_grad)
     ):
         cut_columns(values, cross_part, index * LANES)
     columns_cross = share_columns(cross_part, 0, 4 * LANES)
-    relay(share_late_act)
-    relay(share_late)
-
-    settle(share_late)
-    arrive(columns_dec_in)
-    build(dec_in_part, 0, 0, ff_width, gathered(ref.x_late, width, width), wide=True)
+    cut_cores(enc_second_grad, enc_out_part, 0)
+    cut_cores(enc_first_grad, enc_out_part, width // 2)
+    columns_enc_out = share_cores(enc_out_part)
     advance(dec_in_part)
-    settle(share_late_act)
-    arrive(columns_dec_out)
-    build(dec_out_part, 0, 0, LANES, gathered(ref.x_late_act, 0, hidden))
-    build(dec_out_part, LANES, LANES, LANES, gathered(ref.x_late, 0, width))
     advance(dec_out_part)
-
     arrive(go_self_grad)
     go_self_query_grad, exchange_self = attention_back(att_self)
     arrive(go_enc_grad)
@@ -1462,90 +1545,68 @@
     go_enc_pair_grad = attention_back_pairs(att_enc, exchange_enc)
     go_self_pair_grad = attention_back_pairs(att_self, exchange_self)
     advance(dec_in_part)
+    advance(dec_out_part)
 
     settle(share_early)
-    settle(share_act)
     arrive(columns_enc_in)
-    build(enc_in_part, 0, 0, ff_width, gathered(ref.x_early, width, width), wide=True)
+    build(enc_in_part, 0, 0, ff_width, gathered(ref.x_early, 0, width), wide=True)
     advance(enc_in_part)
-    advance(dec_out_part)
+    settle(share_enc_out)
     arrive(columns_enc_out)
-    build(enc_out_part, 0, 0, LANES, gathered(ref.x_act, 0, hidden))
-    build(enc_out_part, LANES, LANES, LANES, gathered(ref.x_early, 0, width))
+    build_cores(enc_out_part)
     advance(enc_out_part)
     arrive(columns_cross)
-    build(cross_part, 0, 0, LANES, gathered(ref.x_early, 4 * width, width))
-    build(cross_part, column, LANES, 2 * LANES, gathered(ref.x_early, 2 * width, width))
-    build(cross_part, 3 * column, 3 * LANES, LANES, gathered(ref.x_early, 3 * width, width))
+    build(cross_part, 0, 0, LANES, gathered(ref.x_early, 3 * width, width))
+    build(cross_part, column, LANES, 2 * LANES, gathered(ref.x_early, width, width))
+    build(cross_part, 3 * column, 3 * LANES, LANES, gathered(ref.x_early, 2 * width, width))
     advance(cross_part)
     arrive(vec_item)
     ref.vec_a[...] = ref.vec[...] + ref.vec_item[...]
     vec_core = send(ref.vec_a, ref.vec_core, core_dev)
+    arrive(on_dec_in)
+    core_self = head_gradients(att_self, ref.head_self, ref.g_dec_in)
 
     def input_grad(own, weights, first):
         query_grad = query_grad_rows(own)
         key_grad, value_grad = pair_grad_rows(own)
-        total = (
+        return (
             first[...]
             + mm_right_t(query_grad.astype(BF16), weights[0])
             + mm_right_t(key_grad.astype(BF16), weights[1])
             + mm_right_t(value_grad.astype(BF16), weights[2])
         )
-        return total, query_grad, key_grad, value_grad
 
     arrive(go_enc_query_grad)
     arrive(go_enc_pair_grad)
-    total, query_grad, key_grad, value_grad = input_grad(
-        att_enc, weight.enc_qkv(), ref.enc_first_grad
-    )
+    total = input_grad(att_enc, weight.enc_qkv(), ref.enc_first_grad)
     ref.o_enc_grad[...] = total
     store(ref.o_enc_grad, ref.enc_grad)
-    for index, values in enumerate((query_grad, key_grad, value_grad, total)):
-        cut_columns(values, last_part, index * LANES)
-    columns_last = share_columns(last_part, 0, 4 * LANES)
+    cut_columns(total, embed_part, 0)
+    columns_embed = share_columns(embed_part, 0, LANES)
+    on_enc_hidden = gather_x(ref.g_enc_hidden, go_enc_hidden)
+    item_self = heads_item(ref.head_self, core_self)
     arrive(vec_core)
     ref.vec_b[...] = ref.vec_a[...] + ref.vec_core[...]
     vec_x = send(ref.vec_b, ref.vec_x, x_dev)
     arrive(go_self_query_grad)
     arrive(go_self_pair_grad)
-    total, query_grad, key_grad, value_grad = input_grad(
-        att_self, weight.dec_qkv(), ref.first_grad
-    )
+    total = input_grad(att_self, weight.dec_qkv(), ref.first_grad)
     ref.o_dec_grad[...] = total
     store(ref.o_dec_grad, ref.dec_grad)
-    for index, values in enumerate((query_grad, key_grad, value_grad)):
-        cut_columns(values, self_part, index * LANES)
-    columns_self = share_columns(self_part, 0, 3 * LANES)
+    advance(enc_in_part)
+    settle(share_series)
+    arrive(columns_embed)
+    build(embed_part, 0, 0, LANES, gathered(ref.x_series, 0, ref.x_series.shape[2]))
+    advance(embed_part)
+    advance(enc_out_part)
     advance(dec_in_part)
-    settle(share_first)
-    settle(share_enc_hidden)
-    arrive(columns_last)
-    build(last_part, 0, 0, 3 * LANES, gathered(ref.x_enc_hidden, 0, width))
-    build(
-        last_part,
-        3 * column,
-        3 * LANES,
-        LANES,
-        gathered(ref.x_first, width, ref.x_first.shape[2] - width),
-    )
-    arrive(columns_self)
-    build(self_part, 0, 0, 3 * LANES, gathered(ref.x_first, 0, width))
-    totals = [
-        jnp.sum(
-            columns_of(group, index * LANES, (index + 1) * LANES).astype(F32),
-            axis=0,
-            keepdims=True,
-        )
-        for group, index in ((self_part, 0), (self_part, 2), (last_part, 0), (last_part, 2))
-    ]
-    totals = jnp.concatenate(totals + [jnp.zeros((column - 4, LANES), F32)], axis=0)
-    totals = jnp.concatenate([totals, jnp.zeros((column, width - LANES), F32)], axis=1)
-    for level in range(depth):
-        put_rows(last_part.part, level, 5 * column, totals.astype(BF16))
-    advance(last_part)
+    advance(dec_out_part)
+    arrive(on_enc_hidden)
+    core_enc = head_gradients(att_enc, ref.head_enc, ref.g_enc_hidden)
     advance(enc_in_part)
-    advance(self_part)
-    advance(dec_out_part)
+    advance(cross_part)
+    heads_done(ref.head_self, item_self, ref.heads[1])
+    item_enc = heads_item(ref.head_enc, core_enc)
     arrive(vec_x)
     ref.vec_c[...] = ref.vec_b[...] + ref.vec_x[...]
     copies = []
@@ -1555,14 +1616,12 @@
         copies.append((ref.vec_c.at[:, lanes], ref.vec_depth.at[step - 1], device))
     vec_depth = ship(copies, ref.vec_depth)
     advance(enc_out_part)
+    finish(dec_in_part)
+    finish(dec_out_part)
+    advance(enc_in_part)
+    advance(embed_part)
     advance(cross_part)
-    advance(dec_in_part)
-    advance(enc_in_part)
-    advance(last_part)
-    advance(cross_part)
-    advance(enc_out_part)
-    advance(self_part)
-    advance(enc_in_part)
+    heads_done(ref.head_enc, item_enc, ref.heads[0])
     arrive(vec_depth)
     lanes = pl.ds(pl.multiple_of(z_place * LANES, LANES), LANES)
     total = ref.vec_c[:, lanes]
@@ -1570,20 +1629,14 @@
         total = total + ref.vec_depth[step - 1]
     ref.o_vectors[...] = total
     store(ref.o_vectors, ref.vectors)
-    advance(dec_out_part)
-    finish(dec_out_part)
-    advance(last_part)
-    finish(dec_in_part)
+    advance(embed_part)
+    advance(enc_out_part)
+    finish(enc_in_part)
     advance(cross_part)
-    advance(self_part)
-    advance(enc_out_part)
+    advance(embed_part)
     finish(enc_out_part)
-    finish(enc_in_part)
-    advance(last_part)
     finish(cross_part)
-    advance(self_part)
-    finish(last_part)
-    finish(self_part)
+    finish(embed_part)
     for copy in stores:
         copy.wait()
     for batch in batches:
@@ -1598,12 +1651,13 @@
         enc_grad_in,
         dec_grad_in,
         ff_in_two,
-        ff_out_two,
         cross,
         ff_in_one,
+        embed,
+        ff_out_two,
         ff_out_one,
-        self_part,
-        last,
+        head_enc,
+        head_self,
         vectors,
         dec_out,
         enc_grad,
@@ -1638,44 +1692,40 @@
         value = block[...]
         return value.reshape(value.shape[0] * value.shape[1], value.shape[2]).astype(F32)
 
-    def narrow(target, block, start):
-        for piece in range(target.shape[1] // width):
-            target[:, piece * width : (piece + 1) * width] = block[
-                start + piece * column : start + (piece + 1) * column
-            ]
-
     g_dec_ff_in[...] = whole(ff_in_two).T
-    block = whole(ff_out_two)
-    narrow(g_dec_ff_out, block, 0)
-    narrow(g_cross_out, block, LANES)
+    g_enc_ff_in[...] = whole(ff_in_one).T
     block = whole(cross)
     for index in range(3):
         g_cross_qkv[index] = block[index * column : (index + 1) * column]
-    narrow(g_dec_out, block, 3 * column)
-    g_enc_ff_in[...] = whole(ff_in_one).T
-    block = whole(ff_out_one)
-    narrow(g_enc_ff_out, block, 0)
-    narrow(g_enc_out, block, LANES)
-    block = whole(self_part)
-    for index in range(3):
-        g_dec_qkv[index] = block[index * column : (index + 1) * column]
-    block = whole(last)
-    for index in range(3):
-        g_enc_qkv[index] = block[index * column : (index + 1) * column]
-    g_embed[:, 0:width] = block[3 * column : 4 * column]
-    g_embed[:, width:channels] = block[4 * column : 5 * column, 0 : channels - width]
-    late = block[5 * column : 5 * column + 8, 0:LANES]
-    level = place // QUAD
-    late = pltpu.roll(late, lax.rem(LANES - level * column, LANES), axis=1)[:, 0:column]
+    g_dec_out[...] = block[3 * column : 4 * column]
+    for block, wide, narrow in (
+        (ff_out_two, g_dec_ff_out, g_cross_out),
+        (ff_out_one, g_enc_ff_out, g_enc_out),
+    ):
+        for half in range(HALVES):
+            value = block[half].astype(F32)
+            step = wide.shape[1] // 2
+            wide[:, half * step : (half + 1) * step] = value[:, 0:step]
+            rest = width // 2
+            narrow[:, half * rest : (half + 1) * rest] = value[:, step : step + rest]
+    late = []
+    for block, target in ((head_enc, g_enc_qkv), (head_self, g_dec_qkv)):
+        for index in range(3):
+            target[index] = block[index * column : (index + 1) * column, 0:width]
+        late.append(block[:, width : width + LANES].T[0:1])
+    late_enc, late_self = late
+    block = whole(embed)
+    g_embed[:, 0:width] = block[0:column]
+    g_embed[:, width:channels] = block[column : 2 * column, 0 : channels - width]
 
     values = vectors[...]
     moved = pltpu.roll(values, lax.rem(LANES - member * column, LANES), axis=1)
     rows = moved[:, 0:column]
-    g_enc_query_bias[...] = late[2:3]
-    g_enc_bias[...] = jnp.concatenate([late[3:4], rows[2:6]], axis=0)
+    g_enc_query_bias[...] = late_enc[:, 0:column]
+    g_enc_bias[...] = jnp.concatenate([late_enc[:, 2 * column : 3 * column], rows[2:6]], axis=0)
     g_enc_gain[...] = rows[6:8]
     g_dec_bias[...] = jnp.concatenate(
-        [late[0:2], rows[10:18]], axis=0
+        [late_self[:, 0:column], late_self[:, 2 * column : 3 * column], rows[10:18]], axis=0
     )
     g_dec_gain[...] = rows[18:21]
     row_index = lax.broadcasted_iota(jnp.int32, values.shape, 0)
@@ -1790,61 +1840,68 @@
             mixed_t=full(LANES, queries),
         )
 
-    def group_space(count, features, by_item):
-        halves = 2 if by_item else 1
-        half = count // halves
+    def sum_space(half, features):
         return dict(
-            cut=exchanged(features),
-            met=exchanged(features),
-            part=low(halves, 2, 2, half, width),
-            item=low(2, 2, half, width) if by_item else low(half, width),
-            half=low(2, 2, half, width) if by_item else low(half, width),
-            near=low(2, half, width),
-            pair=low(2, half, width),
-            far=low(half, width),
-            sum=low(halves, half, width),
+            part=low(2, 2, 2, half, features),
+            item=low(2, 2, half, features),
+            half=low(2, 2, half, features),
+            near=low(2, half, features),
+            pair=low(2, half, features),
+            far=low(half, features),
+            sum=low(2, half, features),
         )
 
+    def group_space(count, features):
+        return dict(
+            cut=exchanged(features), met=exchanged(features), **sum_space(count // 2, width)
+        )
+
+    def core_group_space():
+        features = (hidden + width) // 2
+        return dict(
+            own=low(HALVES, rows, features),
+            tokens=exchanged(features),
+            cut=low(CORES, rows, width),
+            met=exchanged(width),
+            **sum_space(column, features),
+        )
+
+    def head_space():
+        shape = (3 * column, width + LANES)
+        return dict(
+            mine=low(CORES, *shape),
+            core=low(*shape),
+            both=low(*shape),
+            item=low(*shape),
+            sum=full(*shape),
+        )
+
     ff_width = hidden // QUAD
-    group_rows = (
-        LANES,
-        LANES + column,
-        4 * column,
-        LANES,
-        LANES + column,
-        3 * column,
-        6 * column,
-    )
-    group_features = (
-        ff_width,
-        2 * LANES,
-        4 * LANES,
-        ff_width,
-        2 * LANES,
-        3 * LANES,
-        4 * LANES,
-    )
+    group_rows = (LANES, 4 * column, LANES, 2 * column)
+    group_features = (ff_width, 4 * LANES, ff_width, LANES)
     scratch = dict(
         held={name: low(*value.shape) for name, value in weights.items()},
         held_blocks={
             name: pltpu.VMEM(value.shape, value.dtype) for name, value in blocks.items()
         },
         block_sem=pltpu.SemaphoreType.DMA((len(blocks),)),
-        store_sem=pltpu.SemaphoreType.DMA((4 + len(group_rows),)),
+        store_sem=pltpu.SemaphoreType.DMA((8 + len(group_rows),)),
         o_dec_result=low(rows, width),
         o_enc_grad=full(rows, width),
         o_dec_grad=full(rows, width),
         o_vectors=full(32, LANES),
-        x_first=exchanged(width + padded),
-        x_enc_hidden=exchanged(width),
-        x_early=exchanged(5 * width),
-        x_act=exchanged(hidden),
-        x_late=exchanged(2 * width),
-        x_late_act=exchanged(hidden),
+        g_dec_in=low(depth, 2, rows, width),
+        g_enc_hidden=low(depth, 2, rows, width),
+        x_series=exchanged(padded),
+        x_early=exchanged(4 * width),
+        x_late=exchanged(width),
         enc_slope=full(rows, hidden),
         dec_slope=full(rows, hidden),
         attention=[attention_space() for index in range(3)],
-        group=[group_space(*sizes) for sizes in zip(group_rows, group_features, ITEM_FIRST)],
+        group=[group_space(*sizes) for sizes in zip(group_rows, group_features)],
+        core_group=[core_group_space() for index in range(2)],
+        head_enc=head_space(),
+        head_self=head_space(),
         t_shift=full(8, LANES),
         shift=full(chips, CORES, 8, LANES),
         shift_columns=full(keys_total, LANES),
@@ -1871,10 +1928,9 @@
         dec_result=jax.ShapeDtypeStruct((rows, width), BF16),
         enc_grad=jax.ShapeDtypeStruct((rows, width), F32),
         dec_grad=jax.ShapeDtypeStruct((rows, width), F32),
-        sums=[
-            jax.ShapeDtypeStruct((2, count // 2, width) if by_item else (1, count, width), BF16)
-            for count, by_item in zip(group_rows, ITEM_FIRST)
-        ],
+        sums=[jax.ShapeDtypeStruct((2, count // 2, width), BF16) for count in group_rows]
+        + [jax.ShapeDtypeStruct((2, column, (hidden + width) // 2), BF16)] * 2,
+        heads=[jax.ShapeDtypeStruct((3 * column, width + LANES), F32)] * 2,
         vectors=jax.ShapeDtypeStruct((32, LANES), F32),
     )
     out_shapes, out_structure = jax.tree.flatten(outputs)
@@ -1895,7 +1951,7 @@
     results = jax.tree.unflatten(out_structure, results)
     results = [
         results[key] for key in ("dec_result", "enc_grad", "dec_grad")
-    ] + results["sums"] + [results["vectors"]]
+    ] + results["sums"] + results["heads"] + [results["vectors"]]
 
     final = [
         (rows, width),

time: 127 us -> 113 us (0.89)
  Pallas kernels: 125 us -> 110 us
    pallas_call x1, Pallas kernels: 122 us -> 107 us  [fused_local(): pl.pallas_call(partial(fused_body, structures + [out_structure, scratch_s...]
where the time goes in v4:
time: 113 us; the launch traced here: 112 us
  Pallas kernels  110 us (97%)
  between operations  2.12 us (2%)
    pallas_call x1, Pallas kernels, fused_local(): pl.pallas_call(partial(fused_body, structures + [out_structure, scratch_s...  107 us
    pallas_call x1, Pallas kernels, fused_local(): pl.pallas_call(finish_body, out_shape=[jax.ShapeDtypeStruct(shape, BF16 i...  3.04 us

profile of v4, /device:TPU:0, one launch (start us, length us, event | category | flops | bytes accessed | tf_op | source)
XLA Modules:
  0.0 112.4 jit_solution(2945552565968555643)
XLA Ops:
  2.0 107.2 %layers.1 = (f32[64,512]{1,0:T(8,128)}, bf16[64,512]{1,0:T(8,128)(2,1)}, f32[64,512]{1,0:T(8,128)}, f32[96,640]{1,0:T(8,128)}, f32[96,640]{1,0:T(8,128)}, /*inde...) custom-call(s32[1]{0:T(128)S(6)} %copy.45.refs_0_, ...), custom_call_target="tpu_custom_call" | custom-call | tf_op jit(solution)/shard_map/layers/pallas_call | solution.py:1940
  109.2 3.0 %columns.1 = (bf16[64,512]{1,0:T(8,128)(2,1)}, f32[64,512]{1,0:T(8,128)}, f32[64,512]{1,0:T(8,128)}, f32[32,862]{1,0:T(8,128)}, f32[3,32,512]{2,1,0:T(8,128)}, /...) custom-call(bf16[64,512]{1,0:T(8,128)(2,1)} %get-tuple-element.52.re, ...), custom_call_target="tpu_custom_call" | custom-call | tf_op jit(solution)/shard_map/columns/pallas_call | solution.py:1978

commit v5 on v4

--- a/solution.py
+++ b/solution.py
@@ -1,4 +1,5 @@
 from functools import partial
+from types import SimpleNamespace
 import math
 
 import jax
@@ -644,8 +645,15 @@
 HALVES = 2
 CORES = 2
 LANES = 128
-LINK_COUNT = 83
-VMEM_BYTES = 60 << 20
+LINK_COUNT = 90
+ORDER = (
+    0, 1, 2, 3, 4, 5, 8, 6, 7, 9, 10, 12, 13, 15, 16, 17,
+    41, 14, 18, 19, 20, 21, 22, 11, 23, 24, 42, 37, 27, 25, 30, 49,
+    26, 32, 28, 38, 31, 43, 45, 36, 50, 53, 46, 57, 29, 54, 47, 33,
+    61, 34, 39, 51, 58, 44, 55, 62, 48, 52, 40, 35, 59, 63, 56, 60,
+    64,
+)
+VMEM_BYTES = 56 << 20
 LOAD_FIRST = 3
 LOAD_ORDER = (
     "value_embed",
@@ -838,13 +846,6 @@
     for copy in blocks:
         copy.wait()
 
-    stores = []
-
-    def store(source, target):
-        index = len(stores)
-        stores.append(pltpu.make_async_copy(source, target, ref.store_sem.at[index]))
-        stores[-1].start()
-
     batches = []
 
     def ship(copies, meter=None):
@@ -898,12 +899,12 @@
 
     def relay(shared):
         block = shared[0]
-        arrive(shared[2])
+        arrive(shared.pop())
         shared.append(send(block.at[x_quad], block.at[x_quad], core_dev))
 
     def settle(shared):
-        arrive(shared[1])
-        arrive(shared[3])
+        while len(shared) > 1:
+            arrive(shared.pop())
 
     def gathered(block, start, features):
         value = block[:, :, start : start + features]
@@ -947,7 +948,7 @@
         ]
 
     def relay_item(shared):
-        arrive(shared[2])
+        arrive(shared.pop())
         block = shared[0]
         shared.append(send(block.at[next_quad], block.at[next_quad], core_dev))
 
@@ -1042,27 +1043,35 @@
             group.sum[item] = both_sums(group.pair[z_high], group.far[...])
             return send(group.sum.at[item], group.sum.at[item], item_dev)
 
-        return [lambda: send(group.part.at[1 - which], group.item, device), near, far, last]
+        for level in range(2):
+            group.pushes.append(
+                partial(send, group.part.at[1 - which, level], group.item.at[level], device)
+            )
+        return [near, far, last]
 
     def advance(group):
-        if group.batch is not None:
-            arrive(group.batch)
-        group.batch = group.steps.pop(0)()
+        for batch in group.batches:
+            arrive(batch)
+        group.batches = [group.steps.pop(0)()]
+
+    def push(group, count=1):
+        for index in range(count):
+            group.batches.append(group.pushes.pop(0)())
 
     def finish(group):
-        if group.batch is not None:
-            arrive(group.batch)
-        store(group.sum, group.result)
-
-    def gather_depth(block):
-        copies = []
-        for step in range(1, depth):
-            device = z_peer(step)[1]
-            copies.append((block.at[z_place, x_place], block.at[z_place, x_place], device))
-        return ship(copies, block.at[pl.ds(0, depth - 1), 0])
-
-    def gather_x(block, batch):
-        arrive(batch)
+        for batch in group.batches:
+            arrive(batch)
+
+    def gather_depth(block, part, parts):
+        count = rows // parts
+        cut = pl.ds(part * count, count)
+        here = block.at[z_place, x_place, cut]
+        copies = [(here, here, z_peer(step)[1]) for step in range(1, depth)]
+        return ship(copies, block.at[pl.ds(0, depth - 1), 0, cut])
+
+    def gather_x(block, gathers):
+        for batch in gathers:
+            arrive(batch)
         return send(block.at[:, x_place], block.at[:, x_place], x_dev)
 
     def head_gradients(own, space, block):
@@ -1093,8 +1102,7 @@
 
     def heads_done(space, batch, target):
         arrive(batch)
-        space.sum[...] = space.both[...].astype(F32) + space.item[...].astype(F32)
-        store(space.sum, target)
+        target[...] = space.both[...].astype(F32) + space.item[...].astype(F32)
 
     def set_vector(row, value):
         ref.vec[row : row + 1, :] = value
@@ -1102,12 +1110,14 @@
     att_enc, att_self, att_cross = ref.attention
     dec_in_part, cross_part, enc_in_part, embed_part = ref.group
     dec_out_part, enc_out_part = ref.core_group
+    for group in ref.group + ref.core_group:
+        group.batches, group.pushes = [], []
     for group in ref.group:
         group.steps = steps_of(group, item, item_dev)
     for group in ref.core_group:
         group.steps = steps_of(group, x_place, x_dev)
     for group, result in zip(ref.group + ref.core_group, ref.sums):
-        group.result, group.batch = result, None
+        group.sum = result
     enc_ff = (weight.enc_ff_in, weight.enc_ff_out)
     dec_ff = (weight.dec_ff_in, weight.dec_ff_out)
 
@@ -1237,7 +1247,7 @@
     arrive(go_enc_query)
     arrive(on_enc)
     back_enc = attention(att_enc, True, False)
-    go_dec_in = gather_depth(ref.g_dec_in)
+    go_dec_in = [gather_depth(ref.g_dec_in, 0, 2)]
     share_series = share(ref.x_series)
     arrive(go_self_pair)
     on_self = pass_on(att_self)
@@ -1344,13 +1354,14 @@
     ref.x_early[quad, :, 3 * width : 4 * width] = low
     go_cross_query = send_queries(att_cross, mm(low, qkv[0]) + small.dec_bias[3:4, :])
     share_early = share(ref.x_early)
+    go_dec_in.append(gather_depth(ref.g_dec_in, 1, 2))
 
     arrive(go_cross_pair)
     on_cross = pass_on(att_cross)
     arrive(go_cross_query)
     arrive(on_cross)
     back_cross = attention(att_cross, True, False)
-    go_enc_hidden = gather_depth(ref.g_enc_hidden)
+    go_enc_hidden = [gather_depth(ref.g_enc_hidden, 0, 1)]
     on_dec_in = gather_x(ref.g_dec_in, go_dec_in)
     relay_item(share_enc_out)
     relay(share_series)
@@ -1381,8 +1392,7 @@
         small.dec_gain[2:3, :],
         small.dec_bias[9:10, :],
     )
-    ref.o_dec_result[...] = third.astype(BF16)
-    store(ref.o_dec_result, ref.dec_result)
+    ref.dec_result[...] = third.astype(BF16)
 
     def norm_step(index, upstream, gain, gain_row, gain_vector, shift_vector):
         unit, scale = saved_norm(index)
@@ -1414,14 +1424,6 @@
 
     go_cross_grad = send_mixed_grad(att_cross, second_grad, weight.cross_out())
     ff_width = hidden // QUAD
-    cut_cores(third_grad, dec_out_part, 0)
-    cut_cores(second_grad, dec_out_part, width // 2)
-    columns_dec_out = share_cores(dec_out_part)
-    set_vector(14, column_sum(third_grad))
-    set_vector(13, column_sum(second_grad))
-    share_late = share(ref.x_late)
-    columns_dec_in = share_columns(dec_in_part, 0, ff_width)
-    relay(share_early)
 
     def attention_back(own):
         pairs = own.pair[...].reshape(keys_total, LANES)
@@ -1481,91 +1483,6 @@
     def pair_grad_rows(own):
         return unpack_pairs([own.pair_grad[head].astype(F32) for head in range(chips)])
 
-    arrive(go_cross_grad)
-    go_query, exchange = attention_back(att_cross)
-    relay(share_late)
-    relay_item(share_dec_out)
-    go_pair = attention_back_pairs(att_cross, exchange)
-    settle(share_late)
-    arrive(columns_dec_in)
-    build(dec_in_part, 0, 0, ff_width, gathered(ref.x_late, 0, width), wide=True)
-    advance(dec_in_part)
-    settle(share_dec_out)
-    arrive(columns_dec_out)
-    build_cores(dec_out_part)
-    advance(dec_out_part)
-
-    qkv = weight.cross_qkv()
-    arrive(go_query)
-    cross_query_grad = query_grad_rows(att_cross)
-    first_grad = norm_step(
-        2,
-        ref.second_grad[...] + mm_right_t(cross_query_grad.astype(BF16), qkv[0]),
-        small.dec_gain,
-        0,
-        18,
-        15,
-    )
-    ref.first_grad[...] = first_grad
-    go_self_grad = send_mixed_grad(att_self, first_grad, weight.dec_out())
-    set_vector(10, column_sum(first_grad))
-
-    arrive(go_pair)
-    cross_key_grad, cross_value_grad = pair_grad_rows(att_cross)
-    memory_grad = mm_right_t(cross_key_grad.astype(BF16), qkv[1]) + mm_right_t(
-        cross_value_grad.astype(BF16), qkv[2]
-    )
-    enc_second_grad = norm_step(1, memory_grad, small.enc_gain, 1, 7, 5)
-    from_ff = feed_forward_back(enc_second_grad, enc_ff, ref.enc_slope, 21, enc_in_part)
-    enc_first_grad = norm_step(0, enc_second_grad + from_ff, small.enc_gain, 0, 6, 4)
-    ref.enc_first_grad[...] = enc_first_grad
-    go_enc_grad = send_mixed_grad(att_enc, enc_first_grad, weight.enc_out())
-    set_vector(3, column_sum(enc_second_grad))
-    set_vector(2, column_sum(enc_first_grad))
-    set_vector(11, column_sum(cross_query_grad))
-    set_vector(12, column_sum(cross_value_grad))
-    for row in (0, 1, 8, 9, 29, 30, 31):
-        set_vector(row, jnp.zeros((1, width), F32))
-    vec_item = send(ref.vec, ref.vec_item, item_dev)
-    columns_enc_in = share_columns(enc_in_part, 0, ff_width)
-    for index, values in enumerate(
-        (cross_query_grad, cross_key_grad, cross_value_grad, first_grad)
-    ):
-        cut_columns(values, cross_part, index * LANES)
-    columns_cross = share_columns(cross_part, 0, 4 * LANES)
-    cut_cores(enc_second_grad, enc_out_part, 0)
-    cut_cores(enc_first_grad, enc_out_part, width // 2)
-    columns_enc_out = share_cores(enc_out_part)
-    advance(dec_in_part)
-    advance(dec_out_part)
-    arrive(go_self_grad)
-    go_self_query_grad, exchange_self = attention_back(att_self)
-    arrive(go_enc_grad)
-    go_enc_query_grad, exchange_enc = attention_back(att_enc)
-    go_enc_pair_grad = attention_back_pairs(att_enc, exchange_enc)
-    go_self_pair_grad = attention_back_pairs(att_self, exchange_self)
-    advance(dec_in_part)
-    advance(dec_out_part)
-
-    settle(share_early)
-    arrive(columns_enc_in)
-    build(enc_in_part, 0, 0, ff_width, gathered(ref.x_early, 0, width), wide=True)
-    advance(enc_in_part)
-    settle(share_enc_out)
-    arrive(columns_enc_out)
-    build_cores(enc_out_part)
-    advance(enc_out_part)
-    arrive(columns_cross)
-    build(cross_part, 0, 0, LANES, gathered(ref.x_early, 3 * width, width))
-    build(cross_part, column, LANES, 2 * LANES, gathered(ref.x_early, width, width))
-    build(cross_part, 3 * column, 3 * LANES, LANES, gathered(ref.x_early, 2 * width, width))
-    advance(cross_part)
-    arrive(vec_item)
-    ref.vec_a[...] = ref.vec[...] + ref.vec_item[...]
-    vec_core = send(ref.vec_a, ref.vec_core, core_dev)
-    arrive(on_dec_in)
-    core_self = head_gradients(att_self, ref.head_self, ref.g_dec_in)
-
     def input_grad(own, weights, first):
         query_grad = query_grad_rows(own)
         key_grad, value_grad = pair_grad_rows(own)
@@ -1576,69 +1493,265 @@
             + mm_right_t(value_grad.astype(BF16), weights[2])
         )
 
-    arrive(go_enc_query_grad)
-    arrive(go_enc_pair_grad)
-    total = input_grad(att_enc, weight.enc_qkv(), ref.enc_first_grad)
-    ref.o_enc_grad[...] = total
-    store(ref.o_enc_grad, ref.enc_grad)
-    cut_columns(total, embed_part, 0)
-    columns_embed = share_columns(embed_part, 0, LANES)
-    on_enc_hidden = gather_x(ref.g_enc_hidden, go_enc_hidden)
-    item_self = heads_item(ref.head_self, core_self)
-    arrive(vec_core)
-    ref.vec_b[...] = ref.vec_a[...] + ref.vec_core[...]
-    vec_x = send(ref.vec_b, ref.vec_x, x_dev)
-    arrive(go_self_query_grad)
-    arrive(go_self_pair_grad)
-    total = input_grad(att_self, weight.dec_qkv(), ref.first_grad)
-    ref.o_dec_grad[...] = total
-    store(ref.o_dec_grad, ref.dec_grad)
-    advance(enc_in_part)
-    settle(share_series)
-    arrive(columns_embed)
-    build(embed_part, 0, 0, LANES, gathered(ref.x_series, 0, ref.x_series.shape[2]))
-    advance(embed_part)
-    advance(enc_out_part)
-    advance(dec_in_part)
-    advance(dec_out_part)
-    arrive(on_enc_hidden)
-    core_enc = head_gradients(att_enc, ref.head_enc, ref.g_enc_hidden)
-    advance(enc_in_part)
-    advance(cross_part)
-    heads_done(ref.head_self, item_self, ref.heads[1])
-    item_enc = heads_item(ref.head_enc, core_enc)
-    arrive(vec_x)
-    ref.vec_c[...] = ref.vec_b[...] + ref.vec_x[...]
-    copies = []
-    for step in range(1, depth):
-        peer, device = z_peer(step)
-        lanes = pl.ds(pl.multiple_of(peer * LANES, LANES), LANES)
-        copies.append((ref.vec_c.at[:, lanes], ref.vec_depth.at[step - 1], device))
-    vec_depth = ship(copies, ref.vec_depth)
-    advance(enc_out_part)
-    finish(dec_in_part)
-    finish(dec_out_part)
-    advance(enc_in_part)
-    advance(embed_part)
-    advance(cross_part)
-    heads_done(ref.head_enc, item_enc, ref.heads[0])
-    arrive(vec_depth)
-    lanes = pl.ds(pl.multiple_of(z_place * LANES, LANES), LANES)
-    total = ref.vec_c[:, lanes]
-    for step in range(1, depth):
-        total = total + ref.vec_depth[step - 1]
-    ref.o_vectors[...] = total
-    store(ref.o_vectors, ref.vectors)
-    advance(embed_part)
-    advance(enc_out_part)
-    finish(enc_in_part)
-    advance(cross_part)
-    advance(embed_part)
-    finish(enc_out_part)
-    finish(cross_part)
-    finish(embed_part)
-    for copy in stores:
-        copy.wait()
+    now = SimpleNamespace()
+    steps = []
+
+    def step(body):
+        steps.append(body)
+
+    @step
+    def late_rows():
+        now.share_late = share(ref.x_late)
+
+    @step
+    def dec_in_columns():
+        now.columns_dec_in = share_columns(dec_in_part, 0, ff_width)
+
+    @step
+    def dec_out_columns():
+        cut_cores(third_grad, dec_out_part, 0)
+        cut_cores(second_grad, dec_out_part, width // 2)
+        now.columns_dec_out = share_cores(dec_out_part)
+        set_vector(14, column_sum(third_grad))
+        set_vector(13, column_sum(second_grad))
+
+    @step
+    def early_relay():
+        relay(share_early)
+
+    @step
+    def cross_back():
+        arrive(go_cross_grad)
+        now.go_query, now.exchange = attention_back(att_cross)
+
+    @step
+    def late_relay():
+        relay(now.share_late)
+
+    @step
+    def dec_out_relay():
+        relay_item(share_dec_out)
+
+    @step
+    def cross_pairs():
+        now.go_pair = attention_back_pairs(att_cross, now.exchange)
+
+    @step
+    def dec_in_build():
+        settle(now.share_late)
+        arrive(now.columns_dec_in)
+        build(dec_in_part, 0, 0, ff_width, gathered(ref.x_late, 0, width), wide=True)
+        push(dec_in_part, 2)
+
+    @step
+    def dec_out_build():
+        settle(share_dec_out)
+        arrive(now.columns_dec_out)
+        build_cores(dec_out_part)
+
+    @step
+    def dec_out_push():
+        push(dec_out_part)
+
+    @step
+    def dec_out_push_two():
+        push(dec_out_part)
+
+    @step
+    def self_branch():
+        arrive(now.go_query)
+        now.cross_query_grad = query_grad_rows(att_cross)
+        now.first_grad = norm_step(
+            2,
+            ref.second_grad[...]
+            + mm_right_t(now.cross_query_grad.astype(BF16), weight.cross_qkv()[0]),
+            small.dec_gain,
+            0,
+            18,
+            15,
+        )
+        ref.first_grad[...] = now.first_grad
+        now.go_self_grad = send_mixed_grad(att_self, now.first_grad, weight.dec_out())
+        set_vector(10, column_sum(now.first_grad))
+
+    @step
+    def encoder_back():
+        arrive(now.go_pair)
+        qkv = weight.cross_qkv()
+        now.cross_key_grad, now.cross_value_grad = pair_grad_rows(att_cross)
+        memory_grad = mm_right_t(now.cross_key_grad.astype(BF16), qkv[1]) + mm_right_t(
+            now.cross_value_grad.astype(BF16), qkv[2]
+        )
+        now.second = norm_step(1, memory_grad, small.enc_gain, 1, 7, 5)
+        from_ff = feed_forward_back(now.second, enc_ff, ref.enc_slope, 21, enc_in_part)
+        now.first = norm_step(0, now.second + from_ff, small.enc_gain, 0, 6, 4)
+        ref.enc_first_grad[...] = now.first
+        now.go_enc_grad = send_mixed_grad(att_enc, now.first, weight.enc_out())
+
+    @step
+    def vector_sums():
+        set_vector(3, column_sum(now.second))
+        set_vector(2, column_sum(now.first))
+        set_vector(11, column_sum(now.cross_query_grad))
+        set_vector(12, column_sum(now.cross_value_grad))
+        for row in (0, 1, 8, 9, 29, 30, 31):
+            set_vector(row, jnp.zeros((1, width), F32))
+        now.vec_item = send(ref.vec, ref.vec_item, item_dev)
+
+    @step
+    def cross_columns():
+        for index, values in enumerate(
+            (now.cross_query_grad, now.cross_key_grad, now.cross_value_grad, now.first_grad)
+        ):
+            cut_columns(values, cross_part, index * LANES)
+        now.columns_cross = share_columns(cross_part, 0, 4 * LANES)
+
+    @step
+    def enc_in_columns():
+        now.columns_enc_in = share_columns(enc_in_part, 0, ff_width)
+
+    @step
+    def enc_out_columns():
+        cut_cores(now.second, enc_out_part, 0)
+        cut_cores(now.first, enc_out_part, width // 2)
+        now.columns_enc_out = share_cores(enc_out_part)
+
+    @step
+    def self_back():
+        arrive(now.go_self_grad)
+        now.go_self_query_grad, now.exchange_self = attention_back(att_self)
+
+    @step
+    def enc_back():
+        arrive(now.go_enc_grad)
+        now.go_enc_query_grad, now.exchange_enc = attention_back(att_enc)
+
+    @step
+    def cross_build():
+        settle(share_early)
+        arrive(now.columns_cross)
+        build(cross_part, 0, 0, LANES, gathered(ref.x_early, 3 * width, width))
+        build(cross_part, column, LANES, 2 * LANES, gathered(ref.x_early, width, width))
+        build(cross_part, 3 * column, 3 * LANES, LANES, gathered(ref.x_early, 2 * width, width))
+        push(cross_part, 2)
+
+    @step
+    def enc_pairs():
+        now.go_enc_pair_grad = attention_back_pairs(att_enc, now.exchange_enc)
+
+    @step
+    def self_pairs():
+        now.go_self_pair_grad = attention_back_pairs(att_self, now.exchange_self)
+
+    @step
+    def enc_in_build():
+        settle(share_early)
+        arrive(now.columns_enc_in)
+        build(enc_in_part, 0, 0, ff_width, gathered(ref.x_early, 0, width), wide=True)
+        push(enc_in_part, 2)
+
+    @step
+    def enc_out_build():
+        settle(share_enc_out)
+        arrive(now.columns_enc_out)
+        build_cores(enc_out_part)
+
+    @step
+    def enc_out_push():
+        push(enc_out_part)
+
+    @step
+    def enc_out_push_two():
+        push(enc_out_part)
+
+    @step
+    def self_heads():
+        arrive(on_dec_in)
+        now.core_self = head_gradients(att_self, ref.head_self, ref.g_dec_in)
+
+    @step
+    def self_heads_item():
+        now.item_self = heads_item(ref.head_self, now.core_self)
+
+    @step
+    def self_heads_done():
+        heads_done(ref.head_self, now.item_self, ref.heads[1])
+
+    @step
+    def enc_input():
+        arrive(now.go_enc_query_grad)
+        arrive(now.go_enc_pair_grad)
+        total = input_grad(att_enc, weight.enc_qkv(), ref.enc_first_grad)
+        ref.enc_grad[...] = total
+        cut_columns(total, embed_part, 0)
+        now.columns_embed = share_columns(embed_part, 0, LANES)
+
+    @step
+    def self_input():
+        arrive(now.go_self_query_grad)
+        arrive(now.go_self_pair_grad)
+        ref.dec_grad[...] = input_grad(att_self, weight.dec_qkv(), ref.first_grad)
+
+    @step
+    def enc_hidden_hop():
+        now.on_enc_hidden = gather_x(ref.g_enc_hidden, go_enc_hidden)
+
+    @step
+    def enc_heads():
+        arrive(now.on_enc_hidden)
+        now.core_enc = head_gradients(att_enc, ref.head_enc, ref.g_enc_hidden)
+
+    @step
+    def enc_heads_item():
+        now.item_enc = heads_item(ref.head_enc, now.core_enc)
+
+    @step
+    def enc_heads_done():
+        heads_done(ref.head_enc, now.item_enc, ref.heads[0])
+
+    @step
+    def embed_build():
+        settle(share_series)
+        arrive(now.columns_embed)
+        build(embed_part, 0, 0, LANES, gathered(ref.x_series, 0, ref.x_series.shape[2]))
+        push(embed_part, 2)
+
+    @step
+    def vector_core():
+        arrive(now.vec_item)
+        ref.vec_a[...] = ref.vec[...] + ref.vec_item[...]
+        now.vec_core = send(ref.vec_a, ref.vec_core, core_dev)
+
+    @step
+    def vector_x():
+        arrive(now.vec_core)
+        ref.vec_b[...] = ref.vec_a[...] + ref.vec_core[...]
+        now.vec_x = send(ref.vec_b, ref.vec_x, x_dev)
+
+    @step
+    def vector_depth():
+        arrive(now.vec_x)
+        ref.vec_c[...] = ref.vec_b[...] + ref.vec_x[...]
+        copies = []
+        for distance in range(1, depth):
+            peer, device = z_peer(distance)
+            lanes = pl.ds(pl.multiple_of(peer * LANES, LANES), LANES)
+            copies.append((ref.vec_c.at[:, lanes], ref.vec_depth.at[distance - 1], device))
+        now.vec_depth = ship(copies, ref.vec_depth)
+
+    @step
+    def vector_done():
+        arrive(now.vec_depth)
+        lanes = pl.ds(pl.multiple_of(z_place * LANES, LANES), LANES)
+        total = ref.vec_c[:, lanes]
+        for distance in range(1, depth):
+            total = total + ref.vec_depth[distance - 1]
+        ref.vectors[...] = total
+
+    for group in (dec_in_part, dec_out_part, cross_part, enc_in_part, enc_out_part, embed_part):
+        steps += [partial(advance, group)] * 3 + [partial(finish, group)]
+    for index in ORDER:
+        steps[index]()
     for batch in batches:
         depart(batch)
     if len(batches) != LINK_COUNT:
@@ -1848,7 +1961,6 @@
             near=low(2, half, features),
             pair=low(2, half, features),
             far=low(half, features),
-            sum=low(2, half, features),
         )
 
     def group_space(count, features):
@@ -1873,7 +1985,6 @@
             core=low(*shape),
             both=low(*shape),
             item=low(*shape),
-            sum=full(*shape),
         )
 
     ff_width = hidden // QUAD
@@ -1885,11 +1996,6 @@
             name: pltpu.VMEM(value.shape, value.dtype) for name, value in blocks.items()
         },
         block_sem=pltpu.SemaphoreType.DMA((len(blocks),)),
-        store_sem=pltpu.SemaphoreType.DMA((8 + len(group_rows),)),
-        o_dec_result=low(rows, width),
-        o_enc_grad=full(rows, width),
-        o_dec_grad=full(rows, width),
-        o_vectors=full(32, LANES),
         g_dec_in=low(depth, 2, rows, width),
         g_enc_hidden=low(depth, 2, rows, width),
         x_series=exchanged(padded),
@@ -1939,9 +2045,9 @@
     structures = [jax.tree.structure(part) for part in inputs]
     results = pl.pallas_call(
         partial(fused_body, structures + [out_structure, scratch_structure]),
-        out_shape=out_shapes,
+        out_shape=[pltpu.VMEM(leaf.shape, leaf.dtype) for leaf in out_shapes],
         in_specs=in_specs,
-        out_specs=[anywhere] * len(out_shapes),
+        out_specs=[in_vmem] * len(out_shapes),
         scratch_shapes=scratch_shapes,
         compiler_params=pltpu.CompilerParams(
             collective_id=1, has_side_effects=True, vmem_limit_bytes=VMEM_BYTES
@@ -1983,7 +2089,7 @@
         ],
         in_specs=[in_vmem] * len(results),
         out_specs=[in_vmem] * len(final),
-        compiler_params=pltpu.CompilerParams(vmem_limit_bytes=VMEM_BYTES),
+        compiler_params=pltpu.CompilerParams(vmem_limit_bytes=12 << 20),
         name="columns",
     )(*results)
     outputs = list(outputs)

time: 113 us -> 107 us (0.947)
  Pallas kernels: 110 us -> 105 us
    pallas_call x1, Pallas kernels: 107 us -> 103 us  [fused_local(): pl.pallas_call(partial(fused_body, structures + [out_structure, scratch_s...]
    pallas_call x1, Pallas kernels: 3.04 us -> 1.6 us  [fused_local(): pl.pallas_call(finish_body, out_shape=[jax.ShapeDtypeStruct(shape, BF16 i...]
where the time goes in v5:
time: 107 us
  Pallas kernels  105 us (98%)
  between operations  2.11 us (2%)
    pallas_call x1, Pallas kernels, fused_local(): pl.pallas_call(partial(fused_body, structures + [out_structure, scratch_s...  103 us

profile of v5, /device:TPU:0, one launch (start us, length us, event | category | flops | bytes accessed | tf_op | source)
XLA Modules:
  0.0 106.7 jit_solution(15026226780712746006)
XLA Ops:
  2.0 103.0 %layers.1 = (f32[64,512]{1,0:T(8,128)S(1)}, bf16[64,512]{1,0:T(8,128)(2,1)S(1)}, f32[64,512]{1,0:T(8,128)S(1)}, f32[96,640]{1,0:T(8,128)S(1)}, f32[96,640]{1,0:T...) custom-call(s32[1]{0:T(128)S(6)} %copy.45.refs_0_, ...), custom_call_target="tpu_custom_call" | custom-call | tf_op jit(solution)/shard_map/layers/pallas_call | solution.py:2046
  104.9 1.6 %columns.1 = (bf16[64,512]{1,0:T(8,128)(2,1)}, f32[64,512]{1,0:T(8,128)}, f32[64,512]{1,0:T(8,128)}, f32[32,862]{1,0:T(8,128)}, f32[3,32,512]{2,1,0:T(8,128)}, /...) custom-call(bf16[64,512]{1,0:T(8,128)(2,1)S(1)} %get-tuple-element.5, ...), custom_call_target="tpu_custom_call" | custom-call | tf_op jit(solution)/shard_map/columns/pallas_call | solution.py:2084

commit v6 on v5

--- a/solution.py
+++ b/solution.py
@@ -646,6 +646,7 @@
 CORES = 2
 LANES = 128
 LINK_COUNT = 90
+SENT_ROWS = 40496
 ORDER = (
     0, 1, 2, 3, 4, 5, 8, 6, 7, 9, 10, 12, 13, 15, 16, 17,
     41, 14, 18, 19, 20, 21, 22, 11, 23, 24, 42, 37, 27, 25, 30, 49,
@@ -856,7 +857,7 @@
                 pltpu.make_async_remote_copy(
                     src_ref=source,
                     dst_ref=target,
-                    send_sem=ref.send_sem.at[index],
+                    send_sem=ref.send_sem.at[0],
                     recv_sem=ref.recv_sem.at[index],
                     device_id=device,
                     device_id_type=MESH,
@@ -875,13 +876,6 @@
             made[0].wait_recv()
         else:
             pltpu.make_async_copy(meter, meter, ref.recv_sem.at[index]).wait()
-
-    def depart(batch):
-        index, made, meter = batch
-        if meter is None:
-            made[0].wait_send()
-        else:
-            pltpu.make_async_copy(meter, meter, ref.send_sem.at[index]).wait()
 
     def spread(source, target_at):
         copies = []
@@ -1752,10 +1746,14 @@
         steps += [partial(advance, group)] * 3 + [partial(finish, group)]
     for index in ORDER:
         steps[index]()
-    for batch in batches:
-        depart(batch)
-    if len(batches) != LINK_COUNT:
-        raise ValueError(len(batches))
+    pltpu.make_async_copy(ref.sent, ref.sent, ref.send_sem.at[0]).wait()
+    sent_rows = sum(
+        math.prod(copy.src_ref.shape) * copy.src_ref.dtype.itemsize // (2 * LANES)
+        for index, made, meter in batches
+        for copy in made
+    )
+    if len(batches) != LINK_COUNT or sent_rows != SENT_ROWS:
+        raise ValueError(len(batches), sent_rows)
 
 
 def finish_body(*refs):
@@ -2027,7 +2025,8 @@
         vec_c=full(32, width),
         vec_depth=full(depth - 1, 32, LANES),
         load_sem=pltpu.SemaphoreType.DMA((len(weights),)),
-        send_sem=pltpu.SemaphoreType.DMA((LINK_COUNT,)),
+        send_sem=pltpu.SemaphoreType.DMA((1,)),
+        sent=low(SENT_ROWS, LANES),
         recv_sem=pltpu.SemaphoreType.DMA((LINK_COUNT,)),
     )
     outputs = dict(

time: 107 us -> 106 us (level)
  no operation moved by 1% of the time
where the time goes in v6:
time: 106 us
  Pallas kernels  104 us (98%)
  between operations  2.11 us (2%)
    pallas_call x1, Pallas kernels, fused_local(): pl.pallas_call(partial(fused_body, structures + [out_structure, scratch_s...  102 us

profile of v6, /device:TPU:0, one launch (start us, length us, event | category | flops | bytes accessed | tf_op | source)
XLA Modules:
  0.0 105.7 jit_solution(2542018937320500828)
XLA Ops:
  2.0 102.0 %layers.1 = (f32[64,512]{1,0:T(8,128)S(1)}, bf16[64,512]{1,0:T(8,128)(2,1)S(1)}, f32[64,512]{1,0:T(8,128)S(1)}, f32[96,640]{1,0:T(8,128)S(1)}, f32[96,640]{1,0:T...) custom-call(s32[1]{0:T(128)S(6)} %copy.45.refs_0_, ...), custom_call_target="tpu_custom_call" | custom-call | tf_op jit(solution)/shard_map/layers/pallas_call | solution.py:2045
  104.0 1.6 %columns.1 = (bf16[64,512]{1,0:T(8,128)(2,1)}, f32[64,512]{1,0:T(8,128)}, f32[64,512]{1,0:T(8,128)}, f32[32,862]{1,0:T(8,128)}, f32[3,32,512]{2,1,0:T(8,128)}, /...) custom-call(bf16[64,512]{1,0:T(8,128)(2,1)S(1)} %get-tuple-element.5, ...), custom_call_target="tpu_custom_call" | custom-call | tf_op jit(solution)/shard_map/columns/pallas_call | solution.py:2083
